TPU v7x, 512 devices: a whole 4x8x8 slice. The times are simulated.
512 devices in a mesh: seg: 32 (over y, z_lo, core), fsdp: 16 (over z_hi, x).
Axes of the slice: x: 4, y: 8, z: 8 (z_hi: 4, z_lo: 2; z = z_hi * 2 + z_lo), core: 2. Of those that a mesh axis runs over, the one named last changes fastest.
Arguments:
- tokens: bfloat16 [8192, 8192], P('seg'), may hold values from -72 to 72
- w_query: bfloat16 [8192, 4096], P('seg', 'fsdp'), may hold values from -0.0625 to 0.0625
- key_weight: bfloat16 [8192, 512], P('seg', 'fsdp'), may hold values from -0.0625 to 0.0625
- value_weight: bfloat16 [8192, 512], P('seg', 'fsdp'), may hold values from -0.0625 to 0.0625
- resid_head: bfloat16 [8192], replicated, may hold values from -0.0625 to 0.0625
- head_readout: bfloat16 [4096], P('fsdp'), may hold values from -1.5 to 1.5
- parents: int32 [32], replicated, may hold values from -1 to 29, as said below
- placed: int32 [32], replicated, may hold values from 0 to 31, each once
- lengths: int32 [32], replicated, may hold values from 32 to 256, as said below
Outputs:
- token_values: float32 [8192], P('seg')
- branch_values: float32 [32], replicated
Inputs may be any that keep to these rules, and one draw needn't show every extreme that they name: parents[0] = -1 and parents[i] = i - 1 for 0 < i < 2; every other segment's parent has a smaller index, 1 or more. `placed`: a permutation. `lengths`: segments 0 to 1 are full.
All inputs are finite; a program needn't handle non-finite values.
Results may differ from a plain program's by a relative error of at most 0.015.
The roundings to bfloat16 on the way count: a program that leaves them out, or rounds other values in their place, can miss the bound.
Values may be sent and summed in bfloat16 or wider, within the bound.
No kernel may reach another device: no remote copies, remote signals or barrier semaphores. Data moves between devices by JAX's collectives and lax.ppermute only.
A program may use at most 128 MiB of HBM per device.

v0:
```python
import jax
import jax.numpy as jnp
from jax import lax
from jax.sharding import PartitionSpec as P

KEY_VALUE_HEADS = 4
HEAD_SIZE = 128


rope_base = 1000000.0


def swapped(value, axis, apart):
    mask = 2**apart
    pairs = [(source, source ^ mask) for source in range(lax.axis_size(axis))]
    return lax.ppermute(value, axis, pairs)


def tree_tables(parents, lengths, placed):
    segments = parents.shape[0]
    identity = jnp.eye(segments, dtype=jnp.float32)

    def stepper(ancestors, segment):
        parent_id = parents[segment]
        above_row = lax.dynamic_index_in_dim(
            ancestors, jnp.maximum(parent_id, 0), 0, keepdims=False
        )
        row_value = (
            jnp.where(parent_id >= 0, above_row, jnp.zeros_like(above_row)) + identity[segment]
        )
        return (lax.dynamic_update_index_in_dim(ancestors, row_value, segment, 0), None)

    ancestry, _ = lax.scan(
        stepper, jnp.zeros((segments, segments), jnp.float32), jnp.arange(segments, dtype=jnp.int32)
    )
    strict = ancestry - identity
    seg_ids = jnp.arange(segments, dtype=jnp.int32)
    lengths_real = lengths.astype(jnp.float32)
    offsets = jnp.dot(strict, lengths_real, precision=lax.Precision.HIGHEST)
    children = jnp.sum((parents[:, None] == seg_ids[None, :]).astype(jnp.float32), axis=0)
    leafy = (children < 0.5).astype(jnp.float32)
    placement = (placed[:, None] == seg_ids[None, :]).astype(jnp.float32)
    strict_slot = jnp.dot(
        jnp.dot(placement, strict, precision=lax.Precision.HIGHEST),
        placement.T,
        precision=lax.Precision.HIGHEST,
    )
    length_slot = jnp.dot(placement, lengths_real, precision=lax.Precision.HIGHEST)
    offset_slot = jnp.dot(placement, offsets, precision=lax.Precision.HIGHEST)
    leaf_slot = jnp.dot(placement, leafy, precision=lax.Precision.HIGHEST)
    return (ancestry, leafy, placement, strict_slot, length_slot, offset_slot, leaf_slot)


def rope(projected, positions, pair_index):
    paired = projected.reshape(projected.shape[0], projected.shape[1] // 2, 2)
    frequency = rope_base ** (-2.0 * pair_index / HEAD_SIZE)
    angles = positions[:, None] * frequency[None, :]
    cosine = jnp.cos(angles)
    sine_part = jnp.sin(angles)
    first_part = paired[:, :, 0]
    second_part = paired[:, :, 1]
    turned = jnp.stack(
        [
            first_part * cosine - second_part * sine_part,
            first_part * sine_part + second_part * cosine,
        ],
        axis=2,
    )
    return turned.reshape(projected.shape)


def join_parts(own_part, partner, fsdp_index, swap_bit):
    upper_half = fsdp_index // 2**swap_bit % 2 == 1
    return jnp.where(
        upper_half,
        jnp.concatenate([partner, own_part], axis=2),
        jnp.concatenate([own_part, partner], axis=2),
    )


def on_device(
    tokens, w_query, key_weight, value_weight, resid_head, head_readout, parents, placed, lengths
):
    seg_len = tokens.shape[0]
    seg_index = lax.axis_index("seg")
    fsdp_index = lax.axis_index("fsdp")
    shard_count = lax.axis_size("fsdp")
    ancestry, leafy, placement, strict_slot, length_slot, offset_slot, leaf_slot = tree_tables(
        parents, lengths, placed
    )
    segments = parents.shape[0]
    own_slot = (jnp.arange(segments, dtype=jnp.int32) == seg_index).astype(jnp.float32)
    own_ancestors = jnp.dot(own_slot, strict_slot, precision=lax.Precision.HIGHEST)
    own_length = jnp.dot(own_slot, length_slot, precision=lax.Precision.HIGHEST)
    own_offset = jnp.dot(own_slot, offset_slot, precision=lax.Precision.HIGHEST)
    own_leaf = jnp.dot(own_slot, leaf_slot, precision=lax.Precision.HIGHEST)
    query_width = w_query.shape[1]
    key_width = key_weight.shape[1]
    head_count = query_width // HEAD_SIZE
    incoming = (
        lax.all_gather(w_query, "seg", axis=0, tiled=True),
        lax.all_gather(key_weight, "seg", axis=0, tiled=True),
        lax.all_gather(value_weight, "seg", axis=0, tiled=True),
    )
    query_raw, key_raw, value_raw = tuple(
        (
            jnp.dot(tokens, weight_rows, preferred_element_type=jnp.float32)
            for weight_rows in incoming
        )
    )
    local_index = jnp.arange(seg_len, dtype=jnp.float32)
    positions = own_offset + local_index
    pair_query = (2 * jnp.arange(query_width // 2, dtype=jnp.int32) % HEAD_SIZE // 2).astype(
        jnp.float32
    )
    partner_key = (
        (fsdp_index * key_width + 2 * jnp.arange(key_width // 2, dtype=jnp.int32)) % HEAD_SIZE // 2
    ).astype(jnp.float32)
    query = (
        rope(query_raw, positions, pair_query)
        .astype(jnp.bfloat16)
        .reshape(seg_len, head_count, HEAD_SIZE)
    )
    key_proj = rope(key_raw, positions, partner_key).astype(jnp.bfloat16)
    stacked = jnp.stack([key_proj, value_raw.astype(jnp.bfloat16)])
    exchange_rounds = (shard_count // KEY_VALUE_HEADS).bit_length() - 1
    for swap_bit in range(exchange_rounds):
        partner = swapped(stacked, "fsdp", swap_bit)
        stacked = join_parts(stacked, partner, fsdp_index, swap_bit)
    incoming = lax.all_gather(stacked, "seg", axis=1, tiled=True)
    piece_width = incoming.shape[1]
    token_ids = jnp.arange(piece_width, dtype=jnp.int32)
    key_slot = token_ids // seg_len
    key_index = (token_ids % seg_len).astype(jnp.float32)
    onehot = (key_slot[:, None] == jnp.arange(segments, dtype=jnp.int32)[None, :]).astype(
        jnp.float32
    )
    ancestral = jnp.dot(onehot, own_ancestors, precision=lax.Precision.HIGHEST) > 0.5
    key_length = jnp.dot(onehot, length_slot, precision=lax.Precision.HIGHEST)
    visible = (ancestral & (key_index < key_length))[None, :] | (key_slot == seg_index)[None, :] & (
        key_index[None, :] <= local_index[:, None]
    )
    peak_score = jnp.full((head_count, seg_len), -1e30, jnp.float32)
    scores = jnp.einsum(
        "qhd,kd->hqk", query, incoming[0], preferred_element_type=jnp.float32
    ) * HEAD_SIZE ** (-0.5)
    masked = jnp.where(visible[None], scores, -1e30)
    new_peak = jnp.maximum(peak_score, jnp.max(masked, axis=2))
    weights = jnp.where(visible[None], jnp.exp(scores - new_peak[..., None]), 0.0)
    denominator = jnp.sum(weights, axis=2)
    accumulated = jnp.einsum(
        "hqk,kd->hqd", weights.astype(jnp.bfloat16), incoming[1], preferred_element_type=jnp.float32
    )
    peak_score, denominator, accumulated = (new_peak, denominator, accumulated)
    mixed = (accumulated / denominator[..., None]).astype(jnp.bfloat16)
    readout = head_readout.reshape(head_count, HEAD_SIZE)
    partial_value = jnp.einsum("hqd,hd->q", mixed, readout, preferred_element_type=jnp.float32)
    residual = jnp.dot(tokens, resid_head, preferred_element_type=jnp.float32)
    live_mask = local_index < own_length
    last_mask = local_index == own_length - 1.0
    head_total = lax.psum(partial_value, "fsdp")
    token_values = jnp.where(live_mask, residual + head_total, 0.0)
    leaf_value = jnp.sum(jnp.where(last_mask, token_values, 0.0)) * own_leaf
    leaves = lax.psum(own_slot * leaf_value, "seg")
    leaf_seg = jnp.dot(placement.T, leaves, precision=lax.Precision.HIGHEST)
    backed = jnp.dot(ancestry.T, leaf_seg, precision=lax.Precision.HIGHEST) / jnp.dot(
        ancestry.T, leafy, precision=lax.Precision.HIGHEST
    )
    return (token_values, backed)


def solution(mesh):
    in_specs = (
        P("seg", None),
        P("seg", "fsdp"),
        P("seg", "fsdp"),
        P("seg", "fsdp"),
        P(),
        P("fsdp"),
        P(),
        P(),
        P(),
    )
    out_specs = (P("seg"), P())
    return jax.shard_map(
        on_device, mesh=mesh, in_specs=in_specs, out_specs=out_specs, check_vma=False
    )
```

profile of v0, /device:TPU:1, one launch (start us, length us, event | category | flops | bytes accessed | tf_op | source)
XLA Modules:
  0.0 452.0 jit_solution(3521624800375498331)
XLA Ops:
  7.3 0.7 all-gather.5.cloned.1.call-update
  8.0 38.9 %all_gather.12 = bf16[8192,32]{0,1:T(8,128)(2,1)S(1)} all-gather(bf16[256,32]{0,1:T(8,128)(2,1)} %param.13), channel_id=1, replica_groups=mesh['seg'=32,'fsdp'=16] {'seg'}, dimensions={0}, use_global_device_ids=true | all-gather | bytes 540672 | tf_op jit(solution)/shard_map/all_gather | solution.py:102
  46.9 3.5 fusion.89
  50.6 143.7 %while.10 = (s32[]{:T(128)}, f32[32,32]{1,0:T(8,128)S(1)}, s32[32]{0:T(128)S(1)}, s32[32]{0:T(128)S(1)}, f32[32,32]{1,0:T(8,128)S(1)}, /*index=5*/s32[]{:T(128)}, s32[]{:T(128)}, s32[]{:T(128)}, s32[1]{0:T(128)}) while((s32[]{:T(128)}, f32[32,32]{1,0:T(8,128)S(1)}, s32[32]{0:T(128)S(1)}, s32[32]{0:T(128)S(1)}, f32[32,32]{1,0:T(8,128)S(1)}, ...), condition=%wide.region_1.2_spmd, body=%wide.region_0.1_spmd.sunk | while | flops 71 | bytes 825 | solution.py:33
  53.2 0.6 dynamic_slice.23
  57.6 0.6 dynamic_slice.23
  59.6 0.6 dynamic_slice.22
  62.1 0.6 dynamic_slice.23
  64.1 0.6 dynamic_slice.22
  68.6 0.6 dynamic_slice.22
  71.1 0.6 dynamic_slice.23
  73.1 0.6 dynamic_slice.22
  75.6 0.6 dynamic_slice.23
  77.6 0.6 dynamic_slice.22
  80.1 0.6 dynamic_slice.23
  82.1 0.6 dynamic_slice.22
  84.6 0.6 dynamic_slice.23
  86.6 0.6 dynamic_slice.22
  89.1 0.6 dynamic_slice.23
  91.1 0.6 dynamic_slice.22
  98.1 0.6 dynamic_slice.23
  100.0 0.6 dynamic_slice.22
  102.6 0.6 dynamic_slice.23
  104.5 0.6 dynamic_slice.22
  111.5 0.6 dynamic_slice.23
  194.5 0.8 fusion.27
  195.3 0.7 iota_add_fusion
  196.2 33.7 %all_gather.13 = bf16[8192,32]{0,1:T(8,128)(2,1)S(1)} all-gather(bf16[256,32]{0,1:T(8,128)(2,1)S(1)} %copy-done.2), channel_id=1, replica_groups=mesh['seg'=32,'fsdp'=16] {'seg'}, dimensions={0}, use_global_device_ids=true | all-gather | bytes 540672 | tf_op jit(solution)/shard_map/all_gather | solution.py:103
  229.9 3.5 fusion.12
  233.4 1.9 collective-permute-start
  235.4 2.7 collective-permute-done
  238.1 3.2 collective-permute-start.1
  241.4 3.3 collective-permute-done.1
  244.6 0.7 maximum_select_fusion
  245.4 0.8 select_reduce_fusion
  247.1 0.8 fusion.28
  249.4 3.4 fusion.88
  252.7 7.5 %fusion.9 = pred[256,8192]{0,1:T(8,128)(4,1)S(1)} fusion(f32[8192]{0:T(1024)S(1)} %fusion.46, pred[8192]{0:T(1024)(128)(4,1)S(1)} %get-tuple-element.55, pred[8192]{0:T(1024)(128)(4,1)S(1)} %get-tuple-element.54), kind=kLoop, calls=%fused_computation.12 | loop fusion | flops 6291456 | bytes 2146304 | tf_op jit(solution)/shard_map/or | solution.py:140
  260.2 5.3 %fusion.90 = f32[256,256]{0,1:T(8,128)S(1)} fusion(bf16[256,8192]{1,0:T(8,128)(2,1)} %param.11, bf16[8192,256]{1,0:T(8,128)(2,1)} %all-gather.5.cloned.1.call-done), kind=kOutput, calls=%fused_computation.138 | convolution fusion | flops 1073741824 | bytes 8650752 | tf_op jit(solution)/shard_map/dot_general | solution.py:107
  266.9 56.2 %all-gather.3.cloned.1.call-done = bf16[2,8192,128]{1,2,0:T(8,128)(2,1)} async-done(((bf16[2,256,128]{1,2,0:T(8,128)(2,1)}), bf16[2,8192,128]{1,2,0:T(8,128)(2,1)}) %all-gather.3.cloned.1.call-update) | async-done | bytes 4194320 | tf_op jit(solution)/shard_map/all_gather | solution.py:130
  323.1 4.0 fusion.1
  327.2 3.9 fusion.4
  331.1 1.8 copy-done.1
  332.9 10.0 %fusion.23 = f32[1,256,1]{1,0,2:T(1,128)S(1)} fusion(bf16[2,8192,128]{1,2,0:T(8,128)(2,1)} %all-gather.3.cloned.1.call-done, f32[8192,256,2]{1,0,2:T(8,128)} %copy-done.1, f32[2,256]{1,0:T(2,128)S(1)} %broadcast_maximum_fusion, pred[256,8192]{0,1:T(8,128)(4,1)S(1)} %fusion.9, f32[2,256]{1,0:T(2,128)S(1)} %fusion.4, bf16[2,128,1]{1,0,2:T(2,128)(2,1)S(1)} %bitcast.133), kind=kOutput, calls=%fused_computation.31 | convolution fusion | flops 1090781184 | bytes 20977152 | tf_op jit(solution)/shard_map/hqd,hd->q/dot_general | solution.py:157
  342.9 38.5 %psum.14 = f32[256]{0:T(256)S(1)} all-reduce(f32[256]{0:T(256)S(1)} %bitcast.137), channel_id=1, replica_groups=mesh['seg'=32,'fsdp'=16] {'fsdp'}, use_global_device_ids=true, to_apply=%region_4.5 | all-reduce | flops 256 | bytes 2048 | tf_op jit(solution)/shard_map/psum | solution.py:161
  381.4 1.9 fusion.72
  384.6 59.8 %psum.15 = f32[32]{0:T(128)S(1)} all-reduce(f32[32]{0:T(128)S(1)} %fusion.76), channel_id=1, replica_groups=mesh['seg'=32,'fsdp'=16] {'seg'}, use_global_device_ids=true, to_apply=%region_7.8 | all-reduce | flops 32 | bytes 256 | tf_op jit(solution)/shard_map/psum | solution.py:164
  444.5 0.7 fusion.15
  (160 shorter events, 30.7 us)
Async XLA Ops:
  7.2 325.7 %copy-start = (bf16[256]{0:T(256)(128)(2,1)S(1)}, bf16[256]{0:T(256)(128)(2,1)}, u32[]{:S(2)}) copy-start(bf16[256]{0:T(256)(128)(2,1)} %param.16) | copy-start | bytes 1540
  7.2 43.4 %copy-start.5 = (s32[32]{0:T(128)S(1)}, s32[32]{0:T(128)}, u32[]{:S(2)}) copy-start(s32[32]{0:T(128)} %param.17) | copy-start | bytes 388
  7.2 187.1 %copy-start.4 = (s32[32]{0:T(128)S(1)}, s32[32]{0:T(128)}, u32[]{:S(2)}) copy-start(s32[32]{0:T(128)} %param.19) | copy-start | bytes 388
  7.2 187.3 %copy-start.6 = (s32[32]{0:T(128)S(1)}, s32[32]{0:T(128)}, u32[]{:S(2)}) copy-start(s32[32]{0:T(128)} %param.18) | copy-start | bytes 388
  7.2 189.0 %copy-start.2 = (bf16[256,32]{0,1:T(8,128)(2,1)S(1)}, bf16[256,32]{0,1:T(8,128)(2,1)}, u32[]{:S(2)}) copy-start(bf16[256,32]{0,1:T(8,128)(2,1)} %param.14) | copy-start | bytes 49156
  7.2 253.0 %all-gather.5.cloned.1.call-start = ((), (), s32[]{:S(2)}) async-start(), calls=%async_computation.1 | async-start | bytes 4325376 | tf_op jit(solution)/shard_map/all_gather | solution.py:101
  8.0 315.2 %all-gather.3.cloned.1.call-start = ((), (), s32[]{:S(2)}) async-start(), calls=%async_computation | async-start | bytes 4325376 | tf_op jit(solution)/shard_map/all_gather | solution.py:130
  50.5 194.9 %copy-start.3 = (bf16[8192]{0:T(1024)(128)(2,1)S(1)}, bf16[8192]{0:T(1024)(128)(2,1)}, u32[]{:S(2)}) copy-start(bf16[8192]{0:T(1024)(128)(2,1)} %param.15) | copy-start | bytes 49156
  233.4 4.7 %collective-permute-start = (bf16[2,256,32]{1,2,0:T(8,128)(2,1)S(1)}, bf16[2,256,32]{1,2,0:T(8,128)(2,1)S(1)}, u32[]{:S(2)}, u32[]{:S(2)}) collective-permute-start(bf16[2,256,32]{1,2,0:T(8,128)(2,1)S(1)} %pad_maximum_fusion.1), channel_id=1, source_target_pairs={{0,1},{1,0},{2,3},{3,2},{4,5},{5,4},{6,7},{7,6},{8,9},{9,8},{10,11... | collective-permute-start | bytes 98312 | tf_op jit(solution)/shard_map/ppermute | solution.py:16
  238.1 6.5 %collective-permute-start.1 = (bf16[2,256,64]{1,2,0:T(8,128)(2,1)S(1)}, bf16[2,256,64]{1,2,0:T(8,128)(2,1)S(1)}, u32[]{:S(2)}, u32[]{:S(2)}) collective-permute-start(bf16[2,256,64]{1,2,0:T(8,128)(2,1)S(1)} %maximum_select_fusion.1), channel_id=1, source_target_pairs={{0,2},{1,3},{2,0},{3,1},{4,6},{5,7},{6,4},{7,5},{8,10},{9,11},{10,... | collective-permute-start | bytes 196616 | tf_op jit(solution)/shard_map/ppermute | solution.py:16
  327.1 5.7 %copy-start.1 = (f32[8192,256,2]{1,0,2:T(8,128)}, f32[8192,256,2]{1,0,2:T(8,128)S(1)}, u32[]{:S(2)}) copy-start(f32[8192,256,2]{1,0,2:T(8,128)S(1)} %get-tuple-element.53) | copy-start | bytes 50331652
Sparse Core Ops, SparseCore 0:
  10.2 75.8 all-gather.4
  245.5 77.6 all-gather.2
where the time goes:
time: 454 us; the launch traced here: 452 us
  blocking collectives  171 us (38%)
  loops' own time  104 us (23%)
  waiting for transfers between devices  62.9 us (14%)
  local copies, waits for them, and re-layouts  41.4 us (9%)
  matrix products  34.7 us (8%)
  between operations  16.4 us (4%)
  other arithmetic  16 us (4%)
  starting transfers between devices  5.21 us (1%)
    another operation x1, loops' own time, tree_tables(): lax.scan(stepper, jnp.zeros((segments, segments), jnp.float32), jnp.arang...  104 us
    psum x1, blocking collectives, on_device(): leaves = lax.psum(own_slot * leaf_value, 'seg')  59.8 us
    all_gather x1, waiting for transfers between devices, on_device(): incoming = lax.all_gather(stacked, 'seg', axis=1, tiled=True)  56.2 us
    all_gather x1, blocking collectives, on_device(): lax.all_gather(key_weight, 'seg', axis=0, tiled=True)  38.9 us
    psum x1, blocking collectives, on_device(): head_total = lax.psum(partial_value, 'fsdp')  38.5 us
    all_gather x1, blocking collectives, on_device(): lax.all_gather(value_weight, 'seg', axis=0, tiled=True)  33.7 us
    dynamic_slice x32, local copies, waits for them, and re-layouts, tree_tables(): lax.scan(stepper, jnp.zeros((segments, segments), jnp.float32), jnp.arang...  18.8 us
    dynamic_slice x32, local copies, waits for them, and re-layouts, stepper(): parent_id = parents[segment]  18.8 us
  transfers between devices with their start and end apart: 4, of which 3 were waited for; matrix products, arithmetic and copies ran while one was open for 15% of the time, Pallas kernels for 0%

commit v1 on v0

v1 whole, which is shorter than its diff:
```python
import jax
import jax.numpy as jnp
from jax import lax
from jax.experimental import pallas as pl
from jax.experimental.pallas import tpu as pltpu
from jax.sharding import Mesh
from jax.sharding import PartitionSpec as P

KEY_VALUE_HEADS = 4
HEAD_SIZE = 128
ROPE_BASE = 1000000.0
SEG = ("y", "zl", "c")
FSDP = ("zh", "x")
META = 72
VMEM_LIMIT = 40 * 1024 * 1024

VMEM_SPEC = pl.BlockSpec(memory_space=pltpu.VMEM)
SMEM_SPEC = pl.BlockSpec(memory_space=pltpu.SMEM)


def tree_kernel(seg_ref, parents_ref, placed_ref, lengths_ref, meta_ref, table_ref, slot_of):
    segments = parents_ref.shape[0]
    slot = seg_ref[0]
    own = placed_ref[slot]

    def place(j, carry):
        slot_of[placed_ref[j]] = j
        return carry

    lax.fori_loop(0, segments, place, 0)

    def clear(j, carry):
        meta_ref[j] = 0
        return carry

    lax.fori_loop(0, META, clear, 0)

    def above(state):
        seg, count, offset = state
        meta_ref[8 + count] = slot_of[seg]
        meta_ref[40 + count] = lengths_ref[seg]
        return parents_ref[seg], count + 1, offset + lengths_ref[seg]

    _, count, offset = lax.while_loop(
        lambda state: state[0] >= 0, above, (parents_ref[own], jnp.int32(0), jnp.int32(0))
    )
    meta_ref[0] = count
    meta_ref[1] = offset
    meta_ref[2] = lengths_ref[own]

    row = lax.broadcasted_iota(jnp.int32, (128, 128), 0)
    col = lax.broadcasted_iota(jnp.int32, (128, 128), 1)
    row_s = lax.broadcasted_iota(jnp.int32, (segments, 128), 0)
    col_s = lax.broadcasted_iota(jnp.int32, (segments, 128), 1)
    parent_of = jnp.full((segments, 128), -1, jnp.int32)
    held = jnp.full((segments, 128), -1, jnp.int32)
    for i in range(segments):
        parent_of = jnp.where(row_s == i, parents_ref[i], parent_of)
        held = jnp.where(row_s == i, placed_ref[i], held)
    step = jnp.where(parent_of == col_s, 1.0, 0.0)
    step = jnp.concatenate([step, jnp.zeros((128 - segments, 128), jnp.float32)], axis=0)
    ancestry = jnp.where(row == col, 1.0, 0.0) + step

    def times(a, b):
        return jnp.dot(
            a.astype(jnp.bfloat16), b.astype(jnp.bfloat16), preferred_element_type=jnp.float32
        )

    power = step
    reach = 1
    while 2 * reach <= segments:
        power = times(power, power)
        ancestry = ancestry + times(power, ancestry)
        reach *= 2
    children = jnp.sum(step, axis=0, keepdims=True)
    leafy = jnp.where((children < 0.5) & (col[:1] < segments), 1.0, 0.0)
    leaves = times(jnp.broadcast_to(leafy, (8, 128)), ancestry)[:1]
    placement = jnp.where(held == col_s, 1.0, 0.0)
    share = times(placement * leafy, ancestry)
    table_ref[...] = jnp.where(col_s < segments, share / jnp.maximum(leaves, 1.0), 0.0)


def weights_kernel(seg_ref, value_ref, readout_ref, key_ref, resid_ref, out_ref):
    quarters, part, rows = value_ref.shape
    value = value_ref[...].reshape(quarters * part, rows)
    folded = jnp.dot(readout_ref[...], value, preferred_element_type=jnp.float32)
    heads = readout_ref.shape[0]
    high = folded.astype(jnp.bfloat16).astype(jnp.float32)
    low = folded - high
    start = pl.multiple_of(seg_ref[0] * rows, 128)
    resid = resid_ref[:, pl.ds(start, rows)].astype(jnp.float32)
    pad = jnp.zeros((7 - 2 * heads, rows), jnp.float32)
    piece = jnp.concatenate([high, low, resid, pad], axis=0)
    piece = jnp.concatenate([key_ref[...].astype(jnp.float32), piece], axis=0).astype(jnp.bfloat16)
    for i in range(out_ref.shape[0]):
        out_ref[i] = piece


def turned(raw, cosine, sine, axis):
    extent = raw.shape[axis]
    index = lax.broadcasted_iota(jnp.int32, raw.shape, axis)
    after = pltpu.roll(raw, extent - 1, axis)
    before = pltpu.roll(raw, 1, axis)
    return raw * cosine + jnp.where(index % 2 == 0, after, before) * sine


def keys_kernel(
    quarter_ref, tokens_ref, weights_ref, cosine_ref, sine_ref, out_ref, resid_ref, total
):
    step = pl.program_id(0)
    chunks, _, depth = weights_ref.shape

    @pl.when(step == 0)
    def _():
        total[...] = jnp.zeros_like(total)

    acc = total[...]
    for i in range(chunks):
        acc += lax.dot_general(
            weights_ref[i],
            tokens_ref[:, i * depth : (i + 1) * depth],
            (((1,), (1,)), ((), ())),
            preferred_element_type=jnp.float32,
        )
    total[...] = acc

    @pl.when(step == pl.num_programs(0) - 1)
    def _():
        width = total.shape[0] - 8
        start = pl.multiple_of(quarter_ref[0] * width, width)
        raw = total[:width]
        keys = turned(raw, cosine_ref[pl.ds(start, width)], sine_ref[pl.ds(start, width)], 0)
        last = total[width:]
        row = lax.broadcasted_iota(jnp.int32, last.shape, 0)
        summed = last + pltpu.roll(last, 6, 0)
        high = summed.astype(jnp.bfloat16).astype(jnp.float32)
        low = pltpu.roll(summed - high, 2, 0)
        tail = jnp.where(row < 2, high, jnp.where(row < 4, low, 0.0))
        piece = jnp.concatenate([keys, tail], axis=0).astype(jnp.bfloat16)
        for i in range(out_ref.shape[0]):
            out_ref[i] = piece
        resid_ref[...] = last[4:5]


def attention_kernel(
    place_ref,
    meta_ref,
    query_ref,
    cosine_ref,
    sine_ref,
    near_ref,
    far_ref,
    near_value_ref,
    far_value_ref,
    out_ref,
    query_buf,
    top,
    bottom,
    summed,
):
    seg_len = query_ref.shape[0]
    heads = query_ref.shape[1] // HEAD_SIZE
    own = place_ref[0]
    core = place_ref[1]
    raw = query_ref[...].T
    for h in range(heads):
        query_buf[h] = turned(
            raw[h * HEAD_SIZE : (h + 1) * HEAD_SIZE], cosine_ref[...], sine_ref[...], 0
        ).astype(jnp.bfloat16)
    scale = HEAD_SIZE ** (-0.5)
    key_at = lax.broadcasted_iota(jnp.int32, (seg_len, seg_len), 0)
    query_at = lax.broadcasted_iota(jnp.int32, (seg_len, seg_len), 1)

    def scores(keys, h):
        return scale * lax.dot_general(
            keys, query_buf[h], (((0,), (0,)), ((), ())), preferred_element_type=jnp.float32
        )

    own_keys = near_ref[:, own // 2].reshape(HEAD_SIZE, seg_len)
    own_values = near_value_ref[own // 2]
    for h in range(heads):
        masked = jnp.where(key_at <= query_at, scores(own_keys, h), -1e30)
        peak = jnp.max(masked, axis=0, keepdims=True)
        weights = jnp.where(key_at <= query_at, jnp.exp(masked - peak), 0.0)
        top[h] = peak
        bottom[h] = jnp.sum(weights, axis=0, keepdims=True)
        summed[h] = jnp.dot(
            own_values, weights.astype(jnp.bfloat16), preferred_element_type=jnp.float32
        )

    def visit(n, key_source, value_source):
        slot = meta_ref[8 + n]
        length = meta_ref[40 + n]
        keys = key_source[:, slot // 2].reshape(HEAD_SIZE, seg_len)
        values = value_source[slot // 2]
        for h in range(heads):
            masked = jnp.where(key_at < length, scores(keys, h), -1e30)
            peak = jnp.maximum(top[h], jnp.max(masked, axis=0, keepdims=True))
            shrink = jnp.exp(top[h] - peak)
            weights = jnp.where(key_at < length, jnp.exp(masked - peak), 0.0)
            top[h] = peak
            bottom[h] = bottom[h] * shrink + jnp.sum(weights, axis=0, keepdims=True)
            summed[h] = summed[h] * shrink + jnp.dot(
                values, weights.astype(jnp.bfloat16), preferred_element_type=jnp.float32
            )

    def one(n, carry):
        @pl.when(meta_ref[8 + n] % 2 == core)
        def _():
            visit(n, near_ref, near_value_ref)

        @pl.when(meta_ref[8 + n] % 2 != core)
        def _():
            visit(n, far_ref, far_value_ref)

        return carry

    lax.fori_loop(0, meta_ref[0], one, 0)
    result = jnp.zeros((1, seg_len), jnp.float32)
    for h in range(heads):
        both = summed[h]
        result += (both[h : h + 1] + both[2 + h : 3 + h]) / bottom[h]
    for i in range(out_ref.shape[0]):
        out_ref[i : i + 1] = result


def finish_kernel(meta_ref, parts_ref, resid_ref, out_ref, leaf_ref):
    total = resid_ref[...] + jnp.sum(parts_ref[...], axis=0, keepdims=True)
    index = lax.broadcasted_iota(jnp.int32, total.shape, 1)
    length = meta_ref[2]
    values = jnp.where(index < length, total, 0.0)
    out_ref[...] = values
    leaf = jnp.sum(jnp.where(index == length - 1, values, 0.0), axis=1, keepdims=True)
    leaf_ref[...] = jnp.broadcast_to(leaf, leaf_ref.shape)


def gathered(value, axis):
    return lax.all_to_all(value, axis, 0, 0)


def on_device(
    tokens, w_query, key_weight, value_weight, resid_head, head_readout, parents, placed, lengths
):
    seg_len, model_width = tokens.shape
    seg_index = lax.axis_index(SEG).astype(jnp.int32)
    quarter = lax.axis_index("x").astype(jnp.int32)
    core = lax.axis_index("c").astype(jnp.int32)
    segments = parents.shape[0]
    fsdp_size = lax.axis_size(FSDP)
    quarters = lax.axis_size("x")
    pairs = segments // 2
    width = key_weight.shape[1]
    heads = w_query.shape[1] // HEAD_SIZE
    params = pltpu.CompilerParams(vmem_limit_bytes=VMEM_LIMIT)

    query_weight = lax.all_gather(w_query, SEG, axis=0, tiled=True)

    meta, table = pl.pallas_call(
        tree_kernel,
        out_shape=(
            jax.ShapeDtypeStruct((META,), jnp.int32),
            jax.ShapeDtypeStruct((segments, 128), jnp.float32),
        ),
        in_specs=[SMEM_SPEC] * 4,
        out_specs=(SMEM_SPEC, VMEM_SPEC),
        scratch_shapes=[pltpu.SMEM((segments,), jnp.int32)],
        compiler_params=params,
        name="tree",
    )(seg_index.reshape(1), parents, placed, lengths)

    positions = meta[1].astype(jnp.float32) + jnp.arange(seg_len, dtype=jnp.float32)
    dims = jnp.arange(HEAD_SIZE, dtype=jnp.int32)
    frequency = ROPE_BASE ** (-2.0 * (dims // 2).astype(jnp.float32) / HEAD_SIZE)
    angles = frequency[:, None] * positions[None, :]
    cosine = jnp.cos(angles)
    sine = jnp.sin(angles) * jnp.where(dims % 2 == 0, -1.0, 1.0)[:, None]

    values_x = gathered(jnp.broadcast_to(value_weight.T[None], (quarters, width, seg_len)), "x")
    rows = width + 8
    pieces = pl.pallas_call(
        weights_kernel,
        out_shape=jax.ShapeDtypeStruct((segments, rows, seg_len), jnp.bfloat16),
        in_specs=[SMEM_SPEC] + [VMEM_SPEC] * 4,
        out_specs=VMEM_SPEC,
        compiler_params=params,
        name="fold_weights",
    )(
        seg_index.reshape(1),
        values_x,
        head_readout.reshape(heads, HEAD_SIZE),
        key_weight.T,
        resid_head.reshape(1, model_width),
    )
    key_weights = gathered(pieces, SEG)

    steps = 8
    keys, residual = pl.pallas_call(
        keys_kernel,
        out_shape=(
            jax.ShapeDtypeStruct((pairs, rows, seg_len), jnp.bfloat16),
            jax.ShapeDtypeStruct((1, seg_len), jnp.float32),
        ),
        grid=(steps,),
        in_specs=[
            SMEM_SPEC,
            pl.BlockSpec((seg_len, model_width // steps), lambda k: (0, k)),
            pl.BlockSpec((segments // steps, rows, seg_len), lambda k: (k, 0, 0)),
            pl.BlockSpec((HEAD_SIZE, seg_len), lambda k: (0, 0)),
            pl.BlockSpec((HEAD_SIZE, seg_len), lambda k: (0, 0)),
        ],
        out_specs=(
            pl.BlockSpec((pairs, rows, seg_len), lambda k: (0, 0, 0)),
            pl.BlockSpec((1, seg_len), lambda k: (0, 0)),
        ),
        scratch_shapes=[pltpu.VMEM((rows, seg_len), jnp.float32)],
        compiler_params=params,
        name="project_keys",
    )(quarter.reshape(1), tokens, key_weights, cosine, sine)

    keys_yz = gathered(keys, ("y", "zl"))
    near_values = keys_yz[:, width:]
    swap = [(0, 1), (1, 0)]
    far_values = lax.ppermute(near_values, "c", swap)
    near = gathered(
        jnp.broadcast_to(keys_yz[None, :, :width], (quarters, pairs, width, seg_len)), "x"
    )
    far = lax.ppermute(near, "c", swap)

    query_raw = jnp.dot(tokens, query_weight, preferred_element_type=jnp.float32)
    mixed = pl.pallas_call(
        attention_kernel,
        out_shape=jax.ShapeDtypeStruct((fsdp_size, seg_len), jnp.float32),
        in_specs=[SMEM_SPEC] * 2 + [VMEM_SPEC] * 7,
        out_specs=VMEM_SPEC,
        scratch_shapes=[
            pltpu.VMEM((heads, HEAD_SIZE, seg_len), jnp.bfloat16),
            pltpu.VMEM((heads, 1, seg_len), jnp.float32),
            pltpu.VMEM((heads, 1, seg_len), jnp.float32),
            pltpu.VMEM((heads, 8, seg_len), jnp.float32),
        ],
        compiler_params=params,
        name="attend",
    )(
        jnp.stack([seg_index, core]),
        meta,
        query_raw,
        cosine,
        sine,
        near,
        far,
        near_values,
        far_values,
    )
    parts = gathered(mixed, FSDP)
    token_values, leaf_rows = pl.pallas_call(
        finish_kernel,
        out_shape=(
            jax.ShapeDtypeStruct((1, seg_len), jnp.float32),
            jax.ShapeDtypeStruct((segments, 128), jnp.float32),
        ),
        in_specs=[SMEM_SPEC, VMEM_SPEC, VMEM_SPEC],
        out_specs=(VMEM_SPEC, VMEM_SPEC),
        compiler_params=params,
        name="token_values",
    )(meta, parts, residual)
    leaves = gathered(leaf_rows, SEG)
    branch = jnp.sum(leaves * table, axis=0)[:segments]
    return (token_values.reshape(seg_len), branch)


def solution(mesh):
    fine = Mesh(mesh.devices.reshape(8, 2, 2, 4, 4), SEG + FSDP)
    in_specs = (
        P(SEG, None),
        P(SEG, FSDP),
        P(SEG, FSDP),
        P(SEG, FSDP),
        P(),
        P(FSDP),
        P(),
        P(),
        P(),
    )
    out_specs = (P(SEG), P())
    return jax.shard_map(
        on_device, mesh=fine, in_specs=in_specs, out_specs=out_specs, check_vma=False
    )
```

time: 454 us -> 156 us (0.34)
  loops' own time: 104 us -> 0 us
  blocking collectives: 171 us -> 68 us
  waiting for transfers between devices: 62.9 us -> 23.8 us
  local copies, waits for them, and re-layouts: 41.4 us -> 8.42 us
  matrix products: 34.7 us -> 4.71 us
  starting transfers between devices: 5.21 us -> 23.1 us
  other arithmetic: 16 us -> 1.18 us
  Pallas kernels: 0 us -> 11.1 us
    another operation x1 -> x0, loops' own time: 104 us -> none  [tree_tables(): lax.scan(stepper, jnp.zeros((segments, segments), jnp.float32), jnp.arang...]
    psum x2 -> x0, blocking collectives: 98.3 us -> none  [the longest x1 59.8 us: on_device(): leaves = lax.psum(own_slot * leaf_value, 'seg')]
    all_gather x2 -> x0, blocking collectives: 72.6 us -> none  [the longest x1 38.9 us: on_device(): lax.all_gather(key_weight, 'seg', axis=0, tiled=True)]
    all_to_all x0 -> x4, blocking collectives: none -> 68 us  [gathered(): return lax.all_to_all(value, axis, 0, 0)]
    all_gather x2 -> x1, waiting for transfers between devices: 56.2 us -> 0.02 us  [on_device(): query_weight = lax.all_gather(w_query, SEG, axis=0, tiled=True)]
    dynamic_slice x64 -> x0, local copies, waits for them, and re-layouts: 37.5 us -> none  [the longest x32 18.8 us: tree_tables(): lax.scan(stepper, jnp.zeros((segments, segments), jnp.float32), jnp.arang...]
    dot_general x18 -> x1, matrix products: 34.7 us -> 4.71 us  [on_device(): jnp.dot(tokens, query_weight, preferred_element_type=jnp.float32)]
    all_to_all x0 -> x2, waiting for transfers between devices: none -> 23.1 us  [gathered(): return lax.all_to_all(value, axis, 0, 0)]
  transfers between devices with their start and end apart: 4 -> 5, of which waited for: 3 -> 2; matrix products, arithmetic and copies ran while one was open for 15% -> 5% of each run, Pallas kernels for 0% -> 4%
where the time goes in v1:
time: 156 us; the launch traced here: 155 us
  blocking collectives  68 us (44%)
  waiting for transfers between devices  23.8 us (15%)
  starting transfers between devices  23.1 us (15%)
  between operations  14.8 us (9%)
  Pallas kernels  11.1 us (7%)
  local copies, waits for them, and re-layouts  8.42 us (5%)
  matrix products  4.71 us (3%)
    all_to_all x4, blocking collectives, gathered(): return lax.all_to_all(value, axis, 0, 0)  68 us
    all_to_all x2, waiting for transfers between devices, gathered(): return lax.all_to_all(value, axis, 0, 0)  23.1 us
    all_to_all x2, starting transfers between devices, gathered(): return lax.all_to_all(value, axis, 0, 0)  16 us
    unnamed x13, local copies, waits for them, and re-layouts  5.57 us
    ppermute x1, starting transfers between devices, on_device(): far = lax.ppermute(near, 'c', swap)  5.17 us
    dot_general x1, matrix products, on_device(): jnp.dot(tokens, query_weight, preferred_element_type=jnp.float32)  4.71 us
    pallas_call x1, Pallas kernels, on_device(): pl.pallas_call(attention_kernel, out_shape=jax.ShapeDtypeStruct((fsdp_siz...  4.12 us
  transfers between devices with their start and end apart: 5, of which 2 were waited for; matrix products, arithmetic and copies ran while one was open for 5% of the time, Pallas kernels for 4%

profile of v1, /device:TPU:1, one launch (start us, length us, event | category | flops | bytes accessed | tf_op | source)
XLA Modules:
  0.0 155.2 jit_solution(1507986941443285518)
XLA Ops:
  7.2 0.0 all-gather.2.cloned.1.call-start
  7.2 0.7 all-gather.2.cloned.1.call-update
  7.9 1.3 broadcast_in_dim.14
  9.2 4.8 %all-to-all-start = ((bf16[4,32,256]{2,1,0:T(8,128)(2,1)}), bf16[4,32,256]{2,1,0:T(8,128)(2,1)S(1)}, u32[]{:S(2)}, u32[]{:S(2)}) async-start(bf16[4,32,256]{2,1,0:T(8,128)(2,1)} %broadcast_in_dim.14), calls=%async_computation | async-start | bytes 131072 | tf_op jit(solution)/shard_map/all_to_all | solution.py:238
  14.1 0.7 reshape.61.resid_ref
  14.8 3.7 %all-to-all-done.value_ref = bf16[4,32,256]{2,1,0:T(8,128)(2,1)S(1)} async-done(((bf16[4,32,256]{2,1,0:T(8,128)(2,1)}), bf16[4,32,256]{2,1,0:T(8,128)(2,1)S(1)}, u32[]{:S(2)}, u32[]{:S(2)}) %all-to-all-start) | async-done | bytes 65568 | tf_op jit(solution)/shard_map/all_to_all | solution.py:238
  18.6 0.0 copy-start.1
  18.6 0.7 copy-done.1
  19.3 0.0 copy-start.2
  19.3 0.7 copy-done.2
  19.9 1.0 fold_weights.1
  20.9 11.2 %all-to-all-start.1 = ((bf16[32,40,256]{2,1,0:T(8,128)(2,1)}), bf16[32,40,256]{2,1,0:T(8,128)(2,1)S(1)}, u32[]{:S(2)}, u32[]{:S(2)}) async-start(bf16[32,40,256]{2,1,0:T(8,128)(2,1)} %fold_weights.1), calls=%async_computation.1 | async-start | bytes 1310720 | tf_op jit(solution)/shard_map/all_to_all | solution.py:238
  32.1 0.0 copy-start.3
  32.1 0.6 copy-done.3
  32.8 0.0 copy-start.4
  32.8 0.7 copy-done.4
  33.4 0.0 copy-start.5
  33.4 0.7 copy-done.5
  34.1 2.3 %tree.1 = (s32[72]{0:T(128)S(1)}, f32[32,128]{1,0:T(8,128)S(1)}) custom-call(s32[1]{0:T(128)} %bitcast.seg_ref, s32[32]{0:T(128)S(1)} %copy-done.3, s32[32]{0:T(128)S(1)} %copy-done.4, s32[32]{0:T(128)S(1)} %copy-done.5), custom_call_target="tpu_custom_call" | custom-call | tf_op jit(solution)/shard_map/tree/pallas_call | solution.py:258
  36.4 0.6 slice.12
  37.6 0.6 fusion
  38.2 19.4 %all-to-all-done.1.weights_ref = bf16[32,40,256]{2,1,0:T(8,128)(2,1)S(1)} async-done(((bf16[32,40,256]{2,1,0:T(8,128)(2,1)}), bf16[32,40,256]{2,1,0:T(8,128)(2,1)S(1)}, u32[]{:S(2)}, u32[]{:S(2)}) %all-to-all-start.1) | async-done | bytes 655392 | tf_op jit(solution)/shard_map/all_to_all | solution.py:238
  57.6 0.0 copy-start
  57.6 2.2 %copy-done = bf16[256,8192]{1,0:T(8,128)(2,1)S(1)} copy-done((bf16[256,8192]{1,0:T(8,128)(2,1)S(1)}, bf16[256,8192]{1,0:T(8,128)(2,1)}, u32[]{:S(2)}) %copy-start) | copy-done | bytes 4194328
  59.8 2.6 %project_keys.1 = (bf16[16,40,256]{2,1,0:T(8,128)(2,1)S(1)}, f32[1,256]{1,0:T(1,128)S(1)}) custom-call(s32[1]{0:T(128)} %bitcast.3.quarter_ref, bf16[256,8192]{1,0:T(8,128)(2,1)S(1)} %copy-done, bf16[32,40,256]{2,1,0:T(8,128)(2,1)S(1)} %all-to-all-done.1.weights_ref, f32[128,256]{1,0:T(8,128)S(1)} %get-tuple-element.15.cosine_ref, ...), custom_call_target="tpu_custom_call" | custom-call | tf_op jit(solution)/shard_map/project_keys/pallas_call | solution.py:297
  62.4 18.7 %all_to_all.43 = bf16[16,40,256]{2,1,0:T(8,128)(2,1)S(1)} all-to-all(bf16[16,40,256]{2,1,0:T(8,128)(2,1)S(1)} %get-tuple-element.9), channel_id=1, replica_groups=mesh['y'=8,'zl'=2,'c'=2,'zh'=4,'x'=4] {'y','zl'}, dimensions={0} | all-to-all | bytes 655360 | tf_op jit(solution)/shard_map/all_to_all | solution.py:238
  81.1 0.1 broadcast_in_dim.26
  81.2 15.2 %all_to_all.44.near_ref = bf16[4,16,32,256]{3,2,1,0:T(8,128)(2,1)S(1)} all-to-all(bf16[4,16,32,256]{3,2,1,0:T(8,128)(2,1)S(1)} %broadcast_in_dim.26), channel_id=1, replica_groups=mesh['y'=8,'zl'=2,'c'=2,'zh'=4,'x'=4] {'x'}, dimensions={0} | all-to-all | bytes 2097152 | tf_op jit(solution)/shard_map/all_to_all | solution.py:238
  96.4 5.2 %collective-permute-start = (bf16[4,16,32,256]{3,2,1,0:T(8,128)(2,1)S(1)}, bf16[4,16,32,256]{3,2,1,0:T(8,128)(2,1)S(1)}, u32[]{:S(2)}, u32[]{:S(2)}) collective-permute-start(bf16[4,16,32,256]{3,2,1,0:T(8,128)(2,1)S(1)} %all_to_all.44.near_ref), channel_id=1, source_target_pairs={{0,16},{16,0},{1,17},{17,1},{2,18},{18,2},{3,19},{19,3},{4,20},{20... | collective-permute-start | bytes 3145736 | tf_op jit(solution)/shard_map/ppermute | solution.py:327
  101.6 0.1 pad_add_fusion.place_ref
  101.7 1.9 %collective-permute-start.1 = (bf16[16,8,256]{2,1,0:T(8,128)(2,1)S(1)}, bf16[16,8,256]{2,1,0:T(8,128)(2,1)S(1)}, u32[]{:S(2)}, u32[]{:S(2)}) collective-permute-start(bf16[16,8,256]{2,1,0:T(8,128)(2,1)S(1)} %slice.17.near_value_ref), channel_id=1, source_target_pairs={{0,16},{16,0},{1,17},{17,1},{2,18},{18,2},{3,19},{19,3},{4,20},{20... | collective-permute-start | bytes 196616 | tf_op jit(solution)/shard_map/ppermute | solution.py:323
  103.6 0.0 all-gather.2.cloned.1.call-done
  103.6 4.7 %fusion.4.query_ref = f32[256,256]{1,0:T(8,128)S(1)} fusion(bf16[256,8192]{1,0:T(8,128)(2,1)} %tokens_ref.1, bf16[8192,256]{1,0:T(8,128)(2,1)} %all-gather.2.cloned.1.call-done), kind=kOutput, calls=%fused_computation.16 | convolution fusion | flops 1073741824 | bytes 8650752 | tf_op jit(solution)/shard_map/dot_general | solution.py:329
  108.3 0.0 collective-permute-done.1.far_value_ref
  108.4 0.0 collective-permute-done.far_ref
  108.4 4.1 %attend.1 = f32[16,256]{1,0:T(8,128)S(1)} custom-call(s32[2]{0:T(128)S(1)} %pad_add_fusion.place_ref, s32[72]{0:T(128)S(1)} %get-tuple-element.8.meta_ref, f32[256,256]{1,0:T(8,128)S(1)} %fusion.4.query_ref, f32[128,256]{1,0:T(8,128)S(1)} %get-tuple-element.15.cosine_ref, f32[128,256]{1,0:T(8,128)S(1)} %get-tuple-element.14.sine_ref, ...), custom_call_target="tpu_custom_call" | custom-call | tf_op jit(solution)/shard_map/attend/pallas_call | solution.py:330
  112.5 18.6 %all_to_all.45 = f32[16,1,256]{2,1,0:T(1,128)S(1)} all-to-all(f32[16,1,256]{2,1,0:T(1,128)S(1)} %copy.11), channel_id=1, replica_groups=mesh['y'=8,'zl'=2,'c'=2,'zh'=4,'x'=4] {'zh','x'}, dimensions={0} | all-to-all | bytes 32768 | tf_op jit(solution)/shard_map/all_to_all | solution.py:238
  131.1 1.1 token_values.1
  132.2 15.6 %all_to_all.46 = f32[32,1,128]{2,1,0:T(1,128)S(1)} all-to-all(f32[32,1,128]{2,1,0:T(1,128)S(1)} %bitcast.22), channel_id=1, replica_groups=mesh['y'=8,'zl'=2,'c'=2,'zh'=4,'x'=4] {'y','zl','c'}, dimensions={0} | all-to-all | bytes 32768 | tf_op jit(solution)/shard_map/all_to_all | solution.py:238
  147.8 0.5 multiply_reduce_fusion
  (6 shorter events, 0.1 us)
Async XLA Ops:
  7.2 96.5 %all-gather.2.cloned.1.call-start = ((), (), s32[]{:S(2)}) async-start(), calls=%async_computation.6 | async-start | bytes 4325376 | tf_op jit(solution)/shard_map/all_gather | solution.py:256
  9.2 9.3 %all-to-all-start = ((bf16[4,32,256]{2,1,0:T(8,128)(2,1)}), bf16[4,32,256]{2,1,0:T(8,128)(2,1)S(1)}, u32[]{:S(2)}, u32[]{:S(2)}) async-start(bf16[4,32,256]{2,1,0:T(8,128)(2,1)} %broadcast_in_dim.14), calls=%async_computation | async-start | bytes 131072 | tf_op jit(solution)/shard_map/all_to_all | solution.py:238
  18.6 0.7 copy-start.1
  19.3 0.7 copy-start.2
  20.9 36.7 %all-to-all-start.1 = ((bf16[32,40,256]{2,1,0:T(8,128)(2,1)}), bf16[32,40,256]{2,1,0:T(8,128)(2,1)S(1)}, u32[]{:S(2)}, u32[]{:S(2)}) async-start(bf16[32,40,256]{2,1,0:T(8,128)(2,1)} %fold_weights.1), calls=%async_computation.1 | async-start | bytes 1310720 | tf_op jit(solution)/shard_map/all_to_all | solution.py:238
  32.1 0.7 copy-start.3
  32.8 0.7 copy-start.4
  33.4 0.7 copy-start.5
  57.6 2.2 %copy-start = (bf16[256,8192]{1,0:T(8,128)(2,1)S(1)}, bf16[256,8192]{1,0:T(8,128)(2,1)}, u32[]{:S(2)}) copy-start(bf16[256,8192]{1,0:T(8,128)(2,1)} %tokens_ref.1) | copy-start | bytes 12582916
  96.4 11.9 %collective-permute-start = (bf16[4,16,32,256]{3,2,1,0:T(8,128)(2,1)S(1)}, bf16[4,16,32,256]{3,2,1,0:T(8,128)(2,1)S(1)}, u32[]{:S(2)}, u32[]{:S(2)}) collective-permute-start(bf16[4,16,32,256]{3,2,1,0:T(8,128)(2,1)S(1)} %all_to_all.44.near_ref), channel_id=1, source_target_pairs={{0,16},{16,0},{1,17},{17,1},{2,18},{18,2},{3,19},{19,3},{4,20},{20... | collective-permute-start | bytes 3145736 | tf_op jit(solution)/shard_map/ppermute | solution.py:327
  101.7 6.7 %collective-permute-start.1 = (bf16[16,8,256]{2,1,0:T(8,128)(2,1)S(1)}, bf16[16,8,256]{2,1,0:T(8,128)(2,1)S(1)}, u32[]{:S(2)}, u32[]{:S(2)}) collective-permute-start(bf16[16,8,256]{2,1,0:T(8,128)(2,1)S(1)} %slice.17.near_value_ref), channel_id=1, source_target_pairs={{0,16},{16,0},{1,17},{17,1},{2,18},{18,2},{3,19},{19,3},{4,20},{20... | collective-permute-start | bytes 196616 | tf_op jit(solution)/shard_map/ppermute | solution.py:323
Sparse Core Ops, SparseCore 0:
  10.1 83.9 all-gather.1

commit v2 on v1

v2 whole, which is shorter than its diff:
```python
import jax
import jax.numpy as jnp
from jax import lax
from jax.experimental import pallas as pl
from jax.experimental.pallas import tpu as pltpu
from jax.sharding import Mesh
from jax.sharding import PartitionSpec as P

KEY_VALUE_HEADS = 4
HEAD_SIZE = 128
ROPE_BASE = 1000000.0
SEG = ("y", "zl", "c")
FSDP = ("zh", "x")
NEAR, FAR, LENGTHS, META = 8, 48, 80, 168
VMEM_LIMIT = 40 * 1024 * 1024

VMEM_SPEC = pl.BlockSpec(memory_space=pltpu.VMEM)
SMEM_SPEC = pl.BlockSpec(memory_space=pltpu.SMEM)
HBM_SPEC = pl.BlockSpec(memory_space=pltpu.HBM)


def tree_kernel(
    parents_src,
    placed_src,
    lengths_src,
    meta_ref,
    table_ref,
    position_ref,
    parents_ref,
    placed_ref,
    lengths_ref,
    slot_of,
    sems,
):
    copies = [
        pltpu.make_async_copy(source, there, sems.at[i])
        for i, (source, there) in enumerate(
            ((parents_src, parents_ref), (placed_src, placed_ref), (lengths_src, lengths_ref))
        )
    ]
    for copy in copies:
        copy.start()
    for copy in copies:
        copy.wait()
    segments = parents_ref.shape[0]
    slot = lax.axis_index(SEG)
    own = placed_ref[slot]

    def place(j, carry):
        slot_of[placed_ref[j]] = j
        return carry

    lax.fori_loop(0, segments, place, 0)

    def clear(j, carry):
        meta_ref[j] = 0
        return carry

    lax.fori_loop(0, META, clear, 0)

    def above(state):
        seg, near, far, offset = state
        there = slot_of[seg]
        is_near = (there % 2 == slot % 2).astype(jnp.int32)
        entry = jnp.where(is_near == 1, NEAR + near, FAR + far)
        meta_ref[entry] = there
        meta_ref[LENGTHS + entry] = lengths_ref[seg]
        return parents_ref[seg], near + is_near, far + 1 - is_near, offset + lengths_ref[seg]

    zero = jnp.int32(0)
    _, near, far, offset = lax.while_loop(
        lambda state: state[0] >= 0, above, (parents_ref[own], zero, zero, zero)
    )
    meta_ref[0] = near
    meta_ref[1] = far
    meta_ref[2] = lengths_ref[own]
    index = lax.broadcasted_iota(jnp.int32, position_ref.shape, 1)
    position_ref[...] = (offset + index).astype(jnp.float32)

    row = lax.broadcasted_iota(jnp.int32, (128, 128), 0)
    col = lax.broadcasted_iota(jnp.int32, (128, 128), 1)
    row_s = lax.broadcasted_iota(jnp.int32, (segments, 128), 0)
    col_s = lax.broadcasted_iota(jnp.int32, (segments, 128), 1)
    parent_of = jnp.full((segments, 128), -1, jnp.int32)
    held = jnp.full((segments, 128), -1, jnp.int32)
    for i in range(segments):
        parent_of = jnp.where(row_s == i, parents_ref[i], parent_of)
        held = jnp.where(row_s == i, placed_ref[i], held)
    step = jnp.where(parent_of == col_s, 1.0, 0.0)
    step = jnp.concatenate([step, jnp.zeros((128 - segments, 128), jnp.float32)], axis=0)
    ancestry = jnp.where(row == col, 1.0, 0.0) + step

    def times(a, b):
        return jnp.dot(
            a.astype(jnp.bfloat16), b.astype(jnp.bfloat16), preferred_element_type=jnp.float32
        )

    power = step
    reach = 1
    while 2 * reach <= segments:
        power = times(power, power)
        ancestry = ancestry + times(power, ancestry)
        reach *= 2
    children = jnp.sum(step, axis=0, keepdims=True)
    leafy = jnp.where((children < 0.5) & (col[:1] < segments), 1.0, 0.0)
    leaves = times(jnp.broadcast_to(leafy, (8, 128)), ancestry)[:1]
    placement = jnp.where(held == col_s, 1.0, 0.0)
    share = times(placement * leafy, ancestry)
    table_ref[...] = jnp.where(col_s < segments, share / jnp.maximum(leaves, 1.0), 0.0)


def weights_kernel(value_ref, readout_ref, key_ref, out_ref):
    quarters, part, rows = value_ref.shape
    value = value_ref[...].reshape(quarters * part, rows)
    readout = readout_ref[...].astype(jnp.bfloat16)
    folded = jnp.dot(readout, value, preferred_element_type=jnp.float32)
    heads = readout_ref.shape[0]
    high = folded.astype(jnp.bfloat16).astype(jnp.float32)
    low = folded - high
    pad = jnp.zeros((8 - 2 * heads, rows), jnp.float32)
    piece = jnp.concatenate([key_ref[...], high, low, pad], axis=0).astype(jnp.bfloat16)
    for i in range(out_ref.shape[0]):
        out_ref[i] = piece


def turned(raw, cosine, sine, axis):
    extent = raw.shape[axis]
    index = lax.broadcasted_iota(jnp.int32, raw.shape, axis)
    after = pltpu.roll(raw, extent - 1, axis)
    before = pltpu.roll(raw, 1, axis)
    return raw * cosine + jnp.where(index % 2 == 0, after, before) * sine


def half_projected(tokens_ref, weights_ref, total, parity):
    for even in range(2):

        @pl.when(parity == even)
        def _():
            blocks, _, depth = weights_ref.shape
            acc = total[...]
            for p in range(blocks):
                start = (2 * p + even) * depth
                acc += lax.dot_general(
                    weights_ref[p],
                    tokens_ref[:, start : start + depth],
                    (((1,), (1,)), ((), ())),
                    preferred_element_type=jnp.float32,
                )
            total[...] = acc


def near_keys_kernel(tokens_ref, weights_ref, out_ref):
    out_ref[...] = jnp.zeros_like(out_ref)
    half_projected(tokens_ref, weights_ref, out_ref, lax.axis_index("c"))


def far_keys_kernel(
    tokens_ref, weights_ref, near_ref, cosine_ref, sine_ref, out_ref, total
):
    total[...] = near_ref[...]
    half_projected(tokens_ref, weights_ref, total, 1 - lax.axis_index("c"))
    width = total.shape[0] - 8
    start = pl.multiple_of(lax.axis_index("x") * width, width)
    keys = turned(total[:width], cosine_ref[pl.ds(start, width)], sine_ref[pl.ds(start, width)], 0)
    last = total[width:]
    row = lax.broadcasted_iota(jnp.int32, last.shape, 0)
    summed = last + pltpu.roll(last, 6, 0)
    high = summed.astype(jnp.bfloat16).astype(jnp.float32)
    low = pltpu.roll(summed - high, 2, 0)
    tail = jnp.where(row < 2, high, jnp.where(row < 4, low, 0.0))
    piece = jnp.concatenate([keys, tail], axis=0).astype(jnp.bfloat16)
    for i in range(out_ref.shape[0]):
        out_ref[i] = piece


def queries_kernel(
    tokens_ref, weights_ref, readout_ref, cosine_ref, sine_ref, out_ref, resid_ref, total
):
    readout = jnp.broadcast_to(readout_ref[...], (8, readout_ref.shape[1]))
    resid_ref[...] = lax.dot_general(
        readout.astype(jnp.bfloat16),
        tokens_ref[...],
        (((1,), (1,)), ((), ())),
        preferred_element_type=jnp.float32,
    )[:1]
    blocks, depth, _ = weights_ref.shape
    seg_len = tokens_ref.shape[0]
    half = lax.axis_index("zl")
    for upper in range(2):

        @pl.when(half == upper)
        def _():
            acc = jnp.zeros_like(total)
            for i in range(blocks):
                block = i // 4 * 4 + (i % 2 ^ upper) * 2 + i // 2 % 2
                acc += jnp.dot(
                    tokens_ref[:, block * depth : (block + 1) * depth],
                    weights_ref[i],
                    preferred_element_type=jnp.float32,
                )
            total[...] = acc

    raw = total[...].T
    for h in range(raw.shape[0] // HEAD_SIZE):
        head = raw[h * HEAD_SIZE : (h + 1) * HEAD_SIZE]
        out_ref[:, h * seg_len : (h + 1) * seg_len] = turned(
            head, cosine_ref[...], sine_ref[...], 0
        ).astype(jnp.bfloat16)


def attention_kernel(meta_ref, query_ref, near_ref, far_ref, out_ref, top, bottom, summed):
    seg_len = near_ref.shape[3]
    columns = query_ref.shape[1]
    heads = columns // seg_len
    own = lax.axis_index(SEG)
    quarter = lax.axis_index("x")
    quarters = lax.axis_size("x")
    width = HEAD_SIZE // quarters
    scale = HEAD_SIZE ** (-0.5)
    key_at = lax.broadcasted_iota(jnp.int32, (seg_len, columns), 0)
    query_at = lax.broadcasted_iota(jnp.int32, (seg_len, columns), 1) % seg_len

    def scores(source, slot, seen):
        keys = source[pl.ds(slot // 2 % 2 * quarters, quarters), slot // 4, :width]
        raw = lax.dot_general(
            keys.reshape(HEAD_SIZE, seg_len),
            query_ref[...],
            (((0,), (0,)), ((), ())),
            preferred_element_type=jnp.float32,
        )
        return jnp.where(seen, raw * scale, -1e30)

    def mix(source, slot, weights):
        piece = source[slot // 2 % 2 * quarters + quarter, slot // 4].astype(jnp.float32)
        return jnp.dot(
            piece[width:].astype(jnp.bfloat16),
            weights.astype(jnp.bfloat16),
            preferred_element_type=jnp.float32,
        )

    masked = scores(near_ref, own, key_at <= query_at)
    peak = jnp.max(masked, axis=0, keepdims=True)
    weights = jnp.exp(masked - peak)
    top[...] = peak
    bottom[...] = jnp.sum(weights, axis=0, keepdims=True)
    summed[...] = mix(near_ref, own, weights)

    def visit_two(entry, source):
        slots = [meta_ref[entry + i] for i in range(2)]
        masked = [
            scores(source, slots[i], key_at < meta_ref[LENGTHS + entry + i]) for i in range(2)
        ]
        peak = jnp.max(jnp.maximum(masked[0], masked[1]), axis=0, keepdims=True)
        peak = jnp.maximum(top[...], peak)
        shrink = jnp.exp(top[...] - peak)
        weights = [jnp.exp(m - peak) for m in masked]
        top[...] = peak
        bottom[...] = bottom[...] * shrink + jnp.sum(
            weights[0] + weights[1], axis=0, keepdims=True
        )
        summed[...] = (
            summed[...] * shrink
            + mix(source, slots[0], weights[0])
            + mix(source, slots[1], weights[1])
        )

    def near_two(n, carry):
        visit_two(NEAR + 2 * n, near_ref)
        return carry

    def far_two(n, carry):
        visit_two(FAR + 2 * n, far_ref)
        return carry

    lax.fori_loop(0, (meta_ref[0] + 1) // 2, near_two, 0)
    lax.fori_loop(0, (meta_ref[1] + 1) // 2, far_two, 0)
    scaled = summed[...] / bottom[...]
    result = jnp.zeros((1, seg_len), jnp.float32)
    for h in range(heads):
        part = scaled[:, h * seg_len : (h + 1) * seg_len]
        result += part[h : h + 1] + part[2 + h : 3 + h]
    for i in range(out_ref.shape[0]):
        out_ref[i] = jnp.broadcast_to(result, out_ref.shape[1:])


def finish_kernel(meta_ref, parts_ref, resid_ref, out_ref, leaf_ref):
    total = resid_ref[...] + jnp.sum(parts_ref[...], axis=0)[:1]
    index = lax.broadcasted_iota(jnp.int32, total.shape, 1)
    length = meta_ref[2]
    values = jnp.where(index < length, total, 0.0)
    out_ref[...] = values
    leaf = jnp.sum(jnp.where(index == length - 1, values, 0.0), axis=1, keepdims=True)
    leaf_ref[...] = jnp.broadcast_to(leaf, leaf_ref.shape)


def gathered(value, axis):
    return lax.all_to_all(value, axis, 0, 0)


def on_device(
    tokens, w_query, key_weight, value_weight, resid_head, head_readout, parents, placed, lengths
):
    seg_len, model_width = tokens.shape
    segments = parents.shape[0]
    fsdp_size = lax.axis_size(FSDP)
    quarters = lax.axis_size("x")
    pairs = segments // 2
    width = key_weight.shape[1]
    rows = width + 8
    heads = w_query.shape[1] // HEAD_SIZE
    swap = [(0, 1), (1, 0)]
    params = pltpu.CompilerParams(vmem_limit_bytes=VMEM_LIMIT)

    other = lax.ppermute(w_query, "zl", swap)
    values_x = gathered(jnp.broadcast_to(value_weight.T[None], (quarters, width, seg_len)), "x")
    readout = head_readout.reshape(heads, HEAD_SIZE).astype(jnp.float32)
    key_rows = key_weight.T.astype(jnp.float32)
    values_x, other, readout, key_rows = lax.optimization_barrier(
        (values_x, other, readout, key_rows)
    )
    query_weight = lax.all_gather(
        jnp.concatenate([w_query, other]), ("y", "c"), axis=0, tiled=True
    )
    pieces = pl.pallas_call(
        weights_kernel,
        out_shape=jax.ShapeDtypeStruct((pairs, rows, seg_len), jnp.bfloat16),
        in_specs=[VMEM_SPEC] * 3,
        out_specs=VMEM_SPEC,
        compiler_params=params,
        name="fold_weights",
    )(values_x, readout, key_rows)

    near_weights = gathered(pieces, ("y", "zl"))
    meta, table, positions = pl.pallas_call(
        tree_kernel,
        out_shape=(
            jax.ShapeDtypeStruct((META,), jnp.int32),
            jax.ShapeDtypeStruct((segments, 128), jnp.float32),
            jax.ShapeDtypeStruct((1, seg_len), jnp.float32),
        ),
        in_specs=[HBM_SPEC] * 3,
        out_specs=(SMEM_SPEC, VMEM_SPEC, VMEM_SPEC),
        scratch_shapes=[pltpu.SMEM((segments,), jnp.int32)] * 4
        + [pltpu.SemaphoreType.DMA((3,))],
        compiler_params=params,
        name="tree",
    )(parents, placed, lengths)
    dims = jnp.arange(HEAD_SIZE, dtype=jnp.int32)
    frequency = ROPE_BASE ** (-2.0 * (dims // 2).astype(jnp.float32) / HEAD_SIZE)
    angles = frequency[:, None] * positions
    cosine = jnp.cos(angles)
    sine = jnp.sin(angles) * jnp.where(dims % 2 == 0, -1.0, 1.0)[:, None]
    readout_row = resid_head.reshape(1, model_width).astype(jnp.float32)
    near_weights, cosine, sine, readout_row = lax.optimization_barrier(
        (near_weights, cosine, sine, readout_row)
    )

    far_weights = lax.ppermute(near_weights, "c", swap)
    near_sums = pl.pallas_call(
        near_keys_kernel,
        out_shape=jax.ShapeDtypeStruct((rows, seg_len), jnp.float32),
        in_specs=[VMEM_SPEC] * 2,
        out_specs=VMEM_SPEC,
        compiler_params=params,
        cost_estimate=pl.CostEstimate(
            flops=rows * seg_len * model_width, bytes_accessed=2**21, transcendentals=0
        ),
        name="project_near_keys",
    )(tokens, near_weights)
    far_weights, near_sums = lax.optimization_barrier((far_weights, near_sums))
    keys = pl.pallas_call(
        far_keys_kernel,
        out_shape=jax.ShapeDtypeStruct((lax.axis_size("y"), rows, seg_len), jnp.bfloat16),
        in_specs=[VMEM_SPEC] * 5,
        out_specs=VMEM_SPEC,
        scratch_shapes=[pltpu.VMEM((rows, seg_len), jnp.float32)],
        compiler_params=params,
        name="project_far_keys",
    )(tokens, far_weights, near_sums, cosine, sine)

    keys_y = gathered(keys, "y")
    spread = lax.axis_size(("zl", "x"))
    near = gathered(jnp.broadcast_to(keys_y[None], (spread, *keys_y.shape)), ("zl", "x"))
    queries, residual = pl.pallas_call(
        queries_kernel,
        out_shape=(
            jax.ShapeDtypeStruct((HEAD_SIZE, heads * seg_len), jnp.bfloat16),
            jax.ShapeDtypeStruct((1, seg_len), jnp.float32),
        ),
        in_specs=[VMEM_SPEC] * 5,
        out_specs=(VMEM_SPEC, VMEM_SPEC),
        scratch_shapes=[pltpu.VMEM((seg_len, heads * HEAD_SIZE), jnp.float32)],
        cost_estimate=pl.CostEstimate(
            flops=2 * seg_len * model_width * heads * HEAD_SIZE,
            bytes_accessed=2 * model_width * (seg_len + heads * HEAD_SIZE),
            transcendentals=0,
        ),
        compiler_params=params,
        name="project_queries",
    )(
        tokens,
        query_weight.reshape(segments, seg_len, -1),
        readout_row,
        cosine,
        sine,
    )
    near, queries = lax.optimization_barrier((near, queries))
    far = lax.ppermute(near, "c", swap)
    mixed = pl.pallas_call(
        attention_kernel,
        out_shape=jax.ShapeDtypeStruct((fsdp_size, 8, seg_len), jnp.float32),
        in_specs=[SMEM_SPEC] + [VMEM_SPEC] * 3,
        out_specs=VMEM_SPEC,
        scratch_shapes=[
            pltpu.VMEM((1, heads * seg_len), jnp.float32),
            pltpu.VMEM((1, heads * seg_len), jnp.float32),
            pltpu.VMEM((8, heads * seg_len), jnp.float32),
        ],
        compiler_params=params,
        name="attend",
    )(meta, queries, near, far)
    parts = gathered(mixed, FSDP)
    token_values, leaf_rows = pl.pallas_call(
        finish_kernel,
        out_shape=(
            jax.ShapeDtypeStruct((1, seg_len), jnp.float32),
            jax.ShapeDtypeStruct((segments, 128), jnp.float32),
        ),
        in_specs=[SMEM_SPEC, VMEM_SPEC, VMEM_SPEC],
        out_specs=(VMEM_SPEC, VMEM_SPEC),
        compiler_params=params,
        name="token_values",
    )(meta, parts, residual)
    leaves = gathered(leaf_rows, SEG)
    branch = jnp.sum(leaves * table, axis=0)[:segments]
    return (token_values.reshape(seg_len), branch)


def solution(mesh):
    fine = Mesh(mesh.devices.reshape(8, 2, 2, 4, 4), SEG + FSDP)
    in_specs = (
        P(SEG, None),
        P(SEG, FSDP),
        P(SEG, FSDP),
        P(SEG, FSDP),
        P(),
        P(FSDP),
        P(),
        P(),
        P(),
    )
    out_specs = (P(SEG), P())
    return jax.shard_map(
        on_device, mesh=fine, in_specs=in_specs, out_specs=out_specs, check_vma=False
    )
```

time: 156 us -> 138 us (0.88)
  blocking collectives: 68 us -> 47.2 us
  starting transfers between devices: 23.1 us -> 29.6 us
  matrix products: 4.71 us -> 0 us
  other arithmetic: 1.18 us -> 4.1 us
  waiting for transfers between devices: 23.8 us -> 21.8 us
    all_to_all x4 -> x3, blocking collectives: 68 us -> 47.2 us  [gathered(): return lax.all_to_all(value, axis, 0, 0)]
    all_to_all x2 -> x3, waiting for transfers between devices: 23.1 us -> 12.6 us  [gathered(): return lax.all_to_all(value, axis, 0, 0)]
    ppermute x1 -> x2, starting transfers between devices: 1.91 us -> 9.55 us  [the longest x1 5.56 us: on_device(): far_weights = lax.ppermute(near_weights, 'c', swap)]
    all_gather x1, waiting for transfers between devices: 0.02 us -> 5.29 us  [on_device(): lax.all_gather(jnp.concatenate([w_query, other]), ('y', 'c'), axis=0, til...]
    dot_general x1 -> x0, matrix products: 4.71 us -> none  [on_device(): jnp.dot(tokens, query_weight, preferred_element_type=jnp.float32)]
    ppermute x1, waiting for transfers between devices: 0.01 us -> 2.64 us  [on_device(): far = lax.ppermute(near, 'c', swap)]
    ppermute x1, starting transfers between devices: 5.17 us -> 2.71 us  [on_device(): far = lax.ppermute(near, 'c', swap)]
    pallas_call x1, Pallas kernels: 4.12 us -> 2.38 us  [on_device(): pl.pallas_call(attention_kernel, out_shape=jax.ShapeDtypeStruct((fsdp_siz...]
  transfers between devices with their start and end apart: 5 -> 7, of which waited for: 2 -> 5; matrix products, arithmetic and copies ran while one was open for 5% -> 2% of each run, Pallas kernels for 4% -> 6%
where the time goes in v2:
time: 138 us
  blocking collectives  47.2 us (34%)
  starting transfers between devices  29.6 us (21%)
  waiting for transfers between devices  21.8 us (16%)
  between operations  14.2 us (10%)
  Pallas kernels  11.4 us (8%)
  local copies, waits for them, and re-layouts  9.22 us (7%)
  other arithmetic  4.1 us (3%)
    all_to_all x3, blocking collectives, gathered(): return lax.all_to_all(value, axis, 0, 0)  47.2 us
    all_to_all x3, starting transfers between devices, gathered(): return lax.all_to_all(value, axis, 0, 0)  17.3 us
    all_to_all x3, waiting for transfers between devices, gathered(): return lax.all_to_all(value, axis, 0, 0)  12.6 us
    unnamed x14, local copies, waits for them, and re-layouts  6.66 us
    ppermute x1, starting transfers between devices, on_device(): far_weights = lax.ppermute(near_weights, 'c', swap)  5.56 us
    all_gather x1, waiting for transfers between devices, on_device(): lax.all_gather(jnp.concatenate([w_query, other]), ('y', 'c'), axis=0, til...  5.29 us
    ppermute x1, starting transfers between devices, on_device(): other = lax.ppermute(w_query, 'zl', swap)  3.99 us
    pallas_call x1, Pallas kernels, on_device(): pl.pallas_call(tree_kernel, out_shape=(jax.ShapeDtypeStruct((META,), jnp....  2.94 us
  transfers between devices with their start and end apart: 7, of which 5 were waited for; matrix products, arithmetic and copies ran while one was open for 2% of the time, Pallas kernels for 6%

profile of v2, /device:TPU:1, one launch (start us, length us, event | category | flops | bytes accessed | tf_op | source)
XLA Modules:
  0.0 137.5 jit_solution(15390548498552919559)
XLA Ops:
  7.2 0.0 copy-start.6
  7.2 0.0 copy-start.5
  7.2 0.0 copy-start.4
  7.2 0.0 copy-start.3
  7.2 1.4 broadcast_in_dim.12
  8.6 4.8 %all-to-all-start = ((bf16[4,32,256]{2,1,0:T(8,128)(2,1)}), bf16[4,32,256]{2,1,0:T(8,128)(2,1)S(1)}, u32[]{:S(2)}, u32[]{:S(2)}) async-start(bf16[4,32,256]{2,1,0:T(8,128)(2,1)} %broadcast_in_dim.12), calls=%async_computation | async-start | bytes 131072 | tf_op jit(solution)/shard_map/all_to_all | solution.py:297
  13.4 0.0 all-gather.2.cloned.1.call-start
  13.4 4.0 %collective-permute-start = (bf16[256,256]{1,0:T(8,128)(2,1)}, bf16[256,256]{1,0:T(8,128)(2,1)S(1)}, u32[]{:S(2)}, u32[]{:S(2)}) collective-permute-start(bf16[256,256]{1,0:T(8,128)(2,1)} %param.10), channel_id=1, source_target_pairs={{0,32},{32,0},{1,33},{33,1},{2,34},{34,2},{3,35},{35,3},{4,36},{36... | collective-permute-start | bytes 393224 | tf_op jit(solution)/shard_map/ppermute | solution.py:314
  17.4 0.7 convert_bitcast_fusion.key_ref
  18.1 0.7 bitcast_convert_fusion.readout_ref
  18.8 0.0 all-to-all-done.value_ref
  18.8 1.2 collective-permute-done
  20.0 1.6 %pad_maximum_fusion = bf16[512,256]{1,0:T(8,128)(2,1)} fusion(bf16[256,256]{1,0:T(8,128)(2,1)S(1)} %collective-permute-done, bf16[256,256]{1,0:T(8,128)(2,1)} %param.10), kind=kLoop, calls=%fused_computation | loop fusion | flops 524288 | bytes 524288 | tf_op jit(solution)/shard_map/concatenate | solution.py:322
  21.6 0.0 all-gather.2.cloned.1.call-update
  21.6 0.9 fold_weights.1
  22.5 8.4 %all-to-all-start.1 = ((bf16[16,40,256]{2,1,0:T(8,128)(2,1)}), bf16[16,40,256]{2,1,0:T(8,128)(2,1)S(1)}, u32[]{:S(2)}, u32[]{:S(2)}) async-start(bf16[16,40,256]{2,1,0:T(8,128)(2,1)} %fold_weights.1), calls=%async_computation.1 | async-start | bytes 655360 | tf_op jit(solution)/shard_map/all_to_all | solution.py:297
  30.9 0.0 copy-done.6
  30.9 0.0 copy-done.5
  30.9 0.0 copy-done.4
  30.9 0.0 copy-done.3
  30.9 2.9 %tree.1 = (s32[168]{0:T(256)S(1)}, f32[32,128]{1,0:T(8,128)S(1)}, f32[1,256]{1,0:T(1,128)S(1)}) custom-call(s32[32]{0:T(128)S(1)} %copy-done.3, s32[32]{0:T(128)S(1)} %copy-done.4, s32[32]{0:T(128)S(1)} %copy-done.5), custom_call_target="tpu_custom_call" | custom-call | tf_op jit(solution)/shard_map/tree/pallas_call | solution.py:334
  33.9 0.6 fusion
  34.4 7.1 %all-to-all-done.1.weights_ref = bf16[16,40,256]{2,1,0:T(8,128)(2,1)S(1)} async-done(((bf16[16,40,256]{2,1,0:T(8,128)(2,1)}), bf16[16,40,256]{2,1,0:T(8,128)(2,1)S(1)}, u32[]{:S(2)}, u32[]{:S(2)}) %all-to-all-start.1) | async-done | bytes 327712 | tf_op jit(solution)/shard_map/all_to_all | solution.py:297
  41.6 5.6 %collective-permute-start.1 = (bf16[16,40,256]{2,1,0:T(8,128)(2,1)S(1)}, bf16[16,40,256]{2,1,0:T(8,128)(2,1)S(1)}, u32[]{:S(2)}, u32[]{:S(2)}) collective-permute-start(bf16[16,40,256]{2,1,0:T(8,128)(2,1)S(1)} %all-to-all-done.1.weights_ref), channel_id=1, source_target_pairs={{0,16},{16,0},{1,17},{17,1},{2,18},{18,2},{3,19},{19,3},{4,20},{20... | collective-permute-start | bytes 983048 | tf_op jit(solution)/shard_map/ppermute | solution.py:358
  47.2 0.0 copy-start
  47.2 2.3 %copy-done = bf16[256,8192]{1,0:T(8,128)(2,1)S(1)} copy-done((bf16[256,8192]{1,0:T(8,128)(2,1)S(1)}, bf16[256,8192]{1,0:T(8,128)(2,1)}, u32[]{:S(2)}) %copy-start) | copy-done | bytes 4194328
  49.4 0.7 project_near_keys.1.near_ref
  50.2 0.0 collective-permute-done.1.weights_ref
  50.2 0.8 project_far_keys.1
  51.0 14.0 %all_to_all.37 = bf16[8,40,256]{2,1,0:T(8,128)(2,1)S(1)} all-to-all(bf16[8,40,256]{2,1,0:T(8,128)(2,1)S(1)} %project_far_keys.1), channel_id=1, replica_groups=mesh['y'=8,'zl'=2,'c'=2,'zh'=4,'x'=4] {'y'}, dimensions={0} | all-to-all | bytes 327680 | tf_op jit(solution)/shard_map/all_to_all | solution.py:297
  65.0 1.2 broadcast_in_dim.25
  66.2 4.1 %all-to-all-start.3 = ((bf16[8,8,40,256]{3,2,1,0:T(8,128)(2,1)}), bf16[8,8,40,256]{3,2,1,0:T(8,128)(2,1)S(1)}, u32[]{:S(2)}, u32[]{:S(2)}) async-start(bf16[8,8,40,256]{3,2,1,0:T(8,128)(2,1)} %broadcast_in_dim.25), calls=%async_computation.3 | async-start | bytes 2621440 | tf_op jit(solution)/shard_map/all_to_all | solution.py:297
  70.3 5.3 %all-gather.2.cloned.1.call-done = bf16[8192,256]{1,0:T(8,128)(2,1)} async-done(((bf16[512,256]{1,0:T(8,128)(2,1)}), bf16[8192,256]{1,0:T(8,128)(2,1)}) %all-gather.2.cloned.1.call-update) | async-done | bytes 4194320 | tf_op jit(solution)/shard_map/all_gather | solution.py:321
  75.6 0.0 copy-start.1
  75.6 2.2 %copy-done.1 = bf16[256,8192]{1,0:T(8,128)(2,1)S(1)} copy-done((bf16[256,8192]{1,0:T(8,128)(2,1)S(1)}, bf16[256,8192]{1,0:T(8,128)(2,1)}, u32[]{:S(2)}) %copy-start.1) | copy-done | bytes 4194328
  77.8 0.0 copy-start.2
  77.8 2.2 %copy-done.2 = bf16[8192,256]{1,0:T(8,128)(2,1)S(1)} copy-done((bf16[8192,256]{1,0:T(8,128)(2,1)S(1)}, bf16[8192,256]{1,0:T(8,128)(2,1)}, u32[]{:S(2)}) %copy-start.2) | copy-done | bytes 4194328
  80.0 2.6 %project_queries.1 = (bf16[128,512]{1,0:T(8,128)(2,1)S(1)}, f32[1,256]{1,0:T(1,128)S(1)}) custom-call(bf16[256,8192]{1,0:T(8,128)(2,1)S(1)} %copy-done.1, bf16[32,256,256]{2,1,0:T(8,128)(2,1)S(1)} %bitcast.15, f32[1,8192]{1,0:T(1,128)S(1)} %bitcast.16, f32[128,256]{1,0:T(8,128)S(1)} %get-tuple-element.29.cosine_ref, f32[128,256]{1,0:T(8,128)S(1)} %get-tuple-element.30.sine_ref), custom_call_target="tpu_custom_call" | custom-call | flops 1073741824 | bytes 8388608 | tf_op jit(solution)/shard_map/project_queries/pallas_call | solution.py:384
  82.6 5.5 %all-to-all-done.3.near_ref = bf16[8,8,40,256]{3,2,1,0:T(8,128)(2,1)S(1)} async-done(((bf16[8,8,40,256]{3,2,1,0:T(8,128)(2,1)}), bf16[8,8,40,256]{3,2,1,0:T(8,128)(2,1)S(1)}, u32[]{:S(2)}, u32[]{:S(2)}) %all-to-all-start.3) | async-done | bytes 1310752 | tf_op jit(solution)/shard_map/all_to_all | solution.py:297
  88.1 2.7 %collective-permute-start.2 = (bf16[8,8,40,256]{3,2,1,0:T(8,128)(2,1)S(1)}, bf16[8,8,40,256]{3,2,1,0:T(8,128)(2,1)S(1)}, u32[]{:S(2)}, u32[]{:S(2)}) collective-permute-start(bf16[8,8,40,256]{3,2,1,0:T(8,128)(2,1)S(1)} %all-to-all-done.3.near_ref), channel_id=1, source_target_pairs={{0,16},{16,0},{1,17},{17,1},{2,18},{18,2},{3,19},{19,3},{4,20},{20... | collective-permute-start | bytes 3932168 | tf_op jit(solution)/shard_map/ppermute | solution.py:408
  90.8 2.6 %collective-permute-done.2.far_ref = bf16[8,8,40,256]{3,2,1,0:T(8,128)(2,1)S(1)} collective-permute-done((bf16[8,8,40,256]{3,2,1,0:T(8,128)(2,1)S(1)}, bf16[8,8,40,256]{3,2,1,0:T(8,128)(2,1)S(1)}, u32[]{:S(2)}, u32[]{:S(2)}) %collective-permute-start.2) | collective-permute-done | bytes 1310752 | tf_op jit(solution)/shard_map/ppermute | solution.py:408
  93.4 2.4 %attend.1 = f32[16,8,256]{2,1,0:T(8,128)S(1)} custom-call(s32[168]{0:T(256)S(1)} %get-tuple-element.21.meta_ref, bf16[128,512]{1,0:T(8,128)(2,1)S(1)} %get-tuple-element.34.query_ref, bf16[8,8,40,256]{3,2,1,0:T(8,128)(2,1)S(1)} %all-to-all-done.3.near_ref, bf16[8,8,40,256]{3,2,1,0:T(8,128)(2,1)S(1)} %collective-permute-done.2.far_ref), custom_call_target="tpu_custom_call" | custom-call | tf_op jit(solution)/shard_map/attend/pallas_call | solution.py:409
  95.8 20.1 %all_to_all.38.parts_ref = f32[16,8,256]{2,1,0:T(8,128)S(1)} all-to-all(f32[16,8,256]{2,1,0:T(8,128)S(1)} %attend.1), channel_id=1, replica_groups=mesh['y'=8,'zl'=2,'c'=2,'zh'=4,'x'=4] {'zh','x'}, dimensions={0} | all-to-all | bytes 262144 | tf_op jit(solution)/shard_map/all_to_all | solution.py:297
  116.0 1.1 token_values.1
  117.1 13.0 %all_to_all.39 = f32[32,1,128]{2,1,0:T(1,128)S(1)} all-to-all(f32[32,1,128]{2,1,0:T(1,128)S(1)} %bitcast.17), channel_id=1, replica_groups=mesh['y'=8,'zl'=2,'c'=2,'zh'=4,'x'=4] {'y','zl','c'}, dimensions={0} | all-to-all | bytes 32768 | tf_op jit(solution)/shard_map/all_to_all | solution.py:297
  130.2 0.5 multiply_reduce_fusion
  (2 shorter events, 0.0 us)
Async XLA Ops:
  7.2 23.7 %copy-start.6 = (bf16[8192]{0:T(1024)(128)(2,1)S(1)}, bf16[8192]{0:T(1024)(128)(2,1)}, u32[]{:S(2)}) copy-start(bf16[8192]{0:T(1024)(128)(2,1)} %param.13) | copy-start | bytes 49156
  7.2 23.7 %copy-start.5 = (s32[32]{0:T(128)S(1)}, s32[32]{0:T(128)}, u32[]{:S(2)}) copy-start(s32[32]{0:T(128)} %lengths_src.1) | copy-start | bytes 388
  7.2 23.7 %copy-start.4 = (s32[32]{0:T(128)S(1)}, s32[32]{0:T(128)}, u32[]{:S(2)}) copy-start(s32[32]{0:T(128)} %placed_src.1) | copy-start | bytes 388
  7.2 23.7 %copy-start.3 = (s32[32]{0:T(128)S(1)}, s32[32]{0:T(128)}, u32[]{:S(2)}) copy-start(s32[32]{0:T(128)} %parents_src.1) | copy-start | bytes 388
  8.6 10.2 %all-to-all-start = ((bf16[4,32,256]{2,1,0:T(8,128)(2,1)}), bf16[4,32,256]{2,1,0:T(8,128)(2,1)S(1)}, u32[]{:S(2)}, u32[]{:S(2)}) async-start(bf16[4,32,256]{2,1,0:T(8,128)(2,1)} %broadcast_in_dim.12), calls=%async_computation | async-start | bytes 131072 | tf_op jit(solution)/shard_map/all_to_all | solution.py:297
  13.4 62.2 %all-gather.2.cloned.1.call-start = ((), (), s32[]{:S(2)}) async-start(), calls=%async_computation.6 | async-start | bytes 4456448 | tf_op jit(solution)/shard_map/all_gather | solution.py:321
  13.4 6.6 %collective-permute-start = (bf16[256,256]{1,0:T(8,128)(2,1)}, bf16[256,256]{1,0:T(8,128)(2,1)S(1)}, u32[]{:S(2)}, u32[]{:S(2)}) collective-permute-start(bf16[256,256]{1,0:T(8,128)(2,1)} %param.10), channel_id=1, source_target_pairs={{0,32},{32,0},{1,33},{33,1},{2,34},{34,2},{3,35},{35,3},{4,36},{36... | collective-permute-start | bytes 393224 | tf_op jit(solution)/shard_map/ppermute | solution.py:314
  22.5 19.1 %all-to-all-start.1 = ((bf16[16,40,256]{2,1,0:T(8,128)(2,1)}), bf16[16,40,256]{2,1,0:T(8,128)(2,1)S(1)}, u32[]{:S(2)}, u32[]{:S(2)}) async-start(bf16[16,40,256]{2,1,0:T(8,128)(2,1)} %fold_weights.1), calls=%async_computation.1 | async-start | bytes 655360 | tf_op jit(solution)/shard_map/all_to_all | solution.py:297
  41.6 8.6 %collective-permute-start.1 = (bf16[16,40,256]{2,1,0:T(8,128)(2,1)S(1)}, bf16[16,40,256]{2,1,0:T(8,128)(2,1)S(1)}, u32[]{:S(2)}, u32[]{:S(2)}) collective-permute-start(bf16[16,40,256]{2,1,0:T(8,128)(2,1)S(1)} %all-to-all-done.1.weights_ref), channel_id=1, source_target_pairs={{0,16},{16,0},{1,17},{17,1},{2,18},{18,2},{3,19},{19,3},{4,20},{20... | collective-permute-start | bytes 983048 | tf_op jit(solution)/shard_map/ppermute | solution.py:358
  47.2 2.3 %copy-start = (bf16[256,8192]{1,0:T(8,128)(2,1)S(1)}, bf16[256,8192]{1,0:T(8,128)(2,1)}, u32[]{:S(2)}) copy-start(bf16[256,8192]{1,0:T(8,128)(2,1)} %tokens_ref.5) | copy-start | bytes 12582916
  66.2 21.9 %all-to-all-start.3 = ((bf16[8,8,40,256]{3,2,1,0:T(8,128)(2,1)}), bf16[8,8,40,256]{3,2,1,0:T(8,128)(2,1)S(1)}, u32[]{:S(2)}, u32[]{:S(2)}) async-start(bf16[8,8,40,256]{3,2,1,0:T(8,128)(2,1)} %broadcast_in_dim.25), calls=%async_computation.3 | async-start | bytes 2621440 | tf_op jit(solution)/shard_map/all_to_all | solution.py:297
  75.6 2.2 %copy-start.1 = (bf16[256,8192]{1,0:T(8,128)(2,1)S(1)}, bf16[256,8192]{1,0:T(8,128)(2,1)}, u32[]{:S(2)}) copy-start(bf16[256,8192]{1,0:T(8,128)(2,1)} %tokens_ref.5) | copy-start | bytes 12582916
  77.8 2.2 %copy-start.2 = (bf16[8192,256]{1,0:T(8,128)(2,1)S(1)}, bf16[8192,256]{1,0:T(8,128)(2,1)}, u32[]{:S(2)}) copy-start(bf16[8192,256]{1,0:T(8,128)(2,1)} %all-gather.2.cloned.1.call-done) | copy-start | bytes 12582916
  88.1 5.4 %collective-permute-start.2 = (bf16[8,8,40,256]{3,2,1,0:T(8,128)(2,1)S(1)}, bf16[8,8,40,256]{3,2,1,0:T(8,128)(2,1)S(1)}, u32[]{:S(2)}, u32[]{:S(2)}) collective-permute-start(bf16[8,8,40,256]{3,2,1,0:T(8,128)(2,1)S(1)} %all-to-all-done.3.near_ref), channel_id=1, source_target_pairs={{0,16},{16,0},{1,17},{17,1},{2,18},{18,2},{3,19},{19,3},{4,20},{20... | collective-permute-start | bytes 3932168 | tf_op jit(solution)/shard_map/ppermute | solution.py:408
Sparse Core Ops, SparseCore 0:
  21.7 53.8 all-gather.1

commit v3 on v2

--- a/solution.py
+++ b/solution.py
@@ -114,11 +114,11 @@
     value = value_ref[...].reshape(quarters * part, rows)
     readout = readout_ref[...].astype(jnp.bfloat16)
     folded = jnp.dot(readout, value, preferred_element_type=jnp.float32)
-    heads = readout_ref.shape[0]
     high = folded.astype(jnp.bfloat16).astype(jnp.float32)
     low = folded - high
-    pad = jnp.zeros((8 - 2 * heads, rows), jnp.float32)
-    piece = jnp.concatenate([key_ref[...], high, low, pad], axis=0).astype(jnp.bfloat16)
+    width = key_ref.shape[0] - 8
+    piece = jnp.concatenate([key_ref[:width], high, low, key_ref[width + 4 :]], axis=0)
+    piece = piece.astype(jnp.bfloat16)
     for i in range(out_ref.shape[0]):
         out_ref[i] = piece
 
@@ -155,7 +155,7 @@
 
 
 def far_keys_kernel(
-    tokens_ref, weights_ref, near_ref, cosine_ref, sine_ref, out_ref, total
+    tokens_ref, weights_ref, near_ref, cosine_ref, sine_ref, out_ref, resid_ref, total
 ):
     total[...] = near_ref[...]
     half_projected(tokens_ref, weights_ref, total, 1 - lax.axis_index("c"))
@@ -168,21 +168,13 @@
     high = summed.astype(jnp.bfloat16).astype(jnp.float32)
     low = pltpu.roll(summed - high, 2, 0)
     tail = jnp.where(row < 2, high, jnp.where(row < 4, low, 0.0))
+    resid_ref[...] = last[4:5]
     piece = jnp.concatenate([keys, tail], axis=0).astype(jnp.bfloat16)
     for i in range(out_ref.shape[0]):
         out_ref[i] = piece
 
 
-def queries_kernel(
-    tokens_ref, weights_ref, readout_ref, cosine_ref, sine_ref, out_ref, resid_ref, total
-):
-    readout = jnp.broadcast_to(readout_ref[...], (8, readout_ref.shape[1]))
-    resid_ref[...] = lax.dot_general(
-        readout.astype(jnp.bfloat16),
-        tokens_ref[...],
-        (((1,), (1,)), ((), ())),
-        preferred_element_type=jnp.float32,
-    )[:1]
+def queries_kernel(tokens_ref, weights_ref, cosine_ref, sine_ref, out_ref, total):
     blocks, depth, _ = weights_ref.shape
     seg_len = tokens_ref.shape[0]
     half = lax.axis_index("zl")
@@ -208,47 +200,39 @@
         ).astype(jnp.bfloat16)
 
 
-def attention_kernel(meta_ref, query_ref, near_ref, far_ref, out_ref, top, bottom, summed):
-    seg_len = near_ref.shape[3]
-    columns = query_ref.shape[1]
-    heads = columns // seg_len
-    own = lax.axis_index(SEG)
-    quarter = lax.axis_index("x")
+def scored(query_ref, keys_ref, slot, seen):
     quarters = lax.axis_size("x")
-    width = HEAD_SIZE // quarters
-    scale = HEAD_SIZE ** (-0.5)
-    key_at = lax.broadcasted_iota(jnp.int32, (seg_len, columns), 0)
-    query_at = lax.broadcasted_iota(jnp.int32, (seg_len, columns), 1) % seg_len
-
-    def scores(source, slot, seen):
-        keys = source[pl.ds(slot // 2 % 2 * quarters, quarters), slot // 4, :width]
-        raw = lax.dot_general(
-            keys.reshape(HEAD_SIZE, seg_len),
-            query_ref[...],
-            (((0,), (0,)), ((), ())),
-            preferred_element_type=jnp.float32,
-        )
-        return jnp.where(seen, raw * scale, -1e30)
-
-    def mix(source, slot, weights):
-        piece = source[slot // 2 % 2 * quarters + quarter, slot // 4].astype(jnp.float32)
-        return jnp.dot(
-            piece[width:].astype(jnp.bfloat16),
-            weights.astype(jnp.bfloat16),
-            preferred_element_type=jnp.float32,
-        )
-
-    masked = scores(near_ref, own, key_at <= query_at)
-    peak = jnp.max(masked, axis=0, keepdims=True)
-    weights = jnp.exp(masked - peak)
-    top[...] = peak
-    bottom[...] = jnp.sum(weights, axis=0, keepdims=True)
-    summed[...] = mix(near_ref, own, weights)
-
-    def visit_two(entry, source):
-        slots = [meta_ref[entry + i] for i in range(2)]
+    seg_len = keys_ref.shape[3]
+    keys = keys_ref[pl.ds(slot // 2 % 2 * quarters, quarters), slot // 4]
+    raw = lax.dot_general(
+        keys.reshape(HEAD_SIZE, seg_len),
+        query_ref[...],
+        (((0,), (0,)), ((), ())),
+        preferred_element_type=jnp.float32,
+    )
+    return jnp.where(seen, raw * HEAD_SIZE ** (-0.5), -1e30)
+
+
+def mixed_values(own_ref, other_ref, far, slot, weights):
+    is_other = slot // 2 % 2 != lax.axis_index("zl")
+    own, other = (ref[far, slot // 4].astype(jnp.float32) for ref in (own_ref, other_ref))
+    return jnp.dot(
+        jnp.where(is_other, other, own).astype(jnp.bfloat16),
+        weights.astype(jnp.bfloat16),
+        preferred_element_type=jnp.float32,
+    )
+
+
+def visit(meta_ref, far, query_ref, keys_ref, own_ref, other_ref, top, bottom, summed):
+    key_at = lax.broadcasted_iota(jnp.int32, (keys_ref.shape[3], query_ref.shape[1]), 0)
+    first = (NEAR, FAR)[far]
+
+    def two(n, carry):
+        entries = [first + 2 * n, first + 2 * n + 1]
+        slots = [meta_ref[e] for e in entries]
         masked = [
-            scores(source, slots[i], key_at < meta_ref[LENGTHS + entry + i]) for i in range(2)
+            scored(query_ref, keys_ref, slot, key_at < meta_ref[LENGTHS + e])
+            for e, slot in zip(entries, slots)
         ]
         peak = jnp.max(jnp.maximum(masked[0], masked[1]), axis=0, keepdims=True)
         peak = jnp.maximum(top[...], peak)
@@ -260,23 +244,51 @@
         )
         summed[...] = (
             summed[...] * shrink
-            + mix(source, slots[0], weights[0])
-            + mix(source, slots[1], weights[1])
+            + mixed_values(own_ref, other_ref, far, slots[0], weights[0])
+            + mixed_values(own_ref, other_ref, far, slots[1], weights[1])
         )
-
-    def near_two(n, carry):
-        visit_two(NEAR + 2 * n, near_ref)
         return carry
 
-    def far_two(n, carry):
-        visit_two(FAR + 2 * n, far_ref)
-        return carry
-
-    lax.fori_loop(0, (meta_ref[0] + 1) // 2, near_two, 0)
-    lax.fori_loop(0, (meta_ref[1] + 1) // 2, far_two, 0)
+    lax.fori_loop(0, (meta_ref[far] + 1) // 2, two, 0)
+
+
+def near_kernel(meta_ref, query_ref, keys_ref, own_ref, other_ref, top, bottom, summed):
+    seg_len = keys_ref.shape[3]
+    shape = (seg_len, query_ref.shape[1])
+    key_at = lax.broadcasted_iota(jnp.int32, shape, 0)
+    query_at = lax.broadcasted_iota(jnp.int32, shape, 1) % seg_len
+    own = lax.axis_index(SEG)
+    masked = scored(query_ref, keys_ref, own, key_at <= query_at)
+    peak = jnp.max(masked, axis=0, keepdims=True)
+    weights = jnp.exp(masked - peak)
+    top[...] = peak
+    bottom[...] = jnp.sum(weights, axis=0, keepdims=True)
+    summed[...] = mixed_values(own_ref, other_ref, 0, own, weights)
+    visit(meta_ref, 0, query_ref, keys_ref, own_ref, other_ref, top, bottom, summed)
+
+
+def far_kernel(
+    meta_ref,
+    query_ref,
+    keys_ref,
+    own_ref,
+    other_ref,
+    near_top,
+    near_bottom,
+    near_summed,
+    out_ref,
+    top,
+    bottom,
+    summed,
+):
+    top[...] = near_top[...]
+    bottom[...] = near_bottom[...]
+    summed[...] = near_summed[...]
+    visit(meta_ref, 1, query_ref, keys_ref, own_ref, other_ref, top, bottom, summed)
+    seg_len = keys_ref.shape[3]
     scaled = summed[...] / bottom[...]
     result = jnp.zeros((1, seg_len), jnp.float32)
-    for h in range(heads):
+    for h in range(query_ref.shape[1] // seg_len):
         part = scaled[:, h * seg_len : (h + 1) * seg_len]
         result += part[h : h + 1] + part[2 + h : 3 + h]
     for i in range(out_ref.shape[0]):
@@ -314,13 +326,21 @@
     other = lax.ppermute(w_query, "zl", swap)
     values_x = gathered(jnp.broadcast_to(value_weight.T[None], (quarters, width, seg_len)), "x")
     readout = head_readout.reshape(heads, HEAD_SIZE).astype(jnp.float32)
-    key_rows = key_weight.T.astype(jnp.float32)
-    values_x, other, readout, key_rows = lax.optimization_barrier(
-        (values_x, other, readout, key_rows)
-    )
-    query_weight = lax.all_gather(
-        jnp.concatenate([w_query, other]), ("y", "c"), axis=0, tiled=True
-    )
+    own_readout = lax.dynamic_slice(
+        resid_head, (lax.axis_index(SEG) * seg_len,), (seg_len,)
+    )
+    key_rows = jnp.concatenate(
+        [
+            jnp.pad(key_weight.T.astype(jnp.float32), ((0, 4), (0, 0))),
+            jnp.pad(own_readout.astype(jnp.float32)[None], ((0, 3), (0, 0))),
+        ]
+    )
+    both = jnp.pad(w_query, ((0, w_query.shape[0]), (0, 0)))
+    values_x, other, readout, key_rows, both = lax.optimization_barrier(
+        (values_x, other, readout, key_rows, both)
+    )
+    both = lax.dynamic_update_slice(both, other, (w_query.shape[0], 0))
+    query_weight = lax.all_gather(both, ("y", "c"), axis=0, tiled=True)
     pieces = pl.pallas_call(
         weights_kernel,
         out_shape=jax.ShapeDtypeStruct((pairs, rows, seg_len), jnp.bfloat16),
@@ -350,10 +370,7 @@
     angles = frequency[:, None] * positions
     cosine = jnp.cos(angles)
     sine = jnp.sin(angles) * jnp.where(dims % 2 == 0, -1.0, 1.0)[:, None]
-    readout_row = resid_head.reshape(1, model_width).astype(jnp.float32)
-    near_weights, cosine, sine, readout_row = lax.optimization_barrier(
-        (near_weights, cosine, sine, readout_row)
-    )
+    near_weights, cosine, sine = lax.optimization_barrier((near_weights, cosine, sine))
 
     far_weights = lax.ppermute(near_weights, "c", swap)
     near_sums = pl.pallas_call(
@@ -368,11 +385,14 @@
         name="project_near_keys",
     )(tokens, near_weights)
     far_weights, near_sums = lax.optimization_barrier((far_weights, near_sums))
-    keys = pl.pallas_call(
+    keys, residual = pl.pallas_call(
         far_keys_kernel,
-        out_shape=jax.ShapeDtypeStruct((lax.axis_size("y"), rows, seg_len), jnp.bfloat16),
+        out_shape=(
+            jax.ShapeDtypeStruct((lax.axis_size("y"), rows, seg_len), jnp.bfloat16),
+            jax.ShapeDtypeStruct((1, seg_len), jnp.float32),
+        ),
         in_specs=[VMEM_SPEC] * 5,
-        out_specs=VMEM_SPEC,
+        out_specs=(VMEM_SPEC, VMEM_SPEC),
         scratch_shapes=[pltpu.VMEM((rows, seg_len), jnp.float32)],
         compiler_params=params,
         name="project_far_keys",
@@ -380,15 +400,17 @@
 
     keys_y = gathered(keys, "y")
     spread = lax.axis_size(("zl", "x"))
+    values = keys_y[:, width:]
+    keys_y = keys_y[:, :width]
     near = gathered(jnp.broadcast_to(keys_y[None], (spread, *keys_y.shape)), ("zl", "x"))
-    queries, residual = pl.pallas_call(
+    values = jnp.stack([values, lax.ppermute(values, "c", swap)])
+    values, query_sine = lax.optimization_barrier((values, sine))
+    other_values = lax.ppermute(values, "zl", swap)
+    queries = pl.pallas_call(
         queries_kernel,
-        out_shape=(
-            jax.ShapeDtypeStruct((HEAD_SIZE, heads * seg_len), jnp.bfloat16),
-            jax.ShapeDtypeStruct((1, seg_len), jnp.float32),
-        ),
-        in_specs=[VMEM_SPEC] * 5,
-        out_specs=(VMEM_SPEC, VMEM_SPEC),
+        out_shape=jax.ShapeDtypeStruct((HEAD_SIZE, heads * seg_len), jnp.bfloat16),
+        in_specs=[VMEM_SPEC] * 4,
+        out_specs=VMEM_SPEC,
         scratch_shapes=[pltpu.VMEM((seg_len, heads * HEAD_SIZE), jnp.float32)],
         cost_estimate=pl.CostEstimate(
             flops=2 * seg_len * model_width * heads * HEAD_SIZE,
@@ -397,28 +419,36 @@
         ),
         compiler_params=params,
         name="project_queries",
-    )(
-        tokens,
-        query_weight.reshape(segments, seg_len, -1),
-        readout_row,
-        cosine,
-        sine,
-    )
-    near, queries = lax.optimization_barrier((near, queries))
+    )(tokens, query_weight.reshape(segments, seg_len, -1), cosine, query_sine)
+    near, queries, other_values = lax.optimization_barrier((near, queries, other_values))
     far = lax.ppermute(near, "c", swap)
+    columns = heads * seg_len
+    state = (
+        jax.ShapeDtypeStruct((1, columns), jnp.float32),
+        jax.ShapeDtypeStruct((1, columns), jnp.float32),
+        jax.ShapeDtypeStruct((8, columns), jnp.float32),
+    )
+    near_state = pl.pallas_call(
+        near_kernel,
+        out_shape=state,
+        in_specs=[SMEM_SPEC] + [VMEM_SPEC] * 4,
+        out_specs=(VMEM_SPEC,) * 3,
+        compiler_params=params,
+        cost_estimate=pl.CostEstimate(
+            flops=2**28, bytes_accessed=2**21, transcendentals=2**19
+        ),
+        name="attend_near",
+    )(meta, queries, near, values, other_values)
+    far, near_state = lax.optimization_barrier((far, near_state))
     mixed = pl.pallas_call(
-        attention_kernel,
+        far_kernel,
         out_shape=jax.ShapeDtypeStruct((fsdp_size, 8, seg_len), jnp.float32),
-        in_specs=[SMEM_SPEC] + [VMEM_SPEC] * 3,
+        in_specs=[SMEM_SPEC] + [VMEM_SPEC] * 7,
         out_specs=VMEM_SPEC,
-        scratch_shapes=[
-            pltpu.VMEM((1, heads * seg_len), jnp.float32),
-            pltpu.VMEM((1, heads * seg_len), jnp.float32),
-            pltpu.VMEM((8, heads * seg_len), jnp.float32),
-        ],
-        compiler_params=params,
-        name="attend",
-    )(meta, queries, near, far)
+        scratch_shapes=[pltpu.VMEM(part.shape, part.dtype) for part in state],
+        compiler_params=params,
+        name="attend_far",
+    )(meta, queries, far, values, other_values, *near_state)
     parts = gathered(mixed, FSDP)
     token_values, leaf_rows = pl.pallas_call(
         finish_kernel,

time: 138 us -> 135 us (0.978)
  waiting for transfers between devices: 21.8 us -> 10 us
  starting transfers between devices: 29.6 us -> 34.1 us
  local copies, waits for them, and re-layouts: 9.22 us -> 13.5 us
  blocking collectives: 47.2 us -> 49.4 us
  other arithmetic: 4.1 us -> 2.48 us
    all_to_all x3, waiting for transfers between devices: 12.6 us -> 6.51 us  [gathered(): return lax.all_to_all(value, axis, 0, 0)]
    ppermute x0 -> x2, starting transfers between devices: none -> 5.91 us  [the longest x1 3.55 us: on_device(): other_values = lax.ppermute(values, 'zl', swap)]
    all_gather x1, waiting for transfers between devices: 5.29 us -> 0.02 us  [on_device(): query_weight = lax.all_gather(both, ('y', 'c'), axis=0, tiled=True)]
    ppermute x0 -> x2, waiting for transfers between devices: none -> 2.9 us  [the longest x1 2.06 us: on_device(): other_values = lax.ppermute(values, 'zl', swap)]
    all_to_all x3, starting transfers between devices: 17.3 us -> 14.5 us  [gathered(): return lax.all_to_all(value, axis, 0, 0)]
    unnamed x14, local copies, waits for them, and re-layouts: 6.66 us -> 9.3 us
    all_to_all x3, blocking collectives: 47.2 us -> 49.4 us  [gathered(): return lax.all_to_all(value, axis, 0, 0)]
    ppermute x1, waiting for transfers between devices: 2.64 us -> 0.57 us  [on_device(): far = lax.ppermute(near, 'c', swap)]
  transfers between devices with their start and end apart: 7 -> 9, of which waited for: 5 -> 6; matrix products, arithmetic and copies ran while one was open for 2% -> 5% of each run, Pallas kernels for 6% -> 6%
where the time goes in v3:
time: 135 us; the launch traced here: 134 us
  blocking collectives  49.4 us (37%)
  starting transfers between devices  34.1 us (25%)
  between operations  14.2 us (11%)
  local copies, waits for them, and re-layouts  13.5 us (10%)
  Pallas kernels  10.8 us (8%)
  waiting for transfers between devices  10 us (7%)
  other arithmetic  2.48 us (2%)
    all_to_all x3, blocking collectives, gathered(): return lax.all_to_all(value, axis, 0, 0)  49.4 us
    all_to_all x3, starting transfers between devices, gathered(): return lax.all_to_all(value, axis, 0, 0)  14.5 us
    unnamed x14, local copies, waits for them, and re-layouts  9.3 us
    all_to_all x3, waiting for transfers between devices, gathered(): return lax.all_to_all(value, axis, 0, 0)  6.51 us
    ppermute x1, starting transfers between devices, on_device(): far_weights = lax.ppermute(near_weights, 'c', swap)  5.91 us
    ppermute x1, starting transfers between devices, on_device(): other = lax.ppermute(w_query, 'zl', swap)  4.83 us
    ppermute x1, starting transfers between devices, on_device(): other_values = lax.ppermute(values, 'zl', swap)  3.55 us
    ppermute x1, starting transfers between devices, on_device(): far = lax.ppermute(near, 'c', swap)  2.96 us
  transfers between devices with their start and end apart: 9, of which 6 were waited for; matrix products, arithmetic and copies ran while one was open for 5% of the time, Pallas kernels for 6%

profile of v3, /device:TPU:1, one launch (start us, length us, event | category | flops | bytes accessed | tf_op | source)
XLA Modules:
  0.0 134.5 jit_solution(7995487630639205452)
XLA Ops:
  7.2 4.8 %collective-permute-start = (bf16[256,256]{1,0:T(8,128)(2,1)}, bf16[256,256]{1,0:T(8,128)(2,1)S(1)}, u32[]{:S(2)}, u32[]{:S(2)}) collective-permute-start(bf16[256,256]{1,0:T(8,128)(2,1)} %param.10), channel_id=1, source_target_pairs={{0,32},{32,0},{1,33},{33,1},{2,34},{34,2},{3,35},{35,3},{4,36},{36... | collective-permute-start | bytes 393224 | tf_op jit(solution)/shard_map/ppermute | solution.py:326
  12.0 1.3 broadcast_in_dim.26
  13.3 4.0 %all-to-all-start = ((bf16[4,32,256]{2,1,0:T(8,128)(2,1)}), bf16[4,32,256]{2,1,0:T(8,128)(2,1)S(1)}, u32[]{:S(2)}, u32[]{:S(2)}) async-start(bf16[4,32,256]{2,1,0:T(8,128)(2,1)} %broadcast_in_dim.26), calls=%async_computation | async-start | bytes 131072 | tf_op jit(solution)/shard_map/all_to_all | solution.py:309
  17.4 0.0 all-gather.2.cloned.1.call-start
  17.4 0.7 bitcast_convert_fusion.readout_ref
  18.0 0.8 dynamic_slice.3
  18.8 0.7 fusion.4.key_ref
  19.5 0.9 pad.16
  20.4 1.4 %all-to-all-done.value_ref = bf16[4,32,256]{2,1,0:T(8,128)(2,1)S(1)} async-done(((bf16[4,32,256]{2,1,0:T(8,128)(2,1)}), bf16[4,32,256]{2,1,0:T(8,128)(2,1)S(1)}, u32[]{:S(2)}, u32[]{:S(2)}) %all-to-all-start) | async-done | bytes 65568 | tf_op jit(solution)/shard_map/all_to_all | solution.py:309
  21.8 0.0 collective-permute-done
  21.9 0.7 copy-done.6
  22.6 0.0 all-gather.2.cloned.1.call-update
  22.6 0.9 fold_weights.1
  23.4 6.9 %all-to-all-start.1 = ((bf16[16,40,256]{2,1,0:T(8,128)(2,1)}), bf16[16,40,256]{2,1,0:T(8,128)(2,1)S(1)}, u32[]{:S(2)}, u32[]{:S(2)}) async-start(bf16[16,40,256]{2,1,0:T(8,128)(2,1)} %fold_weights.1), calls=%async_computation.1 | async-start | bytes 655360 | tf_op jit(solution)/shard_map/all_to_all | solution.py:309
  30.4 0.0 copy-start.3
  30.4 0.6 copy-done.3
  31.0 0.7 copy-done.4
  31.7 0.7 copy-done.5
  32.3 2.9 %tree.1 = (s32[168]{0:T(256)S(1)}, f32[32,128]{1,0:T(8,128)S(1)}, f32[1,256]{1,0:T(1,128)S(1)}) custom-call(s32[32]{0:T(128)S(1)} %copy-done.3, s32[32]{0:T(128)S(1)} %copy-done.4, s32[32]{0:T(128)S(1)} %copy-done.5), custom_call_target="tpu_custom_call" | custom-call | tf_op jit(solution)/shard_map/tree/pallas_call | solution.py:354
  35.3 0.6 fusion
  35.9 4.9 %all-to-all-done.1.weights_ref = bf16[16,40,256]{2,1,0:T(8,128)(2,1)S(1)} async-done(((bf16[16,40,256]{2,1,0:T(8,128)(2,1)}), bf16[16,40,256]{2,1,0:T(8,128)(2,1)S(1)}, u32[]{:S(2)}, u32[]{:S(2)}) %all-to-all-start.1) | async-done | bytes 327712 | tf_op jit(solution)/shard_map/all_to_all | solution.py:309
  40.7 5.9 %collective-permute-start.1 = (bf16[16,40,256]{2,1,0:T(8,128)(2,1)S(1)}, bf16[16,40,256]{2,1,0:T(8,128)(2,1)S(1)}, u32[]{:S(2)}, u32[]{:S(2)}) collective-permute-start(bf16[16,40,256]{2,1,0:T(8,128)(2,1)S(1)} %all-to-all-done.1.weights_ref), channel_id=1, source_target_pairs={{0,16},{16,0},{1,17},{17,1},{2,18},{18,2},{3,19},{19,3},{4,20},{20... | collective-permute-start | bytes 983048 | tf_op jit(solution)/shard_map/ppermute | solution.py:375
  46.7 0.0 copy-start
  46.7 2.3 %copy-done = bf16[256,8192]{1,0:T(8,128)(2,1)S(1)} copy-done((bf16[256,8192]{1,0:T(8,128)(2,1)S(1)}, bf16[256,8192]{1,0:T(8,128)(2,1)}, u32[]{:S(2)}) %copy-start) | copy-done | bytes 4194328
  48.9 0.7 project_near_keys.1.near_ref
  49.7 0.0 collective-permute-done.1.weights_ref
  49.7 0.8 project_far_keys.1
  50.5 14.4 %all_to_all.37 = bf16[8,40,256]{2,1,0:T(8,128)(2,1)S(1)} all-to-all(bf16[8,40,256]{2,1,0:T(8,128)(2,1)S(1)} %get-tuple-element.41), channel_id=1, replica_groups=mesh['y'=8,'zl'=2,'c'=2,'zh'=4,'x'=4] {'y'}, dimensions={0} | all-to-all | bytes 327680 | tf_op jit(solution)/shard_map/all_to_all | solution.py:309
  64.9 1.1 broadcast_in_dim.30
  66.0 3.6 %all-to-all-start.3 = ((bf16[8,8,32,256]{3,2,1,0:T(8,128)(2,1)}), bf16[8,8,32,256]{3,2,1,0:T(8,128)(2,1)S(1)}, u32[]{:S(2)}, u32[]{:S(2)}) async-start(bf16[8,8,32,256]{3,2,1,0:T(8,128)(2,1)} %broadcast_in_dim.30), calls=%async_computation.3 | async-start | bytes 2097152 | tf_op jit(solution)/shard_map/all_to_all | solution.py:309
  69.6 2.4 %collective-permute-start.2 = (bf16[8,8,256]{2,1,0:T(8,128)(2,1)S(1)}, bf16[8,8,256]{2,1,0:T(8,128)(2,1)S(1)}, u32[]{:S(2)}, u32[]{:S(2)}) collective-permute-start(bf16[8,8,256]{2,1,0:T(8,128)(2,1)S(1)} %get-tuple-element.61), channel_id=1, source_target_pairs={{0,16},{16,0},{1,17},{17,1},{2,18},{18,2},{3,19},{19,3},{4,20},{20... | collective-permute-start | bytes 98312 | tf_op jit(solution)/shard_map/ppermute | solution.py:406
  72.0 0.8 collective-permute-done.2
  72.8 3.6 %collective-permute-start.3 = (bf16[2,8,8,256]{3,2,1,0:T(8,128)(2,1)S(1)}, bf16[2,8,8,256]{3,2,1,0:T(8,128)(2,1)S(1)}, u32[]{:S(2)}, u32[]{:S(2)}) collective-permute-start(bf16[2,8,8,256]{3,2,1,0:T(8,128)(2,1)S(1)} %pad_maximum_fusion.own_ref), channel_id=1, source_target_pairs={{0,32},{32,0},{1,33},{33,1},{2,34},{34,2},{3,35},{35,3},{4,36},{36... | collective-permute-start | bytes 196616 | tf_op jit(solution)/shard_map/ppermute | solution.py:408
  76.4 0.0 all-gather.2.cloned.1.call-done
  76.4 0.0 copy-start.1
  76.4 2.2 %copy-done.1 = bf16[256,8192]{1,0:T(8,128)(2,1)S(1)} copy-done((bf16[256,8192]{1,0:T(8,128)(2,1)S(1)}, bf16[256,8192]{1,0:T(8,128)(2,1)}, u32[]{:S(2)}) %copy-start.1) | copy-done | bytes 4194328
  78.6 2.2 %copy-done.2 = bf16[8192,256]{1,0:T(8,128)(2,1)S(1)} copy-done((bf16[8192,256]{1,0:T(8,128)(2,1)S(1)}, bf16[8192,256]{1,0:T(8,128)(2,1)}, u32[]{:S(2)}) %copy-start.2) | copy-done | bytes 4194328
  80.8 1.4 %project_queries.1.query_ref = bf16[128,512]{1,0:T(8,128)(2,1)S(1)} custom-call(bf16[256,8192]{1,0:T(8,128)(2,1)S(1)} %copy-done.1, bf16[32,256,256]{2,1,0:T(8,128)(2,1)S(1)} %bitcast.16, f32[128,256]{1,0:T(8,128)S(1)} %get-tuple-element.39.cosine_ref, f32[128,256]{1,0:T(8,128)S(1)} %get-tuple-element.44.sine_ref), custom_call_target="tpu_custom_call" | custom-call | flops 1073741824 | bytes 8388608 | tf_op jit(solution)/shard_map/project_queries/pallas_call | solution.py:409
  82.2 2.1 %collective-permute-done.3.other_ref = bf16[2,8,8,256]{3,2,1,0:T(8,128)(2,1)S(1)} collective-permute-done((bf16[2,8,8,256]{3,2,1,0:T(8,128)(2,1)S(1)}, bf16[2,8,8,256]{3,2,1,0:T(8,128)(2,1)S(1)}, u32[]{:S(2)}, u32[]{:S(2)}) %collective-permute-start.3) | collective-permute-done | bytes 65568 | tf_op jit(solution)/shard_map/ppermute | solution.py:408
  84.3 0.2 all-to-all-done.3.keys_ref
  84.5 3.0 %collective-permute-start.4 = (bf16[8,8,32,256]{3,2,1,0:T(8,128)(2,1)S(1)}, bf16[8,8,32,256]{3,2,1,0:T(8,128)(2,1)S(1)}, u32[]{:S(2)}, u32[]{:S(2)}) collective-permute-start(bf16[8,8,32,256]{3,2,1,0:T(8,128)(2,1)S(1)} %all-to-all-done.3.keys_ref), channel_id=1, source_target_pairs={{0,16},{16,0},{1,17},{17,1},{2,18},{18,2},{3,19},{19,3},{4,20},{20... | collective-permute-start | bytes 3145736 | tf_op jit(solution)/shard_map/ppermute | solution.py:424
  87.5 1.7 %attend_near.1 = (f32[1,512]{1,0:T(1,128)S(1)}, f32[1,512]{1,0:T(1,128)S(1)}, f32[8,512]{1,0:T(8,128)S(1)}) custom-call(s32[168]{0:T(256)S(1)} %get-tuple-element.31.meta_ref, bf16[128,512]{1,0:T(8,128)(2,1)S(1)} %project_queries.1.query_ref, bf16[8,8,32,256]{3,2,1,0:T(8,128)(2,1)S(1)} %all-to-all-done.3.keys_ref, ...), custom_call_target="tpu_custom_call" | custom-call | flops 268435456 | bytes 2097152 | tf_op jit(solution)/shard_map/attend_near/pallas_call | solution.py:431
  89.2 0.6 collective-permute-done.4.keys_ref
  89.7 1.2 attend_far.1
  91.0 22.3 %all_to_all.38.parts_ref = f32[16,8,256]{2,1,0:T(8,128)S(1)} all-to-all(f32[16,8,256]{2,1,0:T(8,128)S(1)} %attend_far.1), channel_id=1, replica_groups=mesh['y'=8,'zl'=2,'c'=2,'zh'=4,'x'=4] {'zh','x'}, dimensions={0} | all-to-all | bytes 262144 | tf_op jit(solution)/shard_map/all_to_all | solution.py:309
  113.3 1.1 token_values.1
  114.4 12.6 %all_to_all.39 = f32[32,1,128]{2,1,0:T(1,128)S(1)} all-to-all(f32[32,1,128]{2,1,0:T(1,128)S(1)} %bitcast.17), channel_id=1, replica_groups=mesh['y'=8,'zl'=2,'c'=2,'zh'=4,'x'=4] {'y','zl','c'}, dimensions={0} | all-to-all | bytes 32768 | tf_op jit(solution)/shard_map/all_to_all | solution.py:309
  127.1 0.5 multiply_reduce_fusion
  (10 shorter events, 0.1 us)
Async XLA Ops:
  7.2 14.7 %collective-permute-start = (bf16[256,256]{1,0:T(8,128)(2,1)}, bf16[256,256]{1,0:T(8,128)(2,1)S(1)}, u32[]{:S(2)}, u32[]{:S(2)}) collective-permute-start(bf16[256,256]{1,0:T(8,128)(2,1)} %param.10), channel_id=1, source_target_pairs={{0,32},{32,0},{1,33},{33,1},{2,34},{34,2},{3,35},{35,3},{4,36},{36... | collective-permute-start | bytes 393224 | tf_op jit(solution)/shard_map/ppermute | solution.py:326
  13.3 8.5 %all-to-all-start = ((bf16[4,32,256]{2,1,0:T(8,128)(2,1)}), bf16[4,32,256]{2,1,0:T(8,128)(2,1)S(1)}, u32[]{:S(2)}, u32[]{:S(2)}) async-start(bf16[4,32,256]{2,1,0:T(8,128)(2,1)} %broadcast_in_dim.26), calls=%async_computation | async-start | bytes 131072 | tf_op jit(solution)/shard_map/all_to_all | solution.py:309
  17.4 59.1 %all-gather.2.cloned.1.call-start = ((), (), s32[]{:S(2)}) async-start(), calls=%async_computation.6 | async-start | bytes 4456448 | tf_op jit(solution)/shard_map/all_gather | solution.py:343
  21.9 0.7 copy-start.6
  23.4 17.3 %all-to-all-start.1 = ((bf16[16,40,256]{2,1,0:T(8,128)(2,1)}), bf16[16,40,256]{2,1,0:T(8,128)(2,1)S(1)}, u32[]{:S(2)}, u32[]{:S(2)}) async-start(bf16[16,40,256]{2,1,0:T(8,128)(2,1)} %fold_weights.1), calls=%async_computation.1 | async-start | bytes 655360 | tf_op jit(solution)/shard_map/all_to_all | solution.py:309
  30.4 0.7 copy-start.3
  31.0 0.7 copy-start.4
  31.7 0.7 copy-start.5
  40.7 9.0 %collective-permute-start.1 = (bf16[16,40,256]{2,1,0:T(8,128)(2,1)S(1)}, bf16[16,40,256]{2,1,0:T(8,128)(2,1)S(1)}, u32[]{:S(2)}, u32[]{:S(2)}) collective-permute-start(bf16[16,40,256]{2,1,0:T(8,128)(2,1)S(1)} %all-to-all-done.1.weights_ref), channel_id=1, source_target_pairs={{0,16},{16,0},{1,17},{17,1},{2,18},{18,2},{3,19},{19,3},{4,20},{20... | collective-permute-start | bytes 983048 | tf_op jit(solution)/shard_map/ppermute | solution.py:375
  46.7 2.3 %copy-start = (bf16[256,8192]{1,0:T(8,128)(2,1)S(1)}, bf16[256,8192]{1,0:T(8,128)(2,1)}, u32[]{:S(2)}) copy-start(bf16[256,8192]{1,0:T(8,128)(2,1)} %tokens_ref.5) | copy-start | bytes 12582916
  66.0 18.5 %all-to-all-start.3 = ((bf16[8,8,32,256]{3,2,1,0:T(8,128)(2,1)}), bf16[8,8,32,256]{3,2,1,0:T(8,128)(2,1)S(1)}, u32[]{:S(2)}, u32[]{:S(2)}) async-start(bf16[8,8,32,256]{3,2,1,0:T(8,128)(2,1)} %broadcast_in_dim.30), calls=%async_computation.3 | async-start | bytes 2097152 | tf_op jit(solution)/shard_map/all_to_all | solution.py:309
  69.6 3.2 %collective-permute-start.2 = (bf16[8,8,256]{2,1,0:T(8,128)(2,1)S(1)}, bf16[8,8,256]{2,1,0:T(8,128)(2,1)S(1)}, u32[]{:S(2)}, u32[]{:S(2)}) collective-permute-start(bf16[8,8,256]{2,1,0:T(8,128)(2,1)S(1)} %get-tuple-element.61), channel_id=1, source_target_pairs={{0,16},{16,0},{1,17},{17,1},{2,18},{18,2},{3,19},{19,3},{4,20},{20... | collective-permute-start | bytes 98312 | tf_op jit(solution)/shard_map/ppermute | solution.py:406
  72.8 11.4 %collective-permute-start.3 = (bf16[2,8,8,256]{3,2,1,0:T(8,128)(2,1)S(1)}, bf16[2,8,8,256]{3,2,1,0:T(8,128)(2,1)S(1)}, u32[]{:S(2)}, u32[]{:S(2)}) collective-permute-start(bf16[2,8,8,256]{3,2,1,0:T(8,128)(2,1)S(1)} %pad_maximum_fusion.own_ref), channel_id=1, source_target_pairs={{0,32},{32,0},{1,33},{33,1},{2,34},{34,2},{3,35},{35,3},{4,36},{36... | collective-permute-start | bytes 196616 | tf_op jit(solution)/shard_map/ppermute | solution.py:408
  76.4 2.2 %copy-start.1 = (bf16[256,8192]{1,0:T(8,128)(2,1)S(1)}, bf16[256,8192]{1,0:T(8,128)(2,1)}, u32[]{:S(2)}) copy-start(bf16[256,8192]{1,0:T(8,128)(2,1)} %tokens_ref.5) | copy-start | bytes 12582916
  78.6 2.2 %copy-start.2 = (bf16[8192,256]{1,0:T(8,128)(2,1)S(1)}, bf16[8192,256]{1,0:T(8,128)(2,1)}, u32[]{:S(2)}) copy-start(bf16[8192,256]{1,0:T(8,128)(2,1)} %all-gather.2.cloned.1.call-done) | copy-start | bytes 12582916
  84.5 5.2 %collective-permute-start.4 = (bf16[8,8,32,256]{3,2,1,0:T(8,128)(2,1)S(1)}, bf16[8,8,32,256]{3,2,1,0:T(8,128)(2,1)S(1)}, u32[]{:S(2)}, u32[]{:S(2)}) collective-permute-start(bf16[8,8,32,256]{3,2,1,0:T(8,128)(2,1)S(1)} %all-to-all-done.3.keys_ref), channel_id=1, source_target_pairs={{0,16},{16,0},{1,17},{17,1},{2,18},{18,2},{3,19},{19,3},{4,20},{20... | collective-permute-start | bytes 3145736 | tf_op jit(solution)/shard_map/ppermute | solution.py:424
Sparse Core Ops, SparseCore 0:
  22.7 51.3 all-gather.1

commit v4 on v3

--- a/solution.py
+++ b/solution.py
@@ -26,6 +26,8 @@
     meta_ref,
     table_ref,
     position_ref,
+    live_ref,
+    last_ref,
     parents_ref,
     placed_ref,
     lengths_ref,
@@ -73,9 +75,10 @@
     )
     meta_ref[0] = near
     meta_ref[1] = far
-    meta_ref[2] = lengths_ref[own]
     index = lax.broadcasted_iota(jnp.int32, position_ref.shape, 1)
     position_ref[...] = (offset + index).astype(jnp.float32)
+    live_ref[...] = jnp.where(index < lengths_ref[own], 1.0, 0.0)
+    last_ref[...] = jnp.where(index == lengths_ref[own] - 1, 1.0, 0.0)
 
     row = lax.broadcasted_iota(jnp.int32, (128, 128), 0)
     col = lax.broadcasted_iota(jnp.int32, (128, 128), 1)
@@ -295,13 +298,11 @@
         out_ref[i] = jnp.broadcast_to(result, out_ref.shape[1:])
 
 
-def finish_kernel(meta_ref, parts_ref, resid_ref, out_ref, leaf_ref):
+def finish_kernel(parts_ref, resid_ref, live_ref, last_ref, out_ref, leaf_ref):
     total = resid_ref[...] + jnp.sum(parts_ref[...], axis=0)[:1]
-    index = lax.broadcasted_iota(jnp.int32, total.shape, 1)
-    length = meta_ref[2]
-    values = jnp.where(index < length, total, 0.0)
+    values = jnp.where(live_ref[...] > 0.5, total, 0.0)
     out_ref[...] = values
-    leaf = jnp.sum(jnp.where(index == length - 1, values, 0.0), axis=1, keepdims=True)
+    leaf = jnp.sum(jnp.where(last_ref[...] > 0.5, values, 0.0), axis=1, keepdims=True)
     leaf_ref[...] = jnp.broadcast_to(leaf, leaf_ref.shape)
 
 
@@ -323,8 +324,10 @@
     swap = [(0, 1), (1, 0)]
     params = pltpu.CompilerParams(vmem_limit_bytes=VMEM_LIMIT)
 
+    sent = jnp.broadcast_to(value_weight.T[None], (quarters, width, seg_len))
+    sent, w_query = lax.optimization_barrier((sent, w_query))
     other = lax.ppermute(w_query, "zl", swap)
-    values_x = gathered(jnp.broadcast_to(value_weight.T[None], (quarters, width, seg_len)), "x")
+    values_x = gathered(sent, "x")
     readout = head_readout.reshape(heads, HEAD_SIZE).astype(jnp.float32)
     own_readout = lax.dynamic_slice(
         resid_head, (lax.axis_index(SEG) * seg_len,), (seg_len,)
@@ -351,15 +354,18 @@
     )(values_x, readout, key_rows)
 
     near_weights = gathered(pieces, ("y", "zl"))
-    meta, table, positions = pl.pallas_call(
+    by_token = jax.ShapeDtypeStruct((1, seg_len), jnp.float32)
+    meta, table, positions, live, last = pl.pallas_call(
         tree_kernel,
         out_shape=(
             jax.ShapeDtypeStruct((META,), jnp.int32),
             jax.ShapeDtypeStruct((segments, 128), jnp.float32),
-            jax.ShapeDtypeStruct((1, seg_len), jnp.float32),
+            by_token,
+            by_token,
+            by_token,
         ),
         in_specs=[HBM_SPEC] * 3,
-        out_specs=(SMEM_SPEC, VMEM_SPEC, VMEM_SPEC),
+        out_specs=(SMEM_SPEC,) + (VMEM_SPEC,) * 4,
         scratch_shapes=[pltpu.SMEM((segments,), jnp.int32)] * 4
         + [pltpu.SemaphoreType.DMA((3,))],
         compiler_params=params,
@@ -456,11 +462,11 @@
             jax.ShapeDtypeStruct((1, seg_len), jnp.float32),
             jax.ShapeDtypeStruct((segments, 128), jnp.float32),
         ),
-        in_specs=[SMEM_SPEC, VMEM_SPEC, VMEM_SPEC],
+        in_specs=[VMEM_SPEC] * 4,
         out_specs=(VMEM_SPEC, VMEM_SPEC),
         compiler_params=params,
         name="token_values",
-    )(meta, parts, residual)
+    )(parts, residual, live, last)
     leaves = gathered(leaf_rows, SEG)
     branch = jnp.sum(leaves * table, axis=0)[:segments]
     return (token_values.reshape(seg_len), branch)

time: 135 us -> 134 us (level)
  blocking collectives: 49.4 us -> 47.7 us
    all_to_all x3, blocking collectives: 49.4 us -> 47.7 us  [gathered(): return lax.all_to_all(value, axis, 0, 0)]
  transfers between devices with their start and end apart: 9 -> 9, of which waited for: 6 -> 6; matrix products, arithmetic and copies ran while one was open for 5% -> 4% of each run, Pallas kernels for 6% -> 6%
where the time goes in v4:
time: 134 us
  blocking collectives  47.7 us (36%)
  starting transfers between devices  34.1 us (25%)
  between operations  14.2 us (11%)
  local copies, waits for them, and re-layouts  13.5 us (10%)
  Pallas kernels  11.6 us (9%)
  waiting for transfers between devices  9.98 us (7%)
  other arithmetic  2.48 us (2%)
    all_to_all x3, blocking collectives, gathered(): return lax.all_to_all(value, axis, 0, 0)  47.7 us
    all_to_all x3, starting transfers between devices, gathered(): return lax.all_to_all(value, axis, 0, 0)  14.5 us
    unnamed x14, local copies, waits for them, and re-layouts  9.3 us
    all_to_all x3, waiting for transfers between devices, gathered(): return lax.all_to_all(value, axis, 0, 0)  6.47 us
    ppermute x1, starting transfers between devices, on_device(): far_weights = lax.ppermute(near_weights, 'c', swap)  5.91 us
    ppermute x1, starting transfers between devices, on_device(): other = lax.ppermute(w_query, 'zl', swap)  4.82 us
    ppermute x1, starting transfers between devices, on_device(): other_values = lax.ppermute(values, 'zl', swap)  3.55 us
    pallas_call x1, Pallas kernels, on_device(): pl.pallas_call(tree_kernel, out_shape=(jax.ShapeDtypeStruct((META,), jnp....  2.99 us
  transfers between devices with their start and end apart: 9, of which 6 were waited for; matrix products, arithmetic and copies ran while one was open for 4% of the time, Pallas kernels for 6%

profile of v4, /device:TPU:1, one launch (start us, length us, event | category | flops | bytes accessed | tf_op | source)
XLA Modules:
  0.0 133.6 jit_solution(2657551123546128989)
XLA Ops:
  7.2 1.3 %broadcast_in_dim.26 = bf16[4,32,256]{2,1,0:T(8,128)(2,1)} broadcast(bf16[32,256]{1,0:T(8,128)(2,1)} %bitcast.21), dimensions={1,2} | broadcast | bytes 81920 | tf_op jit(solution)/shard_map/broadcast_in_dim | solution.py:327
  8.5 4.8 %collective-permute-start = (bf16[256,256]{1,0:T(8,128)(2,1)}, bf16[256,256]{1,0:T(8,128)(2,1)S(1)}, u32[]{:S(2)}, u32[]{:S(2)}) collective-permute-start(bf16[256,256]{1,0:T(8,128)(2,1)} %param.10), channel_id=1, source_target_pairs={{0,32},{32,0},{1,33},{33,1},{2,34},{34,2},{3,35},{35,3},{4,36},{36... | collective-permute-start | bytes 393224 | tf_op jit(solution)/shard_map/ppermute | solution.py:329
  13.3 4.0 %all-to-all-start = ((bf16[4,32,256]{2,1,0:T(8,128)(2,1)}), bf16[4,32,256]{2,1,0:T(8,128)(2,1)S(1)}, u32[]{:S(2)}, u32[]{:S(2)}) async-start(bf16[4,32,256]{2,1,0:T(8,128)(2,1)} %broadcast_in_dim.26), calls=%async_computation | async-start | bytes 131072 | tf_op jit(solution)/shard_map/all_to_all | solution.py:310
  17.4 0.0 all-gather.2.cloned.1.call-start
  17.4 0.7 bitcast_convert_fusion.readout_ref
  18.0 0.8 dynamic_slice.3
  18.8 0.7 fusion.4.key_ref
  19.5 0.9 pad.16
  20.4 1.4 %all-to-all-done.value_ref = bf16[4,32,256]{2,1,0:T(8,128)(2,1)S(1)} async-done(((bf16[4,32,256]{2,1,0:T(8,128)(2,1)}), bf16[4,32,256]{2,1,0:T(8,128)(2,1)S(1)}, u32[]{:S(2)}, u32[]{:S(2)}) %all-to-all-start) | async-done | bytes 65568 | tf_op jit(solution)/shard_map/all_to_all | solution.py:310
  21.8 0.0 collective-permute-done
  21.9 0.7 copy-done.6
  22.6 0.0 all-gather.2.cloned.1.call-update
  22.6 0.9 fold_weights.1
  23.4 6.9 %all-to-all-start.1 = ((bf16[16,40,256]{2,1,0:T(8,128)(2,1)}), bf16[16,40,256]{2,1,0:T(8,128)(2,1)S(1)}, u32[]{:S(2)}, u32[]{:S(2)}) async-start(bf16[16,40,256]{2,1,0:T(8,128)(2,1)} %fold_weights.1), calls=%async_computation.1 | async-start | bytes 655360 | tf_op jit(solution)/shard_map/all_to_all | solution.py:310
  30.4 0.0 copy-start.3
  30.4 0.6 copy-done.3
  31.0 0.7 copy-done.4
  31.7 0.7 copy-done.5
  32.3 3.0 %tree.1 = (s32[168]{0:T(256)S(1)}, f32[32,128]{1,0:T(8,128)S(1)}, f32[1,256]{1,0:T(1,128)S(1)}, f32[1,256]{1,0:T(1,128)S(1)}, f32[1,256]{1,0:T(1,128)S(1)}) custom-call(s32[32]{0:T(128)S(1)} %copy-done.3, s32[32]{0:T(128)S(1)} %copy-done.4, s32[32]{0:T(128)S(1)} %copy-done.5), custom_call_target="tpu_custom_call" | custom-call | tf_op jit(solution)/shard_map/tree/pallas_call | solution.py:358
  35.4 0.6 fusion
  35.9 4.8 %all-to-all-done.1.weights_ref = bf16[16,40,256]{2,1,0:T(8,128)(2,1)S(1)} async-done(((bf16[16,40,256]{2,1,0:T(8,128)(2,1)}), bf16[16,40,256]{2,1,0:T(8,128)(2,1)S(1)}, u32[]{:S(2)}, u32[]{:S(2)}) %all-to-all-start.1) | async-done | bytes 327712 | tf_op jit(solution)/shard_map/all_to_all | solution.py:310
  40.7 5.9 %collective-permute-start.1 = (bf16[16,40,256]{2,1,0:T(8,128)(2,1)S(1)}, bf16[16,40,256]{2,1,0:T(8,128)(2,1)S(1)}, u32[]{:S(2)}, u32[]{:S(2)}) collective-permute-start(bf16[16,40,256]{2,1,0:T(8,128)(2,1)S(1)} %all-to-all-done.1.weights_ref), channel_id=1, source_target_pairs={{0,16},{16,0},{1,17},{17,1},{2,18},{18,2},{3,19},{19,3},{4,20},{20... | collective-permute-start | bytes 983048 | tf_op jit(solution)/shard_map/ppermute | solution.py:381
  46.7 0.0 copy-start
  46.7 2.3 %copy-done = bf16[256,8192]{1,0:T(8,128)(2,1)S(1)} copy-done((bf16[256,8192]{1,0:T(8,128)(2,1)S(1)}, bf16[256,8192]{1,0:T(8,128)(2,1)}, u32[]{:S(2)}) %copy-start) | copy-done | bytes 4194328
  48.9 0.7 project_near_keys.1.near_ref
  49.7 0.0 collective-permute-done.1.weights_ref
  49.7 0.8 project_far_keys.1
  50.5 14.4 %all_to_all.37 = bf16[8,40,256]{2,1,0:T(8,128)(2,1)S(1)} all-to-all(bf16[8,40,256]{2,1,0:T(8,128)(2,1)S(1)} %get-tuple-element.47), channel_id=1, replica_groups=mesh['y'=8,'zl'=2,'c'=2,'zh'=4,'x'=4] {'y'}, dimensions={0} | all-to-all | bytes 327680 | tf_op jit(solution)/shard_map/all_to_all | solution.py:310
  64.9 1.1 broadcast_in_dim.30
  66.0 3.6 %all-to-all-start.3 = ((bf16[8,8,32,256]{3,2,1,0:T(8,128)(2,1)}), bf16[8,8,32,256]{3,2,1,0:T(8,128)(2,1)S(1)}, u32[]{:S(2)}, u32[]{:S(2)}) async-start(bf16[8,8,32,256]{3,2,1,0:T(8,128)(2,1)} %broadcast_in_dim.30), calls=%async_computation.3 | async-start | bytes 2097152 | tf_op jit(solution)/shard_map/all_to_all | solution.py:310
  69.6 2.4 %collective-permute-start.2 = (bf16[8,8,256]{2,1,0:T(8,128)(2,1)S(1)}, bf16[8,8,256]{2,1,0:T(8,128)(2,1)S(1)}, u32[]{:S(2)}, u32[]{:S(2)}) collective-permute-start(bf16[8,8,256]{2,1,0:T(8,128)(2,1)S(1)} %get-tuple-element.69), channel_id=1, source_target_pairs={{0,16},{16,0},{1,17},{17,1},{2,18},{18,2},{3,19},{19,3},{4,20},{20... | collective-permute-start | bytes 98312 | tf_op jit(solution)/shard_map/ppermute | solution.py:412
  72.0 0.8 collective-permute-done.2
  72.8 3.6 %collective-permute-start.3 = (bf16[2,8,8,256]{3,2,1,0:T(8,128)(2,1)S(1)}, bf16[2,8,8,256]{3,2,1,0:T(8,128)(2,1)S(1)}, u32[]{:S(2)}, u32[]{:S(2)}) collective-permute-start(bf16[2,8,8,256]{3,2,1,0:T(8,128)(2,1)S(1)} %pad_maximum_fusion.own_ref), channel_id=1, source_target_pairs={{0,32},{32,0},{1,33},{33,1},{2,34},{34,2},{3,35},{35,3},{4,36},{36... | collective-permute-start | bytes 196616 | tf_op jit(solution)/shard_map/ppermute | solution.py:414
  76.4 0.0 all-gather.2.cloned.1.call-done
  76.4 0.0 copy-start.1
  76.4 2.2 %copy-done.1 = bf16[256,8192]{1,0:T(8,128)(2,1)S(1)} copy-done((bf16[256,8192]{1,0:T(8,128)(2,1)S(1)}, bf16[256,8192]{1,0:T(8,128)(2,1)}, u32[]{:S(2)}) %copy-start.1) | copy-done | bytes 4194328
  78.6 2.2 %copy-done.2 = bf16[8192,256]{1,0:T(8,128)(2,1)S(1)} copy-done((bf16[8192,256]{1,0:T(8,128)(2,1)S(1)}, bf16[8192,256]{1,0:T(8,128)(2,1)}, u32[]{:S(2)}) %copy-start.2) | copy-done | bytes 4194328
  80.8 1.4 %project_queries.1.query_ref = bf16[128,512]{1,0:T(8,128)(2,1)S(1)} custom-call(bf16[256,8192]{1,0:T(8,128)(2,1)S(1)} %copy-done.1, bf16[32,256,256]{2,1,0:T(8,128)(2,1)S(1)} %bitcast.16, f32[128,256]{1,0:T(8,128)S(1)} %get-tuple-element.45.cosine_ref, f32[128,256]{1,0:T(8,128)S(1)} %get-tuple-element.50.sine_ref), custom_call_target="tpu_custom_call" | custom-call | flops 1073741824 | bytes 8388608 | tf_op jit(solution)/shard_map/project_queries/pallas_call | solution.py:415
  82.2 2.1 %collective-permute-done.3.other_ref = bf16[2,8,8,256]{3,2,1,0:T(8,128)(2,1)S(1)} collective-permute-done((bf16[2,8,8,256]{3,2,1,0:T(8,128)(2,1)S(1)}, bf16[2,8,8,256]{3,2,1,0:T(8,128)(2,1)S(1)}, u32[]{:S(2)}, u32[]{:S(2)}) %collective-permute-start.3) | collective-permute-done | bytes 65568 | tf_op jit(solution)/shard_map/ppermute | solution.py:414
  84.3 0.2 all-to-all-done.3.keys_ref
  84.5 3.0 %collective-permute-start.4 = (bf16[8,8,32,256]{3,2,1,0:T(8,128)(2,1)S(1)}, bf16[8,8,32,256]{3,2,1,0:T(8,128)(2,1)S(1)}, u32[]{:S(2)}, u32[]{:S(2)}) collective-permute-start(bf16[8,8,32,256]{3,2,1,0:T(8,128)(2,1)S(1)} %all-to-all-done.3.keys_ref), channel_id=1, source_target_pairs={{0,16},{16,0},{1,17},{17,1},{2,18},{18,2},{3,19},{19,3},{4,20},{20... | collective-permute-start | bytes 3145736 | tf_op jit(solution)/shard_map/ppermute | solution.py:430
  87.5 1.7 %attend_near.1 = (f32[1,512]{1,0:T(1,128)S(1)}, f32[1,512]{1,0:T(1,128)S(1)}, f32[8,512]{1,0:T(8,128)S(1)}) custom-call(s32[168]{0:T(256)S(1)} %get-tuple-element.35.meta_ref, bf16[128,512]{1,0:T(8,128)(2,1)S(1)} %project_queries.1.query_ref, bf16[8,8,32,256]{3,2,1,0:T(8,128)(2,1)S(1)} %all-to-all-done.3.keys_ref, ...), custom_call_target="tpu_custom_call" | custom-call | flops 268435456 | bytes 2097152 | tf_op jit(solution)/shard_map/attend_near/pallas_call | solution.py:437
  89.2 0.6 collective-permute-done.4.keys_ref
  89.7 2.6 %attend_far.1 = f32[16,8,256]{2,1,0:T(8,128)S(1)} custom-call(s32[168]{0:T(256)S(1)} %get-tuple-element.35.meta_ref, bf16[128,512]{1,0:T(8,128)(2,1)S(1)} %project_queries.1.query_ref, bf16[8,8,32,256]{3,2,1,0:T(8,128)(2,1)S(1)} %collective-permute-done.4.keys_ref, bf16[2,8,8,256]{3,2,1,0:T(8,128)(2,1)S(1)} %pad_maximum_fusion.own_ref, ...), custom_call_target="tpu_custom_call" | custom-call | tf_op jit(solution)/shard_map/attend_far/pallas_call | solution.py:449
  92.3 22.5 %all_to_all.38.parts_ref = f32[16,8,256]{2,1,0:T(8,128)S(1)} all-to-all(f32[16,8,256]{2,1,0:T(8,128)S(1)} %attend_far.1), channel_id=1, replica_groups=mesh['y'=8,'zl'=2,'c'=2,'zh'=4,'x'=4] {'zh','x'}, dimensions={0} | all-to-all | bytes 262144 | tf_op jit(solution)/shard_map/all_to_all | solution.py:310
  114.9 0.6 token_values.1
  115.4 10.7 %all_to_all.39 = f32[32,1,128]{2,1,0:T(1,128)S(1)} all-to-all(f32[32,1,128]{2,1,0:T(1,128)S(1)} %bitcast.17), channel_id=1, replica_groups=mesh['y'=8,'zl'=2,'c'=2,'zh'=4,'x'=4] {'y','zl','c'}, dimensions={0} | all-to-all | bytes 32768 | tf_op jit(solution)/shard_map/all_to_all | solution.py:310
  126.2 0.5 multiply_reduce_fusion
  (10 shorter events, 0.1 us)
Async XLA Ops:
  8.5 13.3 %collective-permute-start = (bf16[256,256]{1,0:T(8,128)(2,1)}, bf16[256,256]{1,0:T(8,128)(2,1)S(1)}, u32[]{:S(2)}, u32[]{:S(2)}) collective-permute-start(bf16[256,256]{1,0:T(8,128)(2,1)} %param.10), channel_id=1, source_target_pairs={{0,32},{32,0},{1,33},{33,1},{2,34},{34,2},{3,35},{35,3},{4,36},{36... | collective-permute-start | bytes 393224 | tf_op jit(solution)/shard_map/ppermute | solution.py:329
  13.3 8.5 %all-to-all-start = ((bf16[4,32,256]{2,1,0:T(8,128)(2,1)}), bf16[4,32,256]{2,1,0:T(8,128)(2,1)S(1)}, u32[]{:S(2)}, u32[]{:S(2)}) async-start(bf16[4,32,256]{2,1,0:T(8,128)(2,1)} %broadcast_in_dim.26), calls=%async_computation | async-start | bytes 131072 | tf_op jit(solution)/shard_map/all_to_all | solution.py:310
  17.4 59.1 %all-gather.2.cloned.1.call-start = ((), (), s32[]{:S(2)}) async-start(), calls=%async_computation.6 | async-start | bytes 4456448 | tf_op jit(solution)/shard_map/all_gather | solution.py:346
  21.9 0.7 copy-start.6
  23.4 17.3 %all-to-all-start.1 = ((bf16[16,40,256]{2,1,0:T(8,128)(2,1)}), bf16[16,40,256]{2,1,0:T(8,128)(2,1)S(1)}, u32[]{:S(2)}, u32[]{:S(2)}) async-start(bf16[16,40,256]{2,1,0:T(8,128)(2,1)} %fold_weights.1), calls=%async_computation.1 | async-start | bytes 655360 | tf_op jit(solution)/shard_map/all_to_all | solution.py:310
  30.4 0.7 copy-start.3
  31.0 0.7 copy-start.4
  31.7 0.7 copy-start.5
  40.7 9.0 %collective-permute-start.1 = (bf16[16,40,256]{2,1,0:T(8,128)(2,1)S(1)}, bf16[16,40,256]{2,1,0:T(8,128)(2,1)S(1)}, u32[]{:S(2)}, u32[]{:S(2)}) collective-permute-start(bf16[16,40,256]{2,1,0:T(8,128)(2,1)S(1)} %all-to-all-done.1.weights_ref), channel_id=1, source_target_pairs={{0,16},{16,0},{1,17},{17,1},{2,18},{18,2},{3,19},{19,3},{4,20},{20... | collective-permute-start | bytes 983048 | tf_op jit(solution)/shard_map/ppermute | solution.py:381
  46.7 2.3 %copy-start = (bf16[256,8192]{1,0:T(8,128)(2,1)S(1)}, bf16[256,8192]{1,0:T(8,128)(2,1)}, u32[]{:S(2)}) copy-start(bf16[256,8192]{1,0:T(8,128)(2,1)} %tokens_ref.5) | copy-start | bytes 12582916
  66.0 18.5 %all-to-all-start.3 = ((bf16[8,8,32,256]{3,2,1,0:T(8,128)(2,1)}), bf16[8,8,32,256]{3,2,1,0:T(8,128)(2,1)S(1)}, u32[]{:S(2)}, u32[]{:S(2)}) async-start(bf16[8,8,32,256]{3,2,1,0:T(8,128)(2,1)} %broadcast_in_dim.30), calls=%async_computation.3 | async-start | bytes 2097152 | tf_op jit(solution)/shard_map/all_to_all | solution.py:310
  69.6 3.2 %collective-permute-start.2 = (bf16[8,8,256]{2,1,0:T(8,128)(2,1)S(1)}, bf16[8,8,256]{2,1,0:T(8,128)(2,1)S(1)}, u32[]{:S(2)}, u32[]{:S(2)}) collective-permute-start(bf16[8,8,256]{2,1,0:T(8,128)(2,1)S(1)} %get-tuple-element.69), channel_id=1, source_target_pairs={{0,16},{16,0},{1,17},{17,1},{2,18},{18,2},{3,19},{19,3},{4,20},{20... | collective-permute-start | bytes 98312 | tf_op jit(solution)/shard_map/ppermute | solution.py:412
  72.8 11.4 %collective-permute-start.3 = (bf16[2,8,8,256]{3,2,1,0:T(8,128)(2,1)S(1)}, bf16[2,8,8,256]{3,2,1,0:T(8,128)(2,1)S(1)}, u32[]{:S(2)}, u32[]{:S(2)}) collective-permute-start(bf16[2,8,8,256]{3,2,1,0:T(8,128)(2,1)S(1)} %pad_maximum_fusion.own_ref), channel_id=1, source_target_pairs={{0,32},{32,0},{1,33},{33,1},{2,34},{34,2},{3,35},{35,3},{4,36},{36... | collective-permute-start | bytes 196616 | tf_op jit(solution)/shard_map/ppermute | solution.py:414
  76.4 2.2 %copy-start.1 = (bf16[256,8192]{1,0:T(8,128)(2,1)S(1)}, bf16[256,8192]{1,0:T(8,128)(2,1)}, u32[]{:S(2)}) copy-start(bf16[256,8192]{1,0:T(8,128)(2,1)} %tokens_ref.5) | copy-start | bytes 12582916
  78.6 2.2 %copy-start.2 = (bf16[8192,256]{1,0:T(8,128)(2,1)S(1)}, bf16[8192,256]{1,0:T(8,128)(2,1)}, u32[]{:S(2)}) copy-start(bf16[8192,256]{1,0:T(8,128)(2,1)} %all-gather.2.cloned.1.call-done) | copy-start | bytes 12582916
  84.5 5.2 %collective-permute-start.4 = (bf16[8,8,32,256]{3,2,1,0:T(8,128)(2,1)S(1)}, bf16[8,8,32,256]{3,2,1,0:T(8,128)(2,1)S(1)}, u32[]{:S(2)}, u32[]{:S(2)}) collective-permute-start(bf16[8,8,32,256]{3,2,1,0:T(8,128)(2,1)S(1)} %all-to-all-done.3.keys_ref), channel_id=1, source_target_pairs={{0,16},{16,0},{1,17},{17,1},{2,18},{18,2},{3,19},{19,3},{4,20},{20... | collective-permute-start | bytes 3145736 | tf_op jit(solution)/shard_map/ppermute | solution.py:430
Sparse Core Ops, SparseCore 0:
  22.7 51.3 all-gather.1

commit v5 on v4

--- a/solution.py
+++ b/solution.py
@@ -12,6 +12,8 @@
 SEG = ("y", "zl", "c")
 FSDP = ("zh", "x")
 NEAR, FAR, LENGTHS, META = 8, 48, 80, 168
+UNSEEN = -1e30
+LOG2_E = 1.4426950408889634
 VMEM_LIMIT = 40 * 1024 * 1024
 
 VMEM_SPEC = pl.BlockSpec(memory_space=pltpu.VMEM)
@@ -203,7 +205,17 @@
         ).astype(jnp.bfloat16)
 
 
-def scored(query_ref, keys_ref, slot, seen):
+def spread_kernel(keys_ref, out_ref, sems):
+    copies = [
+        pltpu.make_async_copy(keys_ref, out_ref.at[i], sems.at[i]) for i in range(out_ref.shape[0])
+    ]
+    for copy in copies:
+        copy.start()
+    for copy in copies:
+        copy.wait()
+
+
+def scored(query_ref, keys_ref, slot):
     quarters = lax.axis_size("x")
     seg_len = keys_ref.shape[3]
     keys = keys_ref[pl.ds(slot // 2 % 2 * quarters, quarters), slot // 4]
@@ -213,7 +225,7 @@
         (((0,), (0,)), ((), ())),
         preferred_element_type=jnp.float32,
     )
-    return jnp.where(seen, raw * HEAD_SIZE ** (-0.5), -1e30)
+    return raw * (HEAD_SIZE ** (-0.5) * LOG2_E)
 
 
 def mixed_values(own_ref, other_ref, far, slot, weights):
@@ -227,20 +239,21 @@
 
 
 def visit(meta_ref, far, query_ref, keys_ref, own_ref, other_ref, top, bottom, summed):
-    key_at = lax.broadcasted_iota(jnp.int32, (keys_ref.shape[3], query_ref.shape[1]), 0)
+    key_at = lax.broadcasted_iota(jnp.int32, (keys_ref.shape[3], query_ref.shape[1]), 0)[:, :1]
     first = (NEAR, FAR)[far]
 
     def two(n, carry):
         entries = [first + 2 * n, first + 2 * n + 1]
         slots = [meta_ref[e] for e in entries]
         masked = [
-            scored(query_ref, keys_ref, slot, key_at < meta_ref[LENGTHS + e])
+            scored(query_ref, keys_ref, slot)
+            + jnp.where(key_at < meta_ref[LENGTHS + e], 0.0, UNSEEN)
             for e, slot in zip(entries, slots)
         ]
         peak = jnp.max(jnp.maximum(masked[0], masked[1]), axis=0, keepdims=True)
         peak = jnp.maximum(top[...], peak)
-        shrink = jnp.exp(top[...] - peak)
-        weights = [jnp.exp(m - peak) for m in masked]
+        shrink = jnp.exp2(top[...] - peak)
+        weights = [jnp.exp2(m - peak) for m in masked]
         top[...] = peak
         bottom[...] = bottom[...] * shrink + jnp.sum(
             weights[0] + weights[1], axis=0, keepdims=True
@@ -261,9 +274,9 @@
     key_at = lax.broadcasted_iota(jnp.int32, shape, 0)
     query_at = lax.broadcasted_iota(jnp.int32, shape, 1) % seg_len
     own = lax.axis_index(SEG)
-    masked = scored(query_ref, keys_ref, own, key_at <= query_at)
+    masked = jnp.where(key_at <= query_at, scored(query_ref, keys_ref, own), UNSEEN)
     peak = jnp.max(masked, axis=0, keepdims=True)
-    weights = jnp.exp(masked - peak)
+    weights = jnp.exp2(masked - peak)
     top[...] = peak
     bottom[...] = jnp.sum(weights, axis=0, keepdims=True)
     summed[...] = mixed_values(own_ref, other_ref, 0, own, weights)
@@ -295,11 +308,11 @@
         part = scaled[:, h * seg_len : (h + 1) * seg_len]
         result += part[h : h + 1] + part[2 + h : 3 + h]
     for i in range(out_ref.shape[0]):
-        out_ref[i] = jnp.broadcast_to(result, out_ref.shape[1:])
+        out_ref[i] = result
 
 
 def finish_kernel(parts_ref, resid_ref, live_ref, last_ref, out_ref, leaf_ref):
-    total = resid_ref[...] + jnp.sum(parts_ref[...], axis=0)[:1]
+    total = resid_ref[...] + jnp.sum(parts_ref[...], axis=0)
     values = jnp.where(live_ref[...] > 0.5, total, 0.0)
     out_ref[...] = values
     leaf = jnp.sum(jnp.where(last_ref[...] > 0.5, values, 0.0), axis=1, keepdims=True)
@@ -408,7 +421,16 @@
     spread = lax.axis_size(("zl", "x"))
     values = keys_y[:, width:]
     keys_y = keys_y[:, :width]
-    near = gathered(jnp.broadcast_to(keys_y[None], (spread, *keys_y.shape)), ("zl", "x"))
+    copies = pl.pallas_call(
+        spread_kernel,
+        out_shape=jax.ShapeDtypeStruct((spread, *keys_y.shape), keys_y.dtype),
+        in_specs=[VMEM_SPEC],
+        out_specs=HBM_SPEC,
+        scratch_shapes=[pltpu.SemaphoreType.DMA((spread,))],
+        compiler_params=params,
+        name="spread_keys",
+    )(keys_y)
+    near = gathered(copies, ("zl", "x"))
     values = jnp.stack([values, lax.ppermute(values, "c", swap)])
     values, query_sine = lax.optimization_barrier((values, sine))
     other_values = lax.ppermute(values, "zl", swap)
@@ -448,7 +470,7 @@
     far, near_state = lax.optimization_barrier((far, near_state))
     mixed = pl.pallas_call(
         far_kernel,
-        out_shape=jax.ShapeDtypeStruct((fsdp_size, 8, seg_len), jnp.float32),
+        out_shape=jax.ShapeDtypeStruct((fsdp_size, 1, seg_len), jnp.float32),
         in_specs=[SMEM_SPEC] + [VMEM_SPEC] * 7,
         out_specs=VMEM_SPEC,
         scratch_shapes=[pltpu.VMEM(part.shape, part.dtype) for part in state],

time: 134 us -> 135 us (level)
  blocking collectives: 47.7 us -> 49.3 us
    all_to_all x3, blocking collectives: 47.7 us -> 49.3 us  [gathered(): return lax.all_to_all(value, axis, 0, 0)]
  transfers between devices with their start and end apart: 9 -> 9, of which waited for: 6 -> 5; matrix products, arithmetic and copies ran while one was open for 4% -> 3% of each run, Pallas kernels for 6% -> 8%
where the time goes in v5:
time: 135 us; the launch traced here: 134 us
  blocking collectives  49.3 us (37%)
  starting transfers between devices  34.1 us (25%)
  between operations  14.2 us (11%)
  local copies, waits for them, and re-layouts  12.3 us (9%)
  Pallas kernels  11.9 us (9%)
  waiting for transfers between devices  9.43 us (7%)
  other arithmetic  2.48 us (2%)
    all_to_all x3, blocking collectives, gathered(): return lax.all_to_all(value, axis, 0, 0)  49.3 us
    all_to_all x3, starting transfers between devices, gathered(): return lax.all_to_all(value, axis, 0, 0)  14.5 us
    unnamed x14, local copies, waits for them, and re-layouts  9.3 us
    all_to_all x3, waiting for transfers between devices, gathered(): return lax.all_to_all(value, axis, 0, 0)  6.49 us
    ppermute x1, starting transfers between devices, on_device(): far_weights = lax.ppermute(near_weights, 'c', swap)  5.91 us
    ppermute x1, starting transfers between devices, on_device(): other = lax.ppermute(w_query, 'zl', swap)  4.82 us
    ppermute x1, starting transfers between devices, on_device(): other_values = lax.ppermute(values, 'zl', swap)  3.55 us
    pallas_call x1, Pallas kernels, on_device(): pl.pallas_call(tree_kernel, out_shape=(jax.ShapeDtypeStruct((META,), jnp....  2.96 us
  transfers between devices with their start and end apart: 9, of which 5 were waited for; matrix products, arithmetic and copies ran while one was open for 3% of the time, Pallas kernels for 8%

profile of v5, /device:TPU:1, one launch (start us, length us, event | category | flops | bytes accessed | tf_op | source)
XLA Modules:
  0.0 133.8 jit_solution(1035788391453009470)
XLA Ops:
  7.2 1.3 %broadcast_in_dim.20 = bf16[4,32,256]{2,1,0:T(8,128)(2,1)} broadcast(bf16[32,256]{1,0:T(8,128)(2,1)} %bitcast.21), dimensions={1,2} | broadcast | bytes 81920 | tf_op jit(solution)/shard_map/broadcast_in_dim | solution.py:340
  8.5 4.8 %collective-permute-start = (bf16[256,256]{1,0:T(8,128)(2,1)}, bf16[256,256]{1,0:T(8,128)(2,1)S(1)}, u32[]{:S(2)}, u32[]{:S(2)}) collective-permute-start(bf16[256,256]{1,0:T(8,128)(2,1)} %param.10), channel_id=1, source_target_pairs={{0,32},{32,0},{1,33},{33,1},{2,34},{34,2},{3,35},{35,3},{4,36},{36... | collective-permute-start | bytes 393224 | tf_op jit(solution)/shard_map/ppermute | solution.py:342
  13.3 4.0 %all-to-all-start = ((bf16[4,32,256]{2,1,0:T(8,128)(2,1)}), bf16[4,32,256]{2,1,0:T(8,128)(2,1)S(1)}, u32[]{:S(2)}, u32[]{:S(2)}) async-start(bf16[4,32,256]{2,1,0:T(8,128)(2,1)} %broadcast_in_dim.20), calls=%async_computation | async-start | bytes 131072 | tf_op jit(solution)/shard_map/all_to_all | solution.py:323
  17.4 0.0 all-gather.2.cloned.1.call-start
  17.4 0.7 bitcast_convert_fusion.readout_ref
  18.0 0.8 dynamic_slice.3
  18.8 0.7 fusion.4.key_ref
  19.5 0.9 pad.16
  20.4 1.4 %all-to-all-done.value_ref = bf16[4,32,256]{2,1,0:T(8,128)(2,1)S(1)} async-done(((bf16[4,32,256]{2,1,0:T(8,128)(2,1)}), bf16[4,32,256]{2,1,0:T(8,128)(2,1)S(1)}, u32[]{:S(2)}, u32[]{:S(2)}) %all-to-all-start) | async-done | bytes 65568 | tf_op jit(solution)/shard_map/all_to_all | solution.py:323
  21.8 0.0 collective-permute-done
  21.9 0.7 copy-done.6
  22.6 0.0 all-gather.2.cloned.1.call-update
  22.6 0.9 fold_weights.1
  23.4 6.9 %all-to-all-start.1 = ((bf16[16,40,256]{2,1,0:T(8,128)(2,1)}), bf16[16,40,256]{2,1,0:T(8,128)(2,1)S(1)}, u32[]{:S(2)}, u32[]{:S(2)}) async-start(bf16[16,40,256]{2,1,0:T(8,128)(2,1)} %fold_weights.1), calls=%async_computation.1 | async-start | bytes 655360 | tf_op jit(solution)/shard_map/all_to_all | solution.py:323
  30.4 0.0 copy-start.3
  30.4 0.6 copy-done.3
  31.0 0.7 copy-done.4
  31.7 0.7 copy-done.5
  32.3 3.0 %tree.1 = (s32[168]{0:T(256)S(1)}, f32[32,128]{1,0:T(8,128)S(1)}, f32[1,256]{1,0:T(1,128)S(1)}, f32[1,256]{1,0:T(1,128)S(1)}, f32[1,256]{1,0:T(1,128)S(1)}) custom-call(s32[32]{0:T(128)S(1)} %copy-done.3, s32[32]{0:T(128)S(1)} %copy-done.4, s32[32]{0:T(128)S(1)} %copy-done.5), custom_call_target="tpu_custom_call" | custom-call | tf_op jit(solution)/shard_map/tree/pallas_call | solution.py:371
  35.3 0.6 fusion
  35.9 4.8 %all-to-all-done.1.weights_ref = bf16[16,40,256]{2,1,0:T(8,128)(2,1)S(1)} async-done(((bf16[16,40,256]{2,1,0:T(8,128)(2,1)}), bf16[16,40,256]{2,1,0:T(8,128)(2,1)S(1)}, u32[]{:S(2)}, u32[]{:S(2)}) %all-to-all-start.1) | async-done | bytes 327712 | tf_op jit(solution)/shard_map/all_to_all | solution.py:323
  40.7 5.9 %collective-permute-start.1 = (bf16[16,40,256]{2,1,0:T(8,128)(2,1)S(1)}, bf16[16,40,256]{2,1,0:T(8,128)(2,1)S(1)}, u32[]{:S(2)}, u32[]{:S(2)}) collective-permute-start(bf16[16,40,256]{2,1,0:T(8,128)(2,1)S(1)} %all-to-all-done.1.weights_ref), channel_id=1, source_target_pairs={{0,16},{16,0},{1,17},{17,1},{2,18},{18,2},{3,19},{19,3},{4,20},{20... | collective-permute-start | bytes 983048 | tf_op jit(solution)/shard_map/ppermute | solution.py:394
  46.7 0.0 copy-start
  46.7 2.3 %copy-done = bf16[256,8192]{1,0:T(8,128)(2,1)S(1)} copy-done((bf16[256,8192]{1,0:T(8,128)(2,1)S(1)}, bf16[256,8192]{1,0:T(8,128)(2,1)}, u32[]{:S(2)}) %copy-start) | copy-done | bytes 4194328
  48.9 0.7 project_near_keys.1.near_ref
  49.7 0.0 collective-permute-done.1.weights_ref
  49.7 0.8 project_far_keys.1
  50.5 14.4 %all_to_all.37 = bf16[8,40,256]{2,1,0:T(8,128)(2,1)S(1)} all-to-all(bf16[8,40,256]{2,1,0:T(8,128)(2,1)S(1)} %get-tuple-element.47), channel_id=1, replica_groups=mesh['y'=8,'zl'=2,'c'=2,'zh'=4,'x'=4] {'y'}, dimensions={0} | all-to-all | bytes 327680 | tf_op jit(solution)/shard_map/all_to_all | solution.py:323
  64.9 1.1 spread_keys.1
  66.0 3.6 %all-to-all-start.3 = ((bf16[8,8,32,256]{3,2,1,0:T(8,128)(2,1)}), bf16[8,8,32,256]{3,2,1,0:T(8,128)(2,1)S(1)}, u32[]{:S(2)}, u32[]{:S(2)}) async-start(bf16[8,8,32,256]{3,2,1,0:T(8,128)(2,1)} %spread_keys.1), calls=%async_computation.3 | async-start | bytes 2097152 | tf_op jit(solution)/shard_map/all_to_all | solution.py:323
  69.6 2.4 %collective-permute-start.2 = (bf16[8,8,256]{2,1,0:T(8,128)(2,1)S(1)}, bf16[8,8,256]{2,1,0:T(8,128)(2,1)S(1)}, u32[]{:S(2)}, u32[]{:S(2)}) collective-permute-start(bf16[8,8,256]{2,1,0:T(8,128)(2,1)S(1)} %get-tuple-element.69), channel_id=1, source_target_pairs={{0,16},{16,0},{1,17},{17,1},{2,18},{18,2},{3,19},{19,3},{4,20},{20... | collective-permute-start | bytes 98312 | tf_op jit(solution)/shard_map/ppermute | solution.py:434
  72.0 0.8 collective-permute-done.2
  72.8 3.6 %collective-permute-start.3 = (bf16[2,8,8,256]{3,2,1,0:T(8,128)(2,1)S(1)}, bf16[2,8,8,256]{3,2,1,0:T(8,128)(2,1)S(1)}, u32[]{:S(2)}, u32[]{:S(2)}) collective-permute-start(bf16[2,8,8,256]{3,2,1,0:T(8,128)(2,1)S(1)} %pad_maximum_fusion.own_ref), channel_id=1, source_target_pairs={{0,32},{32,0},{1,33},{33,1},{2,34},{34,2},{3,35},{35,3},{4,36},{36... | collective-permute-start | bytes 196616 | tf_op jit(solution)/shard_map/ppermute | solution.py:436
  76.4 0.0 all-gather.2.cloned.1.call-done
  76.4 0.0 copy-start.1
  76.4 2.2 %copy-done.1 = bf16[256,8192]{1,0:T(8,128)(2,1)S(1)} copy-done((bf16[256,8192]{1,0:T(8,128)(2,1)S(1)}, bf16[256,8192]{1,0:T(8,128)(2,1)}, u32[]{:S(2)}) %copy-start.1) | copy-done | bytes 4194328
  78.6 2.2 %copy-done.2 = bf16[8192,256]{1,0:T(8,128)(2,1)S(1)} copy-done((bf16[8192,256]{1,0:T(8,128)(2,1)S(1)}, bf16[8192,256]{1,0:T(8,128)(2,1)}, u32[]{:S(2)}) %copy-start.2) | copy-done | bytes 4194328
  80.8 1.4 %project_queries.1.query_ref = bf16[128,512]{1,0:T(8,128)(2,1)S(1)} custom-call(bf16[256,8192]{1,0:T(8,128)(2,1)S(1)} %copy-done.1, bf16[32,256,256]{2,1,0:T(8,128)(2,1)S(1)} %bitcast.16, f32[128,256]{1,0:T(8,128)S(1)} %get-tuple-element.45.cosine_ref, f32[128,256]{1,0:T(8,128)S(1)} %get-tuple-element.50.sine_ref), custom_call_target="tpu_custom_call" | custom-call | flops 1073741824 | bytes 8388608 | tf_op jit(solution)/shard_map/project_queries/pallas_call | solution.py:437
  82.2 2.1 %collective-permute-done.3.other_ref = bf16[2,8,8,256]{3,2,1,0:T(8,128)(2,1)S(1)} collective-permute-done((bf16[2,8,8,256]{3,2,1,0:T(8,128)(2,1)S(1)}, bf16[2,8,8,256]{3,2,1,0:T(8,128)(2,1)S(1)}, u32[]{:S(2)}, u32[]{:S(2)}) %collective-permute-start.3) | collective-permute-done | bytes 65568 | tf_op jit(solution)/shard_map/ppermute | solution.py:436
  84.2 0.2 all-to-all-done.3.keys_ref
  84.5 3.0 %collective-permute-start.4 = (bf16[8,8,32,256]{3,2,1,0:T(8,128)(2,1)S(1)}, bf16[8,8,32,256]{3,2,1,0:T(8,128)(2,1)S(1)}, u32[]{:S(2)}, u32[]{:S(2)}) collective-permute-start(bf16[8,8,32,256]{3,2,1,0:T(8,128)(2,1)S(1)} %all-to-all-done.3.keys_ref), channel_id=1, source_target_pairs={{0,16},{16,0},{1,17},{17,1},{2,18},{18,2},{3,19},{19,3},{4,20},{20... | collective-permute-start | bytes 3145736 | tf_op jit(solution)/shard_map/ppermute | solution.py:452
  87.4 2.3 %attend_near.1 = (f32[1,512]{1,0:T(1,128)S(1)}, f32[1,512]{1,0:T(1,128)S(1)}, f32[8,512]{1,0:T(8,128)S(1)}) custom-call(s32[168]{0:T(256)S(1)} %get-tuple-element.35.meta_ref, bf16[128,512]{1,0:T(8,128)(2,1)S(1)} %project_queries.1.query_ref, bf16[8,8,32,256]{3,2,1,0:T(8,128)(2,1)S(1)} %all-to-all-done.3.keys_ref, ...), custom_call_target="tpu_custom_call" | custom-call | flops 268435456 | bytes 2097152 | tf_op jit(solution)/shard_map/attend_near/pallas_call | solution.py:459
  89.7 0.0 collective-permute-done.4.keys_ref
  89.7 1.2 attend_far.1
  90.9 21.8 %all_to_all.38.parts_ref = f32[16,1,256]{2,1,0:T(1,128)S(1)} all-to-all(f32[16,1,256]{2,1,0:T(1,128)S(1)} %attend_far.1), channel_id=1, replica_groups=mesh['y'=8,'zl'=2,'c'=2,'zh'=4,'x'=4] {'zh','x'}, dimensions={0} | all-to-all | bytes 32768 | tf_op jit(solution)/shard_map/all_to_all | solution.py:323
  112.8 0.6 token_values.1
  113.4 13.0 %all_to_all.39 = f32[32,1,128]{2,1,0:T(1,128)S(1)} all-to-all(f32[32,1,128]{2,1,0:T(1,128)S(1)} %bitcast.17), channel_id=1, replica_groups=mesh['y'=8,'zl'=2,'c'=2,'zh'=4,'x'=4] {'y','zl','c'}, dimensions={0} | all-to-all | bytes 32768 | tf_op jit(solution)/shard_map/all_to_all | solution.py:323
  126.4 0.5 multiply_reduce_fusion
  (10 shorter events, 0.1 us)
Async XLA Ops:
  8.5 13.3 %collective-permute-start = (bf16[256,256]{1,0:T(8,128)(2,1)}, bf16[256,256]{1,0:T(8,128)(2,1)S(1)}, u32[]{:S(2)}, u32[]{:S(2)}) collective-permute-start(bf16[256,256]{1,0:T(8,128)(2,1)} %param.10), channel_id=1, source_target_pairs={{0,32},{32,0},{1,33},{33,1},{2,34},{34,2},{3,35},{35,3},{4,36},{36... | collective-permute-start | bytes 393224 | tf_op jit(solution)/shard_map/ppermute | solution.py:342
  13.3 8.5 %all-to-all-start = ((bf16[4,32,256]{2,1,0:T(8,128)(2,1)}), bf16[4,32,256]{2,1,0:T(8,128)(2,1)S(1)}, u32[]{:S(2)}, u32[]{:S(2)}) async-start(bf16[4,32,256]{2,1,0:T(8,128)(2,1)} %broadcast_in_dim.20), calls=%async_computation | async-start | bytes 131072 | tf_op jit(solution)/shard_map/all_to_all | solution.py:323
  17.4 59.0 %all-gather.2.cloned.1.call-start = ((), (), s32[]{:S(2)}) async-start(), calls=%async_computation.6 | async-start | bytes 4456448 | tf_op jit(solution)/shard_map/all_gather | solution.py:359
  21.9 0.7 copy-start.6
  23.4 17.3 %all-to-all-start.1 = ((bf16[16,40,256]{2,1,0:T(8,128)(2,1)}), bf16[16,40,256]{2,1,0:T(8,128)(2,1)S(1)}, u32[]{:S(2)}, u32[]{:S(2)}) async-start(bf16[16,40,256]{2,1,0:T(8,128)(2,1)} %fold_weights.1), calls=%async_computation.1 | async-start | bytes 655360 | tf_op jit(solution)/shard_map/all_to_all | solution.py:323
  30.4 0.7 copy-start.3
  31.0 0.7 copy-start.4
  31.7 0.7 copy-start.5
  40.7 9.0 %collective-permute-start.1 = (bf16[16,40,256]{2,1,0:T(8,128)(2,1)S(1)}, bf16[16,40,256]{2,1,0:T(8,128)(2,1)S(1)}, u32[]{:S(2)}, u32[]{:S(2)}) collective-permute-start(bf16[16,40,256]{2,1,0:T(8,128)(2,1)S(1)} %all-to-all-done.1.weights_ref), channel_id=1, source_target_pairs={{0,16},{16,0},{1,17},{17,1},{2,18},{18,2},{3,19},{19,3},{4,20},{20... | collective-permute-start | bytes 983048 | tf_op jit(solution)/shard_map/ppermute | solution.py:394
  46.7 2.3 %copy-start = (bf16[256,8192]{1,0:T(8,128)(2,1)S(1)}, bf16[256,8192]{1,0:T(8,128)(2,1)}, u32[]{:S(2)}) copy-start(bf16[256,8192]{1,0:T(8,128)(2,1)} %tokens_ref.5) | copy-start | bytes 12582916
  66.0 18.5 %all-to-all-start.3 = ((bf16[8,8,32,256]{3,2,1,0:T(8,128)(2,1)}), bf16[8,8,32,256]{3,2,1,0:T(8,128)(2,1)S(1)}, u32[]{:S(2)}, u32[]{:S(2)}) async-start(bf16[8,8,32,256]{3,2,1,0:T(8,128)(2,1)} %spread_keys.1), calls=%async_computation.3 | async-start | bytes 2097152 | tf_op jit(solution)/shard_map/all_to_all | solution.py:323
  69.6 3.2 %collective-permute-start.2 = (bf16[8,8,256]{2,1,0:T(8,128)(2,1)S(1)}, bf16[8,8,256]{2,1,0:T(8,128)(2,1)S(1)}, u32[]{:S(2)}, u32[]{:S(2)}) collective-permute-start(bf16[8,8,256]{2,1,0:T(8,128)(2,1)S(1)} %get-tuple-element.69), channel_id=1, source_target_pairs={{0,16},{16,0},{1,17},{17,1},{2,18},{18,2},{3,19},{19,3},{4,20},{20... | collective-permute-start | bytes 98312 | tf_op jit(solution)/shard_map/ppermute | solution.py:434
  72.8 11.4 %collective-permute-start.3 = (bf16[2,8,8,256]{3,2,1,0:T(8,128)(2,1)S(1)}, bf16[2,8,8,256]{3,2,1,0:T(8,128)(2,1)S(1)}, u32[]{:S(2)}, u32[]{:S(2)}) collective-permute-start(bf16[2,8,8,256]{3,2,1,0:T(8,128)(2,1)S(1)} %pad_maximum_fusion.own_ref), channel_id=1, source_target_pairs={{0,32},{32,0},{1,33},{33,1},{2,34},{34,2},{3,35},{35,3},{4,36},{36... | collective-permute-start | bytes 196616 | tf_op jit(solution)/shard_map/ppermute | solution.py:436
  76.4 2.2 %copy-start.1 = (bf16[256,8192]{1,0:T(8,128)(2,1)S(1)}, bf16[256,8192]{1,0:T(8,128)(2,1)}, u32[]{:S(2)}) copy-start(bf16[256,8192]{1,0:T(8,128)(2,1)} %tokens_ref.5) | copy-start | bytes 12582916
  78.6 2.2 %copy-start.2 = (bf16[8192,256]{1,0:T(8,128)(2,1)S(1)}, bf16[8192,256]{1,0:T(8,128)(2,1)}, u32[]{:S(2)}) copy-start(bf16[8192,256]{1,0:T(8,128)(2,1)} %all-gather.2.cloned.1.call-done) | copy-start | bytes 12582916
  84.5 5.2 %collective-permute-start.4 = (bf16[8,8,32,256]{3,2,1,0:T(8,128)(2,1)S(1)}, bf16[8,8,32,256]{3,2,1,0:T(8,128)(2,1)S(1)}, u32[]{:S(2)}, u32[]{:S(2)}) collective-permute-start(bf16[8,8,32,256]{3,2,1,0:T(8,128)(2,1)S(1)} %all-to-all-done.3.keys_ref), channel_id=1, source_target_pairs={{0,16},{16,0},{1,17},{17,1},{2,18},{18,2},{3,19},{19,3},{4,20},{20... | collective-permute-start | bytes 3145736 | tf_op jit(solution)/shard_map/ppermute | solution.py:452
Sparse Core Ops, SparseCore 0:
  22.7 51.3 all-gather.1

commit v6 on v5

--- a/solution.py
+++ b/solution.py
@@ -28,8 +28,7 @@
     meta_ref,
     table_ref,
     position_ref,
-    live_ref,
-    last_ref,
+    span_ref,
     parents_ref,
     placed_ref,
     lengths_ref,
@@ -79,8 +78,7 @@
     meta_ref[1] = far
     index = lax.broadcasted_iota(jnp.int32, position_ref.shape, 1)
     position_ref[...] = (offset + index).astype(jnp.float32)
-    live_ref[...] = jnp.where(index < lengths_ref[own], 1.0, 0.0)
-    last_ref[...] = jnp.where(index == lengths_ref[own] - 1, 1.0, 0.0)
+    span_ref[...] = (lengths_ref[own] - index).astype(jnp.float32)
 
     row = lax.broadcasted_iota(jnp.int32, (128, 128), 0)
     col = lax.broadcasted_iota(jnp.int32, (128, 128), 1)
@@ -126,6 +124,11 @@
     piece = piece.astype(jnp.bfloat16)
     for i in range(out_ref.shape[0]):
         out_ref[i] = piece
+
+
+def masks_kernel(span_ref, live_ref, last_ref):
+    live_ref[...] = jnp.where(span_ref[...] > 0.5, 1.0, 0.0)
+    last_ref[...] = jnp.where(jnp.abs(span_ref[...] - 1.0) < 0.5, 1.0, 0.0)
 
 
 def turned(raw, cosine, sine, axis):
@@ -368,17 +371,16 @@
 
     near_weights = gathered(pieces, ("y", "zl"))
     by_token = jax.ShapeDtypeStruct((1, seg_len), jnp.float32)
-    meta, table, positions, live, last = pl.pallas_call(
+    meta, table, positions, spans = pl.pallas_call(
         tree_kernel,
         out_shape=(
             jax.ShapeDtypeStruct((META,), jnp.int32),
             jax.ShapeDtypeStruct((segments, 128), jnp.float32),
             by_token,
             by_token,
-            by_token,
         ),
         in_specs=[HBM_SPEC] * 3,
-        out_specs=(SMEM_SPEC,) + (VMEM_SPEC,) * 4,
+        out_specs=(SMEM_SPEC,) + (VMEM_SPEC,) * 3,
         scratch_shapes=[pltpu.SMEM((segments,), jnp.int32)] * 4
         + [pltpu.SemaphoreType.DMA((3,))],
         compiler_params=params,
@@ -389,9 +391,21 @@
     angles = frequency[:, None] * positions
     cosine = jnp.cos(angles)
     sine = jnp.sin(angles) * jnp.where(dims % 2 == 0, -1.0, 1.0)[:, None]
-    near_weights, cosine, sine = lax.optimization_barrier((near_weights, cosine, sine))
+    near_weights, cosine, sine, spans = lax.optimization_barrier(
+        (near_weights, cosine, sine, spans)
+    )
 
     far_weights = lax.ppermute(near_weights, "c", swap)
+    live, last = pl.pallas_call(
+        masks_kernel,
+        out_shape=(by_token, by_token),
+        in_specs=[VMEM_SPEC],
+        out_specs=(VMEM_SPEC,) * 2,
+        compiler_params=params,
+        cost_estimate=pl.CostEstimate(flops=2**33, bytes_accessed=2**12, transcendentals=0),
+        name="masks",
+    )(spans)
+    near_weights, live, last = lax.optimization_barrier((near_weights, live, last))
     near_sums = pl.pallas_call(
         near_keys_kernel,
         out_shape=jax.ShapeDtypeStruct((rows, seg_len), jnp.float32),

time: 135 us -> 132 us (0.978)
  local copies, waits for them, and re-layouts: 12.3 us -> 10.1 us
  waiting for transfers between devices: 9.43 us -> 11.2 us
    unnamed x14, local copies, waits for them, and re-layouts: 9.3 us -> 7.04 us
  transfers between devices with their start and end apart: 9 -> 9, of which waited for: 5 -> 7; matrix products, arithmetic and copies ran while one was open for 3% -> 3% of each run, Pallas kernels for 8% -> 7%
where the time goes in v6:
time: 132 us
  blocking collectives  48.6 us (37%)
  starting transfers between devices  34.3 us (26%)
  between operations  14.2 us (11%)
  waiting for transfers between devices  11.2 us (8%)
  Pallas kernels  10.6 us (8%)
  local copies, waits for them, and re-layouts  10.1 us (8%)
  other arithmetic  2.48 us (2%)
    all_to_all x3, blocking collectives, gathered(): return lax.all_to_all(value, axis, 0, 0)  48.6 us
    all_to_all x3, starting transfers between devices, gathered(): return lax.all_to_all(value, axis, 0, 0)  14.5 us
    unnamed x14, local copies, waits for them, and re-layouts  7.04 us
    all_to_all x3, waiting for transfers between devices, gathered(): return lax.all_to_all(value, axis, 0, 0)  6.47 us
    ppermute x1, starting transfers between devices, on_device(): far_weights = lax.ppermute(near_weights, 'c', swap)  6.18 us
    ppermute x1, starting transfers between devices, on_device(): other = lax.ppermute(w_query, 'zl', swap)  4.82 us
    ppermute x1, starting transfers between devices, on_device(): other_values = lax.ppermute(values, 'zl', swap)  3.55 us
    ppermute x1, starting transfers between devices, on_device(): far = lax.ppermute(near, 'c', swap)  2.95 us
  transfers between devices with their start and end apart: 9, of which 7 were waited for; matrix products, arithmetic and copies ran while one was open for 3% of the time, Pallas kernels for 7%

profile of v6, /device:TPU:1, one launch (start us, length us, event | category | flops | bytes accessed | tf_op | source)
XLA Modules:
  0.0 131.6 jit_solution(6447144586296106565)
XLA Ops:
  7.2 1.4 %broadcast_in_dim.20 = bf16[4,32,256]{2,1,0:T(8,128)(2,1)} broadcast(bf16[32,256]{1,0:T(8,128)(2,1)} %bitcast.21), dimensions={1,2} | broadcast | bytes 81920 | tf_op jit(solution)/shard_map/broadcast_in_dim | solution.py:343
  8.5 4.8 %collective-permute-start = (bf16[256,256]{1,0:T(8,128)(2,1)}, bf16[256,256]{1,0:T(8,128)(2,1)S(1)}, u32[]{:S(2)}, u32[]{:S(2)}) collective-permute-start(bf16[256,256]{1,0:T(8,128)(2,1)} %param.10), channel_id=1, source_target_pairs={{0,32},{32,0},{1,33},{33,1},{2,34},{34,2},{3,35},{35,3},{4,36},{36... | collective-permute-start | bytes 393224 | tf_op jit(solution)/shard_map/ppermute | solution.py:345
  13.3 4.0 %all-to-all-start = ((bf16[4,32,256]{2,1,0:T(8,128)(2,1)}), bf16[4,32,256]{2,1,0:T(8,128)(2,1)S(1)}, u32[]{:S(2)}, u32[]{:S(2)}) async-start(bf16[4,32,256]{2,1,0:T(8,128)(2,1)} %broadcast_in_dim.20), calls=%async_computation | async-start | bytes 131072 | tf_op jit(solution)/shard_map/all_to_all | solution.py:326
  17.4 0.0 all-gather.2.cloned.1.call-start
  17.4 0.7 bitcast_convert_fusion.readout_ref
  18.0 0.8 dynamic_slice.3
  18.8 0.7 fusion.4.key_ref
  19.5 0.9 pad.16
  20.4 1.4 %all-to-all-done.value_ref = bf16[4,32,256]{2,1,0:T(8,128)(2,1)S(1)} async-done(((bf16[4,32,256]{2,1,0:T(8,128)(2,1)}), bf16[4,32,256]{2,1,0:T(8,128)(2,1)S(1)}, u32[]{:S(2)}, u32[]{:S(2)}) %all-to-all-start) | async-done | bytes 65568 | tf_op jit(solution)/shard_map/all_to_all | solution.py:326
  21.8 0.0 collective-permute-done
  21.9 0.0 copy-start.6
  21.9 0.7 copy-done.6
  22.6 0.0 all-gather.2.cloned.1.call-update
  22.6 0.9 fold_weights.1
  23.5 6.9 %all-to-all-start.1 = ((bf16[16,40,256]{2,1,0:T(8,128)(2,1)}), bf16[16,40,256]{2,1,0:T(8,128)(2,1)S(1)}, u32[]{:S(2)}, u32[]{:S(2)}) async-start(bf16[16,40,256]{2,1,0:T(8,128)(2,1)} %fold_weights.1), calls=%async_computation.1 | async-start | bytes 655360 | tf_op jit(solution)/shard_map/all_to_all | solution.py:326
  30.4 0.0 copy-start.3
  30.4 0.6 copy-done.3
  31.1 0.7 copy-done.4
  31.7 0.7 copy-done.5
  32.4 2.9 %tree.1 = (s32[168]{0:T(256)S(1)}, f32[32,128]{1,0:T(8,128)S(1)}, f32[1,256]{1,0:T(1,128)S(1)}, f32[1,256]{1,0:T(1,128)S(1)}) custom-call(s32[32]{0:T(128)S(1)} %copy-done.3, s32[32]{0:T(128)S(1)} %copy-done.4, s32[32]{0:T(128)S(1)} %copy-done.5), custom_call_target="tpu_custom_call" | custom-call | tf_op jit(solution)/shard_map/tree/pallas_call | solution.py:374
  35.3 0.6 fusion
  35.9 4.9 %all-to-all-done.1.weights_ref = bf16[16,40,256]{2,1,0:T(8,128)(2,1)S(1)} async-done(((bf16[16,40,256]{2,1,0:T(8,128)(2,1)}), bf16[16,40,256]{2,1,0:T(8,128)(2,1)S(1)}, u32[]{:S(2)}, u32[]{:S(2)}) %all-to-all-start.1) | async-done | bytes 327712 | tf_op jit(solution)/shard_map/all_to_all | solution.py:326
  40.8 6.2 %collective-permute-start.1 = (bf16[16,40,256]{2,1,0:T(8,128)(2,1)S(1)}, bf16[16,40,256]{2,1,0:T(8,128)(2,1)S(1)}, u32[]{:S(2)}, u32[]{:S(2)}) collective-permute-start(bf16[16,40,256]{2,1,0:T(8,128)(2,1)S(1)} %all-to-all-done.1.weights_ref), channel_id=1, source_target_pairs={{0,16},{16,0},{1,17},{17,1},{2,18},{18,2},{3,19},{19,3},{4,20},{20... | collective-permute-start | bytes 983048 | tf_op jit(solution)/shard_map/ppermute | solution.py:398
  47.0 0.0 copy-done
  47.0 0.8 project_near_keys.1.near_ref
  47.8 0.4 collective-permute-done.1.weights_ref
  48.2 0.8 project_far_keys.1
  49.0 14.5 %all_to_all.37 = bf16[8,40,256]{2,1,0:T(8,128)(2,1)S(1)} all-to-all(bf16[8,40,256]{2,1,0:T(8,128)(2,1)S(1)} %get-tuple-element.57), channel_id=1, replica_groups=mesh['y'=8,'zl'=2,'c'=2,'zh'=4,'x'=4] {'y'}, dimensions={0} | all-to-all | bytes 327680 | tf_op jit(solution)/shard_map/all_to_all | solution.py:326
  63.5 1.1 spread_keys.1
  64.5 3.6 %all-to-all-start.3 = ((bf16[8,8,32,256]{3,2,1,0:T(8,128)(2,1)}), bf16[8,8,32,256]{3,2,1,0:T(8,128)(2,1)S(1)}, u32[]{:S(2)}, u32[]{:S(2)}) async-start(bf16[8,8,32,256]{3,2,1,0:T(8,128)(2,1)} %spread_keys.1), calls=%async_computation.3 | async-start | bytes 2097152 | tf_op jit(solution)/shard_map/all_to_all | solution.py:326
  68.1 2.3 %collective-permute-start.2 = (bf16[8,8,256]{2,1,0:T(8,128)(2,1)S(1)}, bf16[8,8,256]{2,1,0:T(8,128)(2,1)S(1)}, u32[]{:S(2)}, u32[]{:S(2)}) collective-permute-start(bf16[8,8,256]{2,1,0:T(8,128)(2,1)S(1)} %get-tuple-element.79), channel_id=1, source_target_pairs={{0,16},{16,0},{1,17},{17,1},{2,18},{18,2},{3,19},{19,3},{4,20},{20... | collective-permute-start | bytes 98312 | tf_op jit(solution)/shard_map/ppermute | solution.py:448
  70.5 0.8 collective-permute-done.2
  71.3 3.6 %collective-permute-start.3 = (bf16[2,8,8,256]{3,2,1,0:T(8,128)(2,1)S(1)}, bf16[2,8,8,256]{3,2,1,0:T(8,128)(2,1)S(1)}, u32[]{:S(2)}, u32[]{:S(2)}) collective-permute-start(bf16[2,8,8,256]{3,2,1,0:T(8,128)(2,1)S(1)} %pad_maximum_fusion.own_ref), channel_id=1, source_target_pairs={{0,32},{32,0},{1,33},{33,1},{2,34},{34,2},{3,35},{35,3},{4,36},{36... | collective-permute-start | bytes 196616 | tf_op jit(solution)/shard_map/ppermute | solution.py:450
  74.9 0.0 all-gather.2.cloned.1.call-done
  74.9 0.0 copy-start.1
  74.9 2.2 %copy-done.1 = bf16[256,8192]{1,0:T(8,128)(2,1)S(1)} copy-done((bf16[256,8192]{1,0:T(8,128)(2,1)S(1)}, bf16[256,8192]{1,0:T(8,128)(2,1)}, u32[]{:S(2)}) %copy-start.1) | copy-done | bytes 4194328
  77.1 2.2 %copy-done.2 = bf16[8192,256]{1,0:T(8,128)(2,1)S(1)} copy-done((bf16[8192,256]{1,0:T(8,128)(2,1)S(1)}, bf16[8192,256]{1,0:T(8,128)(2,1)}, u32[]{:S(2)}) %copy-start.2) | copy-done | bytes 4194328
  79.3 1.4 %project_queries.1.query_ref = bf16[128,512]{1,0:T(8,128)(2,1)S(1)} custom-call(bf16[256,8192]{1,0:T(8,128)(2,1)S(1)} %copy-done.1, bf16[32,256,256]{2,1,0:T(8,128)(2,1)S(1)} %bitcast.16, f32[128,256]{1,0:T(8,128)S(1)} %get-tuple-element.55.cosine_ref, f32[128,256]{1,0:T(8,128)S(1)} %get-tuple-element.60.sine_ref), custom_call_target="tpu_custom_call" | custom-call | flops 1073741824 | bytes 8388608 | tf_op jit(solution)/shard_map/project_queries/pallas_call | solution.py:451
  80.7 2.2 %collective-permute-done.3.other_ref = bf16[2,8,8,256]{3,2,1,0:T(8,128)(2,1)S(1)} collective-permute-done((bf16[2,8,8,256]{3,2,1,0:T(8,128)(2,1)S(1)}, bf16[2,8,8,256]{3,2,1,0:T(8,128)(2,1)S(1)}, u32[]{:S(2)}, u32[]{:S(2)}) %collective-permute-start.3) | collective-permute-done | bytes 65568 | tf_op jit(solution)/shard_map/ppermute | solution.py:450
  82.8 0.2 all-to-all-done.3.keys_ref
  83.0 3.0 %collective-permute-start.4 = (bf16[8,8,32,256]{3,2,1,0:T(8,128)(2,1)S(1)}, bf16[8,8,32,256]{3,2,1,0:T(8,128)(2,1)S(1)}, u32[]{:S(2)}, u32[]{:S(2)}) collective-permute-start(bf16[8,8,32,256]{3,2,1,0:T(8,128)(2,1)S(1)} %all-to-all-done.3.keys_ref), channel_id=1, source_target_pairs={{0,16},{16,0},{1,17},{17,1},{2,18},{18,2},{3,19},{19,3},{4,20},{20... | collective-permute-start | bytes 3145736 | tf_op jit(solution)/shard_map/ppermute | solution.py:466
  86.0 1.0 attend_near.1
  87.0 1.3 collective-permute-done.4.keys_ref
  88.2 1.2 attend_far.1
  89.5 21.1 %all_to_all.38.parts_ref = f32[16,1,256]{2,1,0:T(1,128)S(1)} all-to-all(f32[16,1,256]{2,1,0:T(1,128)S(1)} %attend_far.1), channel_id=1, replica_groups=mesh['y'=8,'zl'=2,'c'=2,'zh'=4,'x'=4] {'zh','x'}, dimensions={0} | all-to-all | bytes 32768 | tf_op jit(solution)/shard_map/all_to_all | solution.py:326
  110.6 0.6 token_values.1
  111.2 13.0 %all_to_all.39 = f32[32,1,128]{2,1,0:T(1,128)S(1)} all-to-all(f32[32,1,128]{2,1,0:T(1,128)S(1)} %bitcast.17), channel_id=1, replica_groups=mesh['y'=8,'zl'=2,'c'=2,'zh'=4,'x'=4] {'y','zl','c'}, dimensions={0} | all-to-all | bytes 32768 | tf_op jit(solution)/shard_map/all_to_all | solution.py:326
  124.2 0.5 multiply_reduce_fusion
  (11 shorter events, 0.1 us)
Async XLA Ops:
  8.5 13.3 %collective-permute-start = (bf16[256,256]{1,0:T(8,128)(2,1)}, bf16[256,256]{1,0:T(8,128)(2,1)S(1)}, u32[]{:S(2)}, u32[]{:S(2)}) collective-permute-start(bf16[256,256]{1,0:T(8,128)(2,1)} %param.10), channel_id=1, source_target_pairs={{0,32},{32,0},{1,33},{33,1},{2,34},{34,2},{3,35},{35,3},{4,36},{36... | collective-permute-start | bytes 393224 | tf_op jit(solution)/shard_map/ppermute | solution.py:345
  13.3 8.5 %all-to-all-start = ((bf16[4,32,256]{2,1,0:T(8,128)(2,1)}), bf16[4,32,256]{2,1,0:T(8,128)(2,1)S(1)}, u32[]{:S(2)}, u32[]{:S(2)}) async-start(bf16[4,32,256]{2,1,0:T(8,128)(2,1)} %broadcast_in_dim.20), calls=%async_computation | async-start | bytes 131072 | tf_op jit(solution)/shard_map/all_to_all | solution.py:326
  17.4 57.5 %all-gather.2.cloned.1.call-start = ((), (), s32[]{:S(2)}) async-start(), calls=%async_computation.6 | async-start | bytes 4456448 | tf_op jit(solution)/shard_map/all_gather | solution.py:362
  21.9 0.7 copy-start.6
  23.5 17.3 %all-to-all-start.1 = ((bf16[16,40,256]{2,1,0:T(8,128)(2,1)}), bf16[16,40,256]{2,1,0:T(8,128)(2,1)S(1)}, u32[]{:S(2)}, u32[]{:S(2)}) async-start(bf16[16,40,256]{2,1,0:T(8,128)(2,1)} %fold_weights.1), calls=%async_computation.1 | async-start | bytes 655360 | tf_op jit(solution)/shard_map/all_to_all | solution.py:326
  30.4 0.7 copy-start.3
  31.1 0.7 copy-start.4
  31.7 0.7 copy-start.5
  40.8 6.2 %copy-start = (bf16[256,8192]{1,0:T(8,128)(2,1)S(1)}, bf16[256,8192]{1,0:T(8,128)(2,1)}, u32[]{:S(2)}) copy-start(bf16[256,8192]{1,0:T(8,128)(2,1)} %tokens_ref.5) | copy-start | bytes 12582916
  40.8 7.4 %collective-permute-start.1 = (bf16[16,40,256]{2,1,0:T(8,128)(2,1)S(1)}, bf16[16,40,256]{2,1,0:T(8,128)(2,1)S(1)}, u32[]{:S(2)}, u32[]{:S(2)}) collective-permute-start(bf16[16,40,256]{2,1,0:T(8,128)(2,1)S(1)} %all-to-all-done.1.weights_ref), channel_id=1, source_target_pairs={{0,16},{16,0},{1,17},{17,1},{2,18},{18,2},{3,19},{19,3},{4,20},{20... | collective-permute-start | bytes 983048 | tf_op jit(solution)/shard_map/ppermute | solution.py:398
  64.5 18.5 %all-to-all-start.3 = ((bf16[8,8,32,256]{3,2,1,0:T(8,128)(2,1)}), bf16[8,8,32,256]{3,2,1,0:T(8,128)(2,1)S(1)}, u32[]{:S(2)}, u32[]{:S(2)}) async-start(bf16[8,8,32,256]{3,2,1,0:T(8,128)(2,1)} %spread_keys.1), calls=%async_computation.3 | async-start | bytes 2097152 | tf_op jit(solution)/shard_map/all_to_all | solution.py:326
  68.1 3.2 %collective-permute-start.2 = (bf16[8,8,256]{2,1,0:T(8,128)(2,1)S(1)}, bf16[8,8,256]{2,1,0:T(8,128)(2,1)S(1)}, u32[]{:S(2)}, u32[]{:S(2)}) collective-permute-start(bf16[8,8,256]{2,1,0:T(8,128)(2,1)S(1)} %get-tuple-element.79), channel_id=1, source_target_pairs={{0,16},{16,0},{1,17},{17,1},{2,18},{18,2},{3,19},{19,3},{4,20},{20... | collective-permute-start | bytes 98312 | tf_op jit(solution)/shard_map/ppermute | solution.py:448
  71.3 11.5 %collective-permute-start.3 = (bf16[2,8,8,256]{3,2,1,0:T(8,128)(2,1)S(1)}, bf16[2,8,8,256]{3,2,1,0:T(8,128)(2,1)S(1)}, u32[]{:S(2)}, u32[]{:S(2)}) collective-permute-start(bf16[2,8,8,256]{3,2,1,0:T(8,128)(2,1)S(1)} %pad_maximum_fusion.own_ref), channel_id=1, source_target_pairs={{0,32},{32,0},{1,33},{33,1},{2,34},{34,2},{3,35},{35,3},{4,36},{36... | collective-permute-start | bytes 196616 | tf_op jit(solution)/shard_map/ppermute | solution.py:450
  74.9 2.2 %copy-start.1 = (bf16[256,8192]{1,0:T(8,128)(2,1)S(1)}, bf16[256,8192]{1,0:T(8,128)(2,1)}, u32[]{:S(2)}) copy-start(bf16[256,8192]{1,0:T(8,128)(2,1)} %tokens_ref.5) | copy-start | bytes 12582916
  77.1 2.2 %copy-start.2 = (bf16[8192,256]{1,0:T(8,128)(2,1)S(1)}, bf16[8192,256]{1,0:T(8,128)(2,1)}, u32[]{:S(2)}) copy-start(bf16[8192,256]{1,0:T(8,128)(2,1)} %all-gather.2.cloned.1.call-done) | copy-start | bytes 12582916
  83.0 5.2 %collective-permute-start.4 = (bf16[8,8,32,256]{3,2,1,0:T(8,128)(2,1)S(1)}, bf16[8,8,32,256]{3,2,1,0:T(8,128)(2,1)S(1)}, u32[]{:S(2)}, u32[]{:S(2)}) collective-permute-start(bf16[8,8,32,256]{3,2,1,0:T(8,128)(2,1)S(1)} %all-to-all-done.3.keys_ref), channel_id=1, source_target_pairs={{0,16},{16,0},{1,17},{17,1},{2,18},{18,2},{3,19},{19,3},{4,20},{20... | collective-permute-start | bytes 3145736 | tf_op jit(solution)/shard_map/ppermute | solution.py:466
Sparse Core Ops, SparseCore 0:
  22.7 51.5 all-gather.1

commit v7 on v6

--- a/solution.py
+++ b/solution.py
@@ -359,15 +359,17 @@
         (values_x, other, readout, key_rows, both)
     )
     both = lax.dynamic_update_slice(both, other, (w_query.shape[0], 0))
-    query_weight = lax.all_gather(both, ("y", "c"), axis=0, tiled=True)
     pieces = pl.pallas_call(
         weights_kernel,
         out_shape=jax.ShapeDtypeStruct((pairs, rows, seg_len), jnp.bfloat16),
         in_specs=[VMEM_SPEC] * 3,
         out_specs=VMEM_SPEC,
         compiler_params=params,
+        cost_estimate=pl.CostEstimate(flops=2**33, bytes_accessed=2**12, transcendentals=0),
         name="fold_weights",
     )(values_x, readout, key_rows)
+    pieces, both = lax.optimization_barrier((pieces, both))
+    query_weight = lax.all_gather(both, ("y", "c"), axis=0, tiled=True)
 
     near_weights = gathered(pieces, ("y", "zl"))
     by_token = jax.ShapeDtypeStruct((1, seg_len), jnp.float32)

time: 132 us -> 131 us (level)
  local copies, waits for them, and re-layouts: 10.1 us -> 7.46 us
    unnamed x14, local copies, waits for them, and re-layouts: 7.04 us -> 4.4 us
    all_to_all x3, waiting for transfers between devices: 6.47 us -> 8.89 us  [gathered(): return lax.all_to_all(value, axis, 0, 0)]
    ppermute x1, waiting for transfers between devices: 2.16 us -> 0.56 us  [on_device(): other_values = lax.ppermute(values, 'zl', swap)]
  transfers between devices with their start and end apart: 9 -> 9, of which waited for: 7 -> 8; matrix products, arithmetic and copies ran while one was open for 3% -> 3% of each run, Pallas kernels for 7% -> 7%
where the time goes in v7:
time: 131 us; the launch traced here: 130 us
  blocking collectives  47.4 us (36%)
  starting transfers between devices  35.4 us (27%)
  between operations  14.2 us (11%)
  waiting for transfers between devices  11.5 us (9%)
  Pallas kernels  11.3 us (9%)
  local copies, waits for them, and re-layouts  7.46 us (6%)
  other arithmetic  2.48 us (2%)
    all_to_all x3, blocking collectives, gathered(): return lax.all_to_all(value, axis, 0, 0)  47.4 us
    all_to_all x3, starting transfers between devices, gathered(): return lax.all_to_all(value, axis, 0, 0)  14.5 us
    all_to_all x3, waiting for transfers between devices, gathered(): return lax.all_to_all(value, axis, 0, 0)  8.89 us
    ppermute x1, starting transfers between devices, on_device(): far_weights = lax.ppermute(near_weights, 'c', swap)  6.18 us
    ppermute x1, starting transfers between devices, on_device(): other = lax.ppermute(w_query, 'zl', swap)  4.82 us
    unnamed x14, local copies, waits for them, and re-layouts  4.4 us
    ppermute x1, starting transfers between devices, on_device(): other_values = lax.ppermute(values, 'zl', swap)  3.55 us
    ppermute x1, starting transfers between devices, on_device(): far = lax.ppermute(near, 'c', swap)  3.23 us
  transfers between devices with their start and end apart: 9, of which 8 were waited for; matrix products, arithmetic and copies ran while one was open for 3% of the time, Pallas kernels for 7%

profile of v7, /device:TPU:1, one launch (start us, length us, event | category | flops | bytes accessed | tf_op | source)
XLA Modules:
  0.0 129.7 jit_solution(6318445916886674597)
XLA Ops:
  7.2 1.4 %broadcast_in_dim.20 = bf16[4,32,256]{2,1,0:T(8,128)(2,1)} broadcast(bf16[32,256]{1,0:T(8,128)(2,1)} %bitcast.21), dimensions={1,2} | broadcast | bytes 81920 | tf_op jit(solution)/shard_map/broadcast_in_dim | solution.py:343
  8.5 4.8 %collective-permute-start = (bf16[256,256]{1,0:T(8,128)(2,1)}, bf16[256,256]{1,0:T(8,128)(2,1)S(1)}, u32[]{:S(2)}, u32[]{:S(2)}) collective-permute-start(bf16[256,256]{1,0:T(8,128)(2,1)} %param.10), channel_id=1, source_target_pairs={{0,32},{32,0},{1,33},{33,1},{2,34},{34,2},{3,35},{35,3},{4,36},{36... | collective-permute-start | bytes 393224 | tf_op jit(solution)/shard_map/ppermute | solution.py:345
  13.3 4.0 %all-to-all-start = ((bf16[4,32,256]{2,1,0:T(8,128)(2,1)}), bf16[4,32,256]{2,1,0:T(8,128)(2,1)S(1)}, u32[]{:S(2)}, u32[]{:S(2)}) async-start(bf16[4,32,256]{2,1,0:T(8,128)(2,1)} %broadcast_in_dim.20), calls=%async_computation | async-start | bytes 131072 | tf_op jit(solution)/shard_map/all_to_all | solution.py:326
  17.4 0.0 all-gather.2.cloned.1.call-start
  17.4 0.7 bitcast_convert_fusion.readout_ref
  18.0 0.8 dynamic_slice.3
  18.8 0.7 fusion.4.key_ref
  19.5 0.9 pad.16
  20.4 1.4 %all-to-all-done.value_ref = bf16[4,32,256]{2,1,0:T(8,128)(2,1)S(1)} async-done(((bf16[4,32,256]{2,1,0:T(8,128)(2,1)}), bf16[4,32,256]{2,1,0:T(8,128)(2,1)S(1)}, u32[]{:S(2)}, u32[]{:S(2)}) %all-to-all-start) | async-done | bytes 65568 | tf_op jit(solution)/shard_map/all_to_all | solution.py:326
  21.8 0.0 collective-permute-done
  21.9 0.0 copy-start.6
  21.9 0.0 copy-start.3
  21.9 0.0 copy-start.4
  21.9 0.0 copy-start.5
  21.9 0.9 fold_weights.1
  22.8 0.0 all-gather.2.cloned.1.call-update
  22.8 6.9 %all-to-all-start.1 = ((bf16[16,40,256]{2,1,0:T(8,128)(2,1)}), bf16[16,40,256]{2,1,0:T(8,128)(2,1)S(1)}, u32[]{:S(2)}, u32[]{:S(2)}) async-start(bf16[16,40,256]{2,1,0:T(8,128)(2,1)} %fold_weights.1), calls=%async_computation.1 | async-start | bytes 655360 | tf_op jit(solution)/shard_map/all_to_all | solution.py:326
  29.8 0.0 copy-done.3
  29.8 0.0 copy-done.4
  29.8 0.0 copy-done.5
  29.8 3.0 %tree.1 = (s32[168]{0:T(256)S(1)}, f32[32,128]{1,0:T(8,128)S(1)}, f32[1,256]{1,0:T(1,128)S(1)}, f32[1,256]{1,0:T(1,128)S(1)}) custom-call(s32[32]{0:T(128)S(1)} %copy-done.3, s32[32]{0:T(128)S(1)} %copy-done.4, s32[32]{0:T(128)S(1)} %copy-done.5), custom_call_target="tpu_custom_call" | custom-call | tf_op jit(solution)/shard_map/tree/pallas_call | solution.py:376
  32.8 0.6 fusion
  33.3 6.8 %all-to-all-done.1.weights_ref = bf16[16,40,256]{2,1,0:T(8,128)(2,1)S(1)} async-done(((bf16[16,40,256]{2,1,0:T(8,128)(2,1)}), bf16[16,40,256]{2,1,0:T(8,128)(2,1)S(1)}, u32[]{:S(2)}, u32[]{:S(2)}) %all-to-all-start.1) | async-done | bytes 327712 | tf_op jit(solution)/shard_map/all_to_all | solution.py:326
  40.1 6.2 %collective-permute-start.1 = (bf16[16,40,256]{2,1,0:T(8,128)(2,1)S(1)}, bf16[16,40,256]{2,1,0:T(8,128)(2,1)S(1)}, u32[]{:S(2)}, u32[]{:S(2)}) collective-permute-start(bf16[16,40,256]{2,1,0:T(8,128)(2,1)S(1)} %all-to-all-done.1.weights_ref), channel_id=1, source_target_pairs={{0,16},{16,0},{1,17},{17,1},{2,18},{18,2},{3,19},{19,3},{4,20},{20... | collective-permute-start | bytes 983048 | tf_op jit(solution)/shard_map/ppermute | solution.py:400
  46.3 0.0 copy-done
  46.3 0.8 project_near_keys.1.near_ref
  47.1 0.5 collective-permute-done.1.weights_ref
  47.6 0.8 project_far_keys.1
  48.4 13.8 %all_to_all.37 = bf16[8,40,256]{2,1,0:T(8,128)(2,1)S(1)} all-to-all(bf16[8,40,256]{2,1,0:T(8,128)(2,1)S(1)} %get-tuple-element.62), channel_id=1, replica_groups=mesh['y'=8,'zl'=2,'c'=2,'zh'=4,'x'=4] {'y'}, dimensions={0} | all-to-all | bytes 327680 | tf_op jit(solution)/shard_map/all_to_all | solution.py:326
  62.2 1.1 spread_keys.1
  63.3 3.6 %all-to-all-start.3 = ((bf16[8,8,32,256]{3,2,1,0:T(8,128)(2,1)}), bf16[8,8,32,256]{3,2,1,0:T(8,128)(2,1)S(1)}, u32[]{:S(2)}, u32[]{:S(2)}) async-start(bf16[8,8,32,256]{3,2,1,0:T(8,128)(2,1)} %spread_keys.1), calls=%async_computation.3 | async-start | bytes 2097152 | tf_op jit(solution)/shard_map/all_to_all | solution.py:326
  66.9 3.0 %collective-permute-start.2 = (bf16[8,8,256]{2,1,0:T(8,128)(2,1)S(1)}, bf16[8,8,256]{2,1,0:T(8,128)(2,1)S(1)}, u32[]{:S(2)}, u32[]{:S(2)}) collective-permute-start(bf16[8,8,256]{2,1,0:T(8,128)(2,1)S(1)} %get-tuple-element.83), channel_id=1, source_target_pairs={{0,16},{16,0},{1,17},{17,1},{2,18},{18,2},{3,19},{19,3},{4,20},{20... | collective-permute-start | bytes 98312 | tf_op jit(solution)/shard_map/ppermute | solution.py:450
  69.9 0.8 collective-permute-done.2
  70.8 3.6 %collective-permute-start.3 = (bf16[2,8,8,256]{3,2,1,0:T(8,128)(2,1)S(1)}, bf16[2,8,8,256]{3,2,1,0:T(8,128)(2,1)S(1)}, u32[]{:S(2)}, u32[]{:S(2)}) collective-permute-start(bf16[2,8,8,256]{3,2,1,0:T(8,128)(2,1)S(1)} %pad_maximum_fusion.own_ref), channel_id=1, source_target_pairs={{0,32},{32,0},{1,33},{33,1},{2,34},{34,2},{3,35},{35,3},{4,36},{36... | collective-permute-start | bytes 196616 | tf_op jit(solution)/shard_map/ppermute | solution.py:452
  74.3 0.1 all-gather.2.cloned.1.call-done
  74.4 2.2 %copy-done.1 = bf16[256,8192]{1,0:T(8,128)(2,1)S(1)} copy-done((bf16[256,8192]{1,0:T(8,128)(2,1)S(1)}, bf16[256,8192]{1,0:T(8,128)(2,1)}, u32[]{:S(2)}) %copy-start.1) | copy-done | bytes 4194328
  76.6 2.2 %copy-done.2 = bf16[8192,256]{1,0:T(8,128)(2,1)S(1)} copy-done((bf16[8192,256]{1,0:T(8,128)(2,1)S(1)}, bf16[8192,256]{1,0:T(8,128)(2,1)}, u32[]{:S(2)}) %copy-start.2) | copy-done | bytes 4194328
  78.8 1.4 %project_queries.1.query_ref = bf16[128,512]{1,0:T(8,128)(2,1)S(1)} custom-call(bf16[256,8192]{1,0:T(8,128)(2,1)S(1)} %copy-done.1, bf16[32,256,256]{2,1,0:T(8,128)(2,1)S(1)} %bitcast.16, f32[128,256]{1,0:T(8,128)S(1)} %get-tuple-element.60.cosine_ref, f32[128,256]{1,0:T(8,128)S(1)} %get-tuple-element.64.sine_ref), custom_call_target="tpu_custom_call" | custom-call | flops 1073741824 | bytes 8388608 | tf_op jit(solution)/shard_map/project_queries/pallas_call | solution.py:453
  80.2 0.6 collective-permute-done.3.other_ref
  80.7 0.7 all-to-all-done.3.keys_ref
  81.4 3.2 %collective-permute-start.4 = (bf16[8,8,32,256]{3,2,1,0:T(8,128)(2,1)S(1)}, bf16[8,8,32,256]{3,2,1,0:T(8,128)(2,1)S(1)}, u32[]{:S(2)}, u32[]{:S(2)}) collective-permute-start(bf16[8,8,32,256]{3,2,1,0:T(8,128)(2,1)S(1)} %all-to-all-done.3.keys_ref), channel_id=1, source_target_pairs={{0,16},{16,0},{1,17},{17,1},{2,18},{18,2},{3,19},{19,3},{4,20},{20... | collective-permute-start | bytes 3145736 | tf_op jit(solution)/shard_map/ppermute | solution.py:468
  84.7 1.7 %attend_near.1 = (f32[1,512]{1,0:T(1,128)S(1)}, f32[1,512]{1,0:T(1,128)S(1)}, f32[8,512]{1,0:T(8,128)S(1)}) custom-call(s32[168]{0:T(256)S(1)} %get-tuple-element.42.meta_ref, bf16[128,512]{1,0:T(8,128)(2,1)S(1)} %project_queries.1.query_ref, bf16[8,8,32,256]{3,2,1,0:T(8,128)(2,1)S(1)} %all-to-all-done.3.keys_ref, ...), custom_call_target="tpu_custom_call" | custom-call | flops 268435456 | bytes 2097152 | tf_op jit(solution)/shard_map/attend_near/pallas_call | solution.py:475
  86.3 0.6 collective-permute-done.4.keys_ref
  86.9 1.2 attend_far.1
  88.1 20.7 %all_to_all.38.parts_ref = f32[16,1,256]{2,1,0:T(1,128)S(1)} all-to-all(f32[16,1,256]{2,1,0:T(1,128)S(1)} %attend_far.1), channel_id=1, replica_groups=mesh['y'=8,'zl'=2,'c'=2,'zh'=4,'x'=4] {'zh','x'}, dimensions={0} | all-to-all | bytes 32768 | tf_op jit(solution)/shard_map/all_to_all | solution.py:326
  108.9 0.6 token_values.1
  109.5 12.9 %all_to_all.39 = f32[32,1,128]{2,1,0:T(1,128)S(1)} all-to-all(f32[32,1,128]{2,1,0:T(1,128)S(1)} %bitcast.17), channel_id=1, replica_groups=mesh['y'=8,'zl'=2,'c'=2,'zh'=4,'x'=4] {'y','zl','c'}, dimensions={0} | all-to-all | bytes 32768 | tf_op jit(solution)/shard_map/all_to_all | solution.py:326
  122.3 0.5 multiply_reduce_fusion
  (11 shorter events, 0.1 us)
Async XLA Ops:
  8.5 13.3 %collective-permute-start = (bf16[256,256]{1,0:T(8,128)(2,1)}, bf16[256,256]{1,0:T(8,128)(2,1)S(1)}, u32[]{:S(2)}, u32[]{:S(2)}) collective-permute-start(bf16[256,256]{1,0:T(8,128)(2,1)} %param.10), channel_id=1, source_target_pairs={{0,32},{32,0},{1,33},{33,1},{2,34},{34,2},{3,35},{35,3},{4,36},{36... | collective-permute-start | bytes 393224 | tf_op jit(solution)/shard_map/ppermute | solution.py:345
  13.3 8.5 %all-to-all-start = ((bf16[4,32,256]{2,1,0:T(8,128)(2,1)}), bf16[4,32,256]{2,1,0:T(8,128)(2,1)S(1)}, u32[]{:S(2)}, u32[]{:S(2)}) async-start(bf16[4,32,256]{2,1,0:T(8,128)(2,1)} %broadcast_in_dim.20), calls=%async_computation | async-start | bytes 131072 | tf_op jit(solution)/shard_map/all_to_all | solution.py:326
  17.4 57.0 %all-gather.2.cloned.1.call-start = ((), (), s32[]{:S(2)}) async-start(), calls=%async_computation.6 | async-start | bytes 4456448 | tf_op jit(solution)/shard_map/all_gather | solution.py:372
  21.9 0.9 copy-start.6
  21.9 7.9 %copy-start.3 = (s32[32]{0:T(128)S(1)}, s32[32]{0:T(128)}, u32[]{:S(2)}) copy-start(s32[32]{0:T(128)} %parents_src.1) | copy-start | bytes 388
  21.9 7.9 %copy-start.4 = (s32[32]{0:T(128)S(1)}, s32[32]{0:T(128)}, u32[]{:S(2)}) copy-start(s32[32]{0:T(128)} %placed_src.1) | copy-start | bytes 388
  21.9 7.9 %copy-start.5 = (s32[32]{0:T(128)S(1)}, s32[32]{0:T(128)}, u32[]{:S(2)}) copy-start(s32[32]{0:T(128)} %lengths_src.1) | copy-start | bytes 388
  22.8 17.3 %all-to-all-start.1 = ((bf16[16,40,256]{2,1,0:T(8,128)(2,1)}), bf16[16,40,256]{2,1,0:T(8,128)(2,1)S(1)}, u32[]{:S(2)}, u32[]{:S(2)}) async-start(bf16[16,40,256]{2,1,0:T(8,128)(2,1)} %fold_weights.1), calls=%async_computation.1 | async-start | bytes 655360 | tf_op jit(solution)/shard_map/all_to_all | solution.py:326
  40.1 6.2 %copy-start = (bf16[256,8192]{1,0:T(8,128)(2,1)S(1)}, bf16[256,8192]{1,0:T(8,128)(2,1)}, u32[]{:S(2)}) copy-start(bf16[256,8192]{1,0:T(8,128)(2,1)} %tokens_ref.5) | copy-start | bytes 12582916
  40.1 7.5 %collective-permute-start.1 = (bf16[16,40,256]{2,1,0:T(8,128)(2,1)S(1)}, bf16[16,40,256]{2,1,0:T(8,128)(2,1)S(1)}, u32[]{:S(2)}, u32[]{:S(2)}) collective-permute-start(bf16[16,40,256]{2,1,0:T(8,128)(2,1)S(1)} %all-to-all-done.1.weights_ref), channel_id=1, source_target_pairs={{0,16},{16,0},{1,17},{17,1},{2,18},{18,2},{3,19},{19,3},{4,20},{20... | collective-permute-start | bytes 983048 | tf_op jit(solution)/shard_map/ppermute | solution.py:400
  63.3 18.2 %all-to-all-start.3 = ((bf16[8,8,32,256]{3,2,1,0:T(8,128)(2,1)}), bf16[8,8,32,256]{3,2,1,0:T(8,128)(2,1)S(1)}, u32[]{:S(2)}, u32[]{:S(2)}) async-start(bf16[8,8,32,256]{3,2,1,0:T(8,128)(2,1)} %spread_keys.1), calls=%async_computation.3 | async-start | bytes 2097152 | tf_op jit(solution)/shard_map/all_to_all | solution.py:326
  66.9 3.9 %collective-permute-start.2 = (bf16[8,8,256]{2,1,0:T(8,128)(2,1)S(1)}, bf16[8,8,256]{2,1,0:T(8,128)(2,1)S(1)}, u32[]{:S(2)}, u32[]{:S(2)}) collective-permute-start(bf16[8,8,256]{2,1,0:T(8,128)(2,1)S(1)} %get-tuple-element.83), channel_id=1, source_target_pairs={{0,16},{16,0},{1,17},{17,1},{2,18},{18,2},{3,19},{19,3},{4,20},{20... | collective-permute-start | bytes 98312 | tf_op jit(solution)/shard_map/ppermute | solution.py:450
  70.8 10.0 %collective-permute-start.3 = (bf16[2,8,8,256]{3,2,1,0:T(8,128)(2,1)S(1)}, bf16[2,8,8,256]{3,2,1,0:T(8,128)(2,1)S(1)}, u32[]{:S(2)}, u32[]{:S(2)}) collective-permute-start(bf16[2,8,8,256]{3,2,1,0:T(8,128)(2,1)S(1)} %pad_maximum_fusion.own_ref), channel_id=1, source_target_pairs={{0,32},{32,0},{1,33},{33,1},{2,34},{34,2},{3,35},{35,3},{4,36},{36... | collective-permute-start | bytes 196616 | tf_op jit(solution)/shard_map/ppermute | solution.py:452
  74.4 2.2 %copy-start.1 = (bf16[256,8192]{1,0:T(8,128)(2,1)S(1)}, bf16[256,8192]{1,0:T(8,128)(2,1)}, u32[]{:S(2)}) copy-start(bf16[256,8192]{1,0:T(8,128)(2,1)} %tokens_ref.5) | copy-start | bytes 12582916
  76.6 2.2 %copy-start.2 = (bf16[8192,256]{1,0:T(8,128)(2,1)S(1)}, bf16[8192,256]{1,0:T(8,128)(2,1)}, u32[]{:S(2)}) copy-start(bf16[8192,256]{1,0:T(8,128)(2,1)} %all-gather.2.cloned.1.call-done) | copy-start | bytes 12582916
  81.4 5.5 %collective-permute-start.4 = (bf16[8,8,32,256]{3,2,1,0:T(8,128)(2,1)S(1)}, bf16[8,8,32,256]{3,2,1,0:T(8,128)(2,1)S(1)}, u32[]{:S(2)}, u32[]{:S(2)}) collective-permute-start(bf16[8,8,32,256]{3,2,1,0:T(8,128)(2,1)S(1)} %all-to-all-done.3.keys_ref), channel_id=1, source_target_pairs={{0,16},{16,0},{1,17},{17,1},{2,18},{18,2},{3,19},{19,3},{4,20},{20... | collective-permute-start | bytes 3145736 | tf_op jit(solution)/shard_map/ppermute | solution.py:468
Sparse Core Ops, SparseCore 0:
  22.9 51.4 all-gather.1

commit v8 on v7

--- a/solution.py
+++ b/solution.py
@@ -341,7 +341,6 @@
     params = pltpu.CompilerParams(vmem_limit_bytes=VMEM_LIMIT)
 
     sent = jnp.broadcast_to(value_weight.T[None], (quarters, width, seg_len))
-    sent, w_query = lax.optimization_barrier((sent, w_query))
     other = lax.ppermute(w_query, "zl", swap)
     values_x = gathered(sent, "x")
     readout = head_readout.reshape(heads, HEAD_SIZE).astype(jnp.float32)
@@ -355,8 +354,8 @@
         ]
     )
     both = jnp.pad(w_query, ((0, w_query.shape[0]), (0, 0)))
-    values_x, other, readout, key_rows, both = lax.optimization_barrier(
-        (values_x, other, readout, key_rows, both)
+    values_x, readout, key_rows, both = lax.optimization_barrier(
+        (values_x, readout, key_rows, both)
     )
     both = lax.dynamic_update_slice(both, other, (w_query.shape[0], 0))
     pieces = pl.pallas_call(

time: 131 us -> 130 us (level)
  waiting for transfers between devices: 11.5 us -> 9.29 us
  blocking collectives: 47.4 us -> 45.2 us
  starting transfers between devices: 35.4 us -> 36.9 us
    all_to_all x3, blocking collectives: 47.4 us -> 45.2 us  [gathered(): return lax.all_to_all(value, axis, 0, 0)]
    all_to_all x3, waiting for transfers between devices: 8.89 us -> 7.12 us  [gathered(): return lax.all_to_all(value, axis, 0, 0)]
    all_to_all x3, starting transfers between devices: 14.5 us -> 16.1 us  [gathered(): return lax.all_to_all(value, axis, 0, 0)]
  transfers between devices with their start and end apart: 9 -> 9, of which waited for: 8 -> 5; matrix products, arithmetic and copies ran while one was open for 3% -> 3% of each run, Pallas kernels for 7% -> 7%
where the time goes in v8:
time: 130 us; the launch traced here: 129 us
  blocking collectives  45.2 us (35%)
  starting transfers between devices  36.9 us (28%)
  between operations  14.3 us (11%)
  Pallas kernels  12.6 us (10%)
  waiting for transfers between devices  9.29 us (7%)
  local copies, waits for them, and re-layouts  8.17 us (6%)
  other arithmetic  2.48 us (2%)
    all_to_all x3, blocking collectives, gathered(): return lax.all_to_all(value, axis, 0, 0)  45.2 us
    all_to_all x3, starting transfers between devices, gathered(): return lax.all_to_all(value, axis, 0, 0)  16.1 us
    all_to_all x3, waiting for transfers between devices, gathered(): return lax.all_to_all(value, axis, 0, 0)  7.12 us
    ppermute x1, starting transfers between devices, on_device(): far_weights = lax.ppermute(near_weights, 'c', swap)  5.83 us
    unnamed x14, local copies, waits for them, and re-layouts  5.11 us
    ppermute x1, starting transfers between devices, on_device(): other = lax.ppermute(w_query, 'zl', swap)  3.99 us
    ppermute x1, starting transfers between devices, on_device(): far = lax.ppermute(near, 'c', swap)  3.93 us
    ppermute x1, starting transfers between devices, on_device(): other_values = lax.ppermute(values, 'zl', swap)  3.64 us
  transfers between devices with their start and end apart: 9, of which 5 were waited for; matrix products, arithmetic and copies ran while one was open for 3% of the time, Pallas kernels for 7%

profile of v8, /device:TPU:1, one launch (start us, length us, event | category | flops | bytes accessed | tf_op | source)
XLA Modules:
  0.0 128.8 jit_solution(17053334636908736838)
XLA Ops:
  7.2 1.4 %broadcast_in_dim.20 = bf16[4,32,256]{2,1,0:T(8,128)(2,1)} broadcast(bf16[32,256]{1,0:T(8,128)(2,1)} %bitcast.21), dimensions={1,2} | broadcast | bytes 81920 | tf_op jit(solution)/shard_map/broadcast_in_dim | solution.py:343
  8.5 4.8 %all-to-all-start = ((bf16[4,32,256]{2,1,0:T(8,128)(2,1)}), bf16[4,32,256]{2,1,0:T(8,128)(2,1)S(1)}, u32[]{:S(2)}, u32[]{:S(2)}) async-start(bf16[4,32,256]{2,1,0:T(8,128)(2,1)} %broadcast_in_dim.20), calls=%async_computation | async-start | bytes 131072 | tf_op jit(solution)/shard_map/all_to_all | solution.py:326
  13.4 0.0 all-gather.2.cloned.1.call-start
  13.4 4.0 %collective-permute-start = (bf16[256,256]{1,0:T(8,128)(2,1)}, bf16[256,256]{1,0:T(8,128)(2,1)S(1)}, u32[]{:S(2)}, u32[]{:S(2)}) collective-permute-start(bf16[256,256]{1,0:T(8,128)(2,1)} %param.10), channel_id=1, source_target_pairs={{0,32},{32,0},{1,33},{33,1},{2,34},{34,2},{3,35},{35,3},{4,36},{36... | collective-permute-start | bytes 393224 | tf_op jit(solution)/shard_map/ppermute | solution.py:344
  17.4 0.8 dynamic_slice.3
  18.1 0.7 bitcast_convert_fusion.readout_ref
  18.8 0.7 fusion.4.key_ref
  19.5 0.9 pad.16
  20.4 0.0 copy-start.3
  20.5 0.0 copy-start.4
  20.5 0.0 copy-start.5
  20.5 0.0 all-to-all-done.value_ref
  20.5 0.9 fold_weights.1
  21.4 0.0 collective-permute-done
  21.4 0.0 copy-start.6
  21.4 0.7 copy-done.6
  22.1 0.0 all-gather.2.cloned.1.call-update
  22.1 6.9 %all-to-all-start.1 = ((bf16[16,40,256]{2,1,0:T(8,128)(2,1)}), bf16[16,40,256]{2,1,0:T(8,128)(2,1)S(1)}, u32[]{:S(2)}, u32[]{:S(2)}) async-start(bf16[16,40,256]{2,1,0:T(8,128)(2,1)} %fold_weights.1), calls=%async_computation.1 | async-start | bytes 655360 | tf_op jit(solution)/shard_map/all_to_all | solution.py:326
  29.1 0.0 copy-done.3
  29.1 0.0 copy-done.4
  29.1 3.0 %tree.1 = (s32[168]{0:T(256)S(1)}, f32[32,128]{1,0:T(8,128)S(1)}, f32[1,256]{1,0:T(1,128)S(1)}, f32[1,256]{1,0:T(1,128)S(1)}) custom-call(s32[32]{0:T(128)S(1)} %copy-done.3, s32[32]{0:T(128)S(1)} %copy-done.4, s32[32]{0:T(128)S(1)} %copy-done.5), custom_call_target="tpu_custom_call" | custom-call | tf_op jit(solution)/shard_map/tree/pallas_call | solution.py:375
  32.1 0.6 fusion
  32.7 7.1 %all-to-all-done.1.weights_ref = bf16[16,40,256]{2,1,0:T(8,128)(2,1)S(1)} async-done(((bf16[16,40,256]{2,1,0:T(8,128)(2,1)}), bf16[16,40,256]{2,1,0:T(8,128)(2,1)S(1)}, u32[]{:S(2)}, u32[]{:S(2)}) %all-to-all-start.1) | async-done | bytes 327712 | tf_op jit(solution)/shard_map/all_to_all | solution.py:326
  39.8 5.8 %collective-permute-start.1 = (bf16[16,40,256]{2,1,0:T(8,128)(2,1)S(1)}, bf16[16,40,256]{2,1,0:T(8,128)(2,1)S(1)}, u32[]{:S(2)}, u32[]{:S(2)}) collective-permute-start(bf16[16,40,256]{2,1,0:T(8,128)(2,1)S(1)} %all-to-all-done.1.weights_ref), channel_id=1, source_target_pairs={{0,16},{16,0},{1,17},{17,1},{2,18},{18,2},{3,19},{19,3},{4,20},{20... | collective-permute-start | bytes 983048 | tf_op jit(solution)/shard_map/ppermute | solution.py:399
  45.6 0.0 copy-done
  45.6 0.8 project_near_keys.1.near_ref
  46.4 0.4 collective-permute-done.1.weights_ref
  46.9 0.8 project_far_keys.1
  47.6 13.7 %all_to_all.37 = bf16[8,40,256]{2,1,0:T(8,128)(2,1)S(1)} all-to-all(bf16[8,40,256]{2,1,0:T(8,128)(2,1)S(1)} %get-tuple-element.56), channel_id=1, replica_groups=mesh['y'=8,'zl'=2,'c'=2,'zh'=4,'x'=4] {'y'}, dimensions={0} | all-to-all | bytes 327680 | tf_op jit(solution)/shard_map/all_to_all | solution.py:326
  61.3 1.1 spread_keys.1
  62.4 4.3 %all-to-all-start.3 = ((bf16[8,8,32,256]{3,2,1,0:T(8,128)(2,1)}), bf16[8,8,32,256]{3,2,1,0:T(8,128)(2,1)S(1)}, u32[]{:S(2)}, u32[]{:S(2)}) async-start(bf16[8,8,32,256]{3,2,1,0:T(8,128)(2,1)} %spread_keys.1), calls=%async_computation.3 | async-start | bytes 2097152 | tf_op jit(solution)/shard_map/all_to_all | solution.py:326
  66.7 3.4 %collective-permute-start.2 = (bf16[8,8,256]{2,1,0:T(8,128)(2,1)S(1)}, bf16[8,8,256]{2,1,0:T(8,128)(2,1)S(1)}, u32[]{:S(2)}, u32[]{:S(2)}) collective-permute-start(bf16[8,8,256]{2,1,0:T(8,128)(2,1)S(1)} %get-tuple-element.77), channel_id=1, source_target_pairs={{0,16},{16,0},{1,17},{17,1},{2,18},{18,2},{3,19},{19,3},{4,20},{20... | collective-permute-start | bytes 98312 | tf_op jit(solution)/shard_map/ppermute | solution.py:449
  70.1 0.8 collective-permute-done.2
  71.0 3.6 %collective-permute-start.3 = (bf16[2,8,8,256]{3,2,1,0:T(8,128)(2,1)S(1)}, bf16[2,8,8,256]{3,2,1,0:T(8,128)(2,1)S(1)}, u32[]{:S(2)}, u32[]{:S(2)}) collective-permute-start(bf16[2,8,8,256]{3,2,1,0:T(8,128)(2,1)S(1)} %pad_maximum_fusion.own_ref), channel_id=1, source_target_pairs={{0,32},{32,0},{1,33},{33,1},{2,34},{34,2},{3,35},{35,3},{4,36},{36... | collective-permute-start | bytes 196616 | tf_op jit(solution)/shard_map/ppermute | solution.py:451
  74.6 0.2 all-gather.2.cloned.1.call-done
  74.9 2.2 %copy-done.1 = bf16[256,8192]{1,0:T(8,128)(2,1)S(1)} copy-done((bf16[256,8192]{1,0:T(8,128)(2,1)S(1)}, bf16[256,8192]{1,0:T(8,128)(2,1)}, u32[]{:S(2)}) %copy-start.1) | copy-done | bytes 4194328
  77.1 2.2 %copy-done.2 = bf16[8192,256]{1,0:T(8,128)(2,1)S(1)} copy-done((bf16[8192,256]{1,0:T(8,128)(2,1)S(1)}, bf16[8192,256]{1,0:T(8,128)(2,1)}, u32[]{:S(2)}) %copy-start.2) | copy-done | bytes 4194328
  79.2 1.4 %project_queries.1.query_ref = bf16[128,512]{1,0:T(8,128)(2,1)S(1)} custom-call(bf16[256,8192]{1,0:T(8,128)(2,1)S(1)} %copy-done.1, bf16[32,256,256]{2,1,0:T(8,128)(2,1)S(1)} %bitcast.16, f32[128,256]{1,0:T(8,128)S(1)} %get-tuple-element.54.cosine_ref, f32[128,256]{1,0:T(8,128)S(1)} %get-tuple-element.58.sine_ref), custom_call_target="tpu_custom_call" | custom-call | flops 1073741824 | bytes 8388608 | tf_op jit(solution)/shard_map/project_queries/pallas_call | solution.py:452
  80.6 0.0 collective-permute-done.3.other_ref
  80.7 0.0 all-to-all-done.3.keys_ref
  80.7 3.9 %collective-permute-start.4 = (bf16[8,8,32,256]{3,2,1,0:T(8,128)(2,1)S(1)}, bf16[8,8,32,256]{3,2,1,0:T(8,128)(2,1)S(1)}, u32[]{:S(2)}, u32[]{:S(2)}) collective-permute-start(bf16[8,8,32,256]{3,2,1,0:T(8,128)(2,1)S(1)} %all-to-all-done.3.keys_ref), channel_id=1, source_target_pairs={{0,16},{16,0},{1,17},{17,1},{2,18},{18,2},{3,19},{19,3},{4,20},{20... | collective-permute-start | bytes 3145736 | tf_op jit(solution)/shard_map/ppermute | solution.py:467
  84.6 1.6 %attend_near.1 = (f32[1,512]{1,0:T(1,128)S(1)}, f32[1,512]{1,0:T(1,128)S(1)}, f32[8,512]{1,0:T(8,128)S(1)}) custom-call(s32[168]{0:T(256)S(1)} %get-tuple-element.39.meta_ref, bf16[128,512]{1,0:T(8,128)(2,1)S(1)} %project_queries.1.query_ref, bf16[8,8,32,256]{3,2,1,0:T(8,128)(2,1)S(1)} %all-to-all-done.3.keys_ref, ...), custom_call_target="tpu_custom_call" | custom-call | flops 268435456 | bytes 2097152 | tf_op jit(solution)/shard_map/attend_near/pallas_call | solution.py:474
  86.2 0.6 collective-permute-done.4.keys_ref
  86.9 2.5 %attend_far.1 = f32[16,1,256]{2,1,0:T(1,128)S(1)} custom-call(s32[168]{0:T(256)S(1)} %get-tuple-element.39.meta_ref, bf16[128,512]{1,0:T(8,128)(2,1)S(1)} %project_queries.1.query_ref, bf16[8,8,32,256]{3,2,1,0:T(8,128)(2,1)S(1)} %collective-permute-done.4.keys_ref, bf16[2,8,8,256]{3,2,1,0:T(8,128)(2,1)S(1)} %pad_maximum_fusion.own_ref, ...), custom_call_target="tpu_custom_call" | custom-call | tf_op jit(solution)/shard_map/attend_far/pallas_call | solution.py:486
  89.3 21.0 %all_to_all.38.parts_ref = f32[16,1,256]{2,1,0:T(1,128)S(1)} all-to-all(f32[16,1,256]{2,1,0:T(1,128)S(1)} %attend_far.1), channel_id=1, replica_groups=mesh['y'=8,'zl'=2,'c'=2,'zh'=4,'x'=4] {'zh','x'}, dimensions={0} | all-to-all | bytes 32768 | tf_op jit(solution)/shard_map/all_to_all | solution.py:326
  110.4 0.6 token_values.1
  110.9 10.5 %all_to_all.39 = f32[32,1,128]{2,1,0:T(1,128)S(1)} all-to-all(f32[32,1,128]{2,1,0:T(1,128)S(1)} %bitcast.17), channel_id=1, replica_groups=mesh['y'=8,'zl'=2,'c'=2,'zh'=4,'x'=4] {'y','zl','c'}, dimensions={0} | all-to-all | bytes 32768 | tf_op jit(solution)/shard_map/all_to_all | solution.py:326
  121.5 0.5 multiply_reduce_fusion
  (11 shorter events, 0.1 us)
Async XLA Ops:
  8.5 12.0 %all-to-all-start = ((bf16[4,32,256]{2,1,0:T(8,128)(2,1)}), bf16[4,32,256]{2,1,0:T(8,128)(2,1)S(1)}, u32[]{:S(2)}, u32[]{:S(2)}) async-start(bf16[4,32,256]{2,1,0:T(8,128)(2,1)} %broadcast_in_dim.20), calls=%async_computation | async-start | bytes 131072 | tf_op jit(solution)/shard_map/all_to_all | solution.py:326
  13.4 61.5 %all-gather.2.cloned.1.call-start = ((), (), s32[]{:S(2)}) async-start(), calls=%async_computation.6 | async-start | bytes 4456448 | tf_op jit(solution)/shard_map/all_gather | solution.py:371
  13.4 8.0 %collective-permute-start = (bf16[256,256]{1,0:T(8,128)(2,1)}, bf16[256,256]{1,0:T(8,128)(2,1)S(1)}, u32[]{:S(2)}, u32[]{:S(2)}) collective-permute-start(bf16[256,256]{1,0:T(8,128)(2,1)} %param.10), channel_id=1, source_target_pairs={{0,32},{32,0},{1,33},{33,1},{2,34},{34,2},{3,35},{35,3},{4,36},{36... | collective-permute-start | bytes 393224 | tf_op jit(solution)/shard_map/ppermute | solution.py:344
  20.4 8.6 %copy-start.3 = (s32[32]{0:T(128)S(1)}, s32[32]{0:T(128)}, u32[]{:S(2)}) copy-start(s32[32]{0:T(128)} %parents_src.1) | copy-start | bytes 388
  20.5 8.6 %copy-start.4 = (s32[32]{0:T(128)S(1)}, s32[32]{0:T(128)}, u32[]{:S(2)}) copy-start(s32[32]{0:T(128)} %placed_src.1) | copy-start | bytes 388
  20.5 8.6 %copy-start.5 = (s32[32]{0:T(128)S(1)}, s32[32]{0:T(128)}, u32[]{:S(2)}) copy-start(s32[32]{0:T(128)} %lengths_src.1) | copy-start | bytes 388
  21.4 0.7 copy-start.6
  22.1 17.7 %all-to-all-start.1 = ((bf16[16,40,256]{2,1,0:T(8,128)(2,1)}), bf16[16,40,256]{2,1,0:T(8,128)(2,1)S(1)}, u32[]{:S(2)}, u32[]{:S(2)}) async-start(bf16[16,40,256]{2,1,0:T(8,128)(2,1)} %fold_weights.1), calls=%async_computation.1 | async-start | bytes 655360 | tf_op jit(solution)/shard_map/all_to_all | solution.py:326
  39.8 5.9 %copy-start = (bf16[256,8192]{1,0:T(8,128)(2,1)S(1)}, bf16[256,8192]{1,0:T(8,128)(2,1)}, u32[]{:S(2)}) copy-start(bf16[256,8192]{1,0:T(8,128)(2,1)} %tokens_ref.5) | copy-start | bytes 12582916
  39.8 7.1 %collective-permute-start.1 = (bf16[16,40,256]{2,1,0:T(8,128)(2,1)S(1)}, bf16[16,40,256]{2,1,0:T(8,128)(2,1)S(1)}, u32[]{:S(2)}, u32[]{:S(2)}) collective-permute-start(bf16[16,40,256]{2,1,0:T(8,128)(2,1)S(1)} %all-to-all-done.1.weights_ref), channel_id=1, source_target_pairs={{0,16},{16,0},{1,17},{17,1},{2,18},{18,2},{3,19},{19,3},{4,20},{20... | collective-permute-start | bytes 983048 | tf_op jit(solution)/shard_map/ppermute | solution.py:399
  62.4 18.3 %all-to-all-start.3 = ((bf16[8,8,32,256]{3,2,1,0:T(8,128)(2,1)}), bf16[8,8,32,256]{3,2,1,0:T(8,128)(2,1)S(1)}, u32[]{:S(2)}, u32[]{:S(2)}) async-start(bf16[8,8,32,256]{3,2,1,0:T(8,128)(2,1)} %spread_keys.1), calls=%async_computation.3 | async-start | bytes 2097152 | tf_op jit(solution)/shard_map/all_to_all | solution.py:326
  66.7 4.3 %collective-permute-start.2 = (bf16[8,8,256]{2,1,0:T(8,128)(2,1)S(1)}, bf16[8,8,256]{2,1,0:T(8,128)(2,1)S(1)}, u32[]{:S(2)}, u32[]{:S(2)}) collective-permute-start(bf16[8,8,256]{2,1,0:T(8,128)(2,1)S(1)} %get-tuple-element.77), channel_id=1, source_target_pairs={{0,16},{16,0},{1,17},{17,1},{2,18},{18,2},{3,19},{19,3},{4,20},{20... | collective-permute-start | bytes 98312 | tf_op jit(solution)/shard_map/ppermute | solution.py:449
  71.0 9.7 %collective-permute-start.3 = (bf16[2,8,8,256]{3,2,1,0:T(8,128)(2,1)S(1)}, bf16[2,8,8,256]{3,2,1,0:T(8,128)(2,1)S(1)}, u32[]{:S(2)}, u32[]{:S(2)}) collective-permute-start(bf16[2,8,8,256]{3,2,1,0:T(8,128)(2,1)S(1)} %pad_maximum_fusion.own_ref), channel_id=1, source_target_pairs={{0,32},{32,0},{1,33},{33,1},{2,34},{34,2},{3,35},{35,3},{4,36},{36... | collective-permute-start | bytes 196616 | tf_op jit(solution)/shard_map/ppermute | solution.py:451
  74.9 2.2 %copy-start.1 = (bf16[256,8192]{1,0:T(8,128)(2,1)S(1)}, bf16[256,8192]{1,0:T(8,128)(2,1)}, u32[]{:S(2)}) copy-start(bf16[256,8192]{1,0:T(8,128)(2,1)} %tokens_ref.5) | copy-start | bytes 12582916
  77.1 2.2 %copy-start.2 = (bf16[8192,256]{1,0:T(8,128)(2,1)S(1)}, bf16[8192,256]{1,0:T(8,128)(2,1)}, u32[]{:S(2)}) copy-start(bf16[8192,256]{1,0:T(8,128)(2,1)} %all-gather.2.cloned.1.call-done) | copy-start | bytes 12582916
  80.7 6.2 %collective-permute-start.4 = (bf16[8,8,32,256]{3,2,1,0:T(8,128)(2,1)S(1)}, bf16[8,8,32,256]{3,2,1,0:T(8,128)(2,1)S(1)}, u32[]{:S(2)}, u32[]{:S(2)}) collective-permute-start(bf16[8,8,32,256]{3,2,1,0:T(8,128)(2,1)S(1)} %all-to-all-done.3.keys_ref), channel_id=1, source_target_pairs={{0,16},{16,0},{1,17},{17,1},{2,18},{18,2},{3,19},{19,3},{4,20},{20... | collective-permute-start | bytes 3145736 | tf_op jit(solution)/shard_map/ppermute | solution.py:467
Sparse Core Ops, SparseCore 0:
  22.2 52.5 all-gather.1

commit v9 on v8

--- a/solution.py
+++ b/solution.py
@@ -210,7 +210,10 @@
 
 def spread_kernel(keys_ref, out_ref, sems):
     copies = [
-        pltpu.make_async_copy(keys_ref, out_ref.at[i], sems.at[i]) for i in range(out_ref.shape[0])
+        pltpu.make_async_copy(
+            keys_ref.at[:, pl.ds(0, out_ref.shape[2])], out_ref.at[i], sems.at[i]
+        )
+        for i in range(out_ref.shape[0])
     ]
     for copy in copies:
         copy.start()
@@ -231,13 +234,15 @@
     return raw * (HEAD_SIZE ** (-0.5) * LOG2_E)
 
 
-def mixed_values(own_ref, other_ref, far, slot, weights):
+def valued(own_ref, other_ref, far, slot, weights):
     is_other = slot // 2 % 2 != lax.axis_index("zl")
     own, other = (ref[far, slot // 4].astype(jnp.float32) for ref in (own_ref, other_ref))
-    return jnp.dot(
-        jnp.where(is_other, other, own).astype(jnp.bfloat16),
-        weights.astype(jnp.bfloat16),
-        preferred_element_type=jnp.float32,
+    rows = jnp.where(is_other, other, own)
+    columns = (rows + pltpu.roll(rows, 6, 0)).T
+    keys = columns.shape[0]
+    heads = weights.shape[1] // keys
+    return weights * jnp.concatenate(
+        [jnp.broadcast_to(columns[:, h : h + 1], (keys, keys)) for h in range(heads)], axis=1
     )
 
 
@@ -261,10 +266,11 @@
         bottom[...] = bottom[...] * shrink + jnp.sum(
             weights[0] + weights[1], axis=0, keepdims=True
         )
-        summed[...] = (
-            summed[...] * shrink
-            + mixed_values(own_ref, other_ref, far, slots[0], weights[0])
-            + mixed_values(own_ref, other_ref, far, slots[1], weights[1])
+        summed[...] = summed[...] * shrink + jnp.sum(
+            valued(own_ref, other_ref, far, slots[0], weights[0])
+            + valued(own_ref, other_ref, far, slots[1], weights[1]),
+            axis=0,
+            keepdims=True,
         )
         return carry
 
@@ -282,7 +288,9 @@
     weights = jnp.exp2(masked - peak)
     top[...] = peak
     bottom[...] = jnp.sum(weights, axis=0, keepdims=True)
-    summed[...] = mixed_values(own_ref, other_ref, 0, own, weights)
+    summed[...] = jnp.sum(
+        valued(own_ref, other_ref, 0, own, weights), axis=0, keepdims=True
+    )
     visit(meta_ref, 0, query_ref, keys_ref, own_ref, other_ref, top, bottom, summed)
 
 
@@ -308,8 +316,7 @@
     scaled = summed[...] / bottom[...]
     result = jnp.zeros((1, seg_len), jnp.float32)
     for h in range(query_ref.shape[1] // seg_len):
-        part = scaled[:, h * seg_len : (h + 1) * seg_len]
-        result += part[h : h + 1] + part[2 + h : 3 + h]
+        result += scaled[:, h * seg_len : (h + 1) * seg_len]
     for i in range(out_ref.shape[0]):
         out_ref[i] = result
 
@@ -435,10 +442,11 @@
     keys_y = gathered(keys, "y")
     spread = lax.axis_size(("zl", "x"))
     values = keys_y[:, width:]
-    keys_y = keys_y[:, :width]
     copies = pl.pallas_call(
         spread_kernel,
-        out_shape=jax.ShapeDtypeStruct((spread, *keys_y.shape), keys_y.dtype),
+        out_shape=jax.ShapeDtypeStruct(
+            (spread, keys_y.shape[0], width, seg_len), keys_y.dtype
+        ),
         in_specs=[VMEM_SPEC],
         out_specs=HBM_SPEC,
         scratch_shapes=[pltpu.SemaphoreType.DMA((spread,))],
@@ -469,7 +477,7 @@
     state = (
         jax.ShapeDtypeStruct((1, columns), jnp.float32),
         jax.ShapeDtypeStruct((1, columns), jnp.float32),
-        jax.ShapeDtypeStruct((8, columns), jnp.float32),
+        jax.ShapeDtypeStruct((1, columns), jnp.float32),
     )
     near_state = pl.pallas_call(
         near_kernel,

time: 130 us -> 130 us (level)
  Pallas kernels: 12.6 us -> 11.2 us
where the time goes in v9:
time: 130 us; the launch traced here: 129 us
  blocking collectives  46.5 us (36%)
  starting transfers between devices  36.9 us (28%)
  between operations  14.3 us (11%)
  Pallas kernels  11.2 us (9%)
  waiting for transfers between devices  10 us (8%)
  local copies, waits for them, and re-layouts  8.16 us (6%)
  other arithmetic  2.48 us (2%)
    all_to_all x3, blocking collectives, gathered(): return lax.all_to_all(value, axis, 0, 0)  46.5 us
    all_to_all x3, starting transfers between devices, gathered(): return lax.all_to_all(value, axis, 0, 0)  16.1 us
    all_to_all x3, waiting for transfers between devices, gathered(): return lax.all_to_all(value, axis, 0, 0)  7.16 us
    ppermute x1, starting transfers between devices, on_device(): far_weights = lax.ppermute(near_weights, 'c', swap)  5.83 us
    unnamed x14, local copies, waits for them, and re-layouts  5.11 us
    ppermute x1, starting transfers between devices, on_device(): other = lax.ppermute(w_query, 'zl', swap)  3.99 us
    ppermute x1, starting transfers between devices, on_device(): far = lax.ppermute(near, 'c', swap)  3.91 us
    ppermute x1, starting transfers between devices, on_device(): other_values = lax.ppermute(values, 'zl', swap)  3.64 us
  transfers between devices with their start and end apart: 9, of which 5 were waited for; matrix products, arithmetic and copies ran while one was open for 3% of the time, Pallas kernels for 7%

profile of v9, /device:TPU:1, one launch (start us, length us, event | category | flops | bytes accessed | tf_op | source)
XLA Modules:
  0.0 129.4 jit_solution(16145568457255441889)
XLA Ops:
  7.2 1.4 %broadcast_in_dim.20 = bf16[4,32,256]{2,1,0:T(8,128)(2,1)} broadcast(bf16[32,256]{1,0:T(8,128)(2,1)} %bitcast.21), dimensions={1,2} | broadcast | bytes 81920 | tf_op jit(solution)/shard_map/broadcast_in_dim | solution.py:350
  8.5 4.8 %all-to-all-start = ((bf16[4,32,256]{2,1,0:T(8,128)(2,1)}), bf16[4,32,256]{2,1,0:T(8,128)(2,1)S(1)}, u32[]{:S(2)}, u32[]{:S(2)}) async-start(bf16[4,32,256]{2,1,0:T(8,128)(2,1)} %broadcast_in_dim.20), calls=%async_computation | async-start | bytes 131072 | tf_op jit(solution)/shard_map/all_to_all | solution.py:333
  13.4 0.0 all-gather.2.cloned.1.call-start
  13.4 4.0 %collective-permute-start = (bf16[256,256]{1,0:T(8,128)(2,1)}, bf16[256,256]{1,0:T(8,128)(2,1)S(1)}, u32[]{:S(2)}, u32[]{:S(2)}) collective-permute-start(bf16[256,256]{1,0:T(8,128)(2,1)} %param.10), channel_id=1, source_target_pairs={{0,32},{32,0},{1,33},{33,1},{2,34},{34,2},{3,35},{35,3},{4,36},{36... | collective-permute-start | bytes 393224 | tf_op jit(solution)/shard_map/ppermute | solution.py:351
  17.4 0.8 dynamic_slice.3
  18.1 0.7 bitcast_convert_fusion.readout_ref
  18.8 0.7 fusion.4.key_ref
  19.5 0.9 pad.16
  20.4 0.0 copy-start.3
  20.5 0.0 copy-start.4
  20.5 0.0 copy-start.5
  20.5 0.0 all-to-all-done.value_ref
  20.5 0.9 fold_weights.1
  21.4 0.0 collective-permute-done
  21.4 0.0 copy-start.6
  21.4 0.7 copy-done.6
  22.1 0.0 all-gather.2.cloned.1.call-update
  22.1 6.9 %all-to-all-start.1 = ((bf16[16,40,256]{2,1,0:T(8,128)(2,1)}), bf16[16,40,256]{2,1,0:T(8,128)(2,1)S(1)}, u32[]{:S(2)}, u32[]{:S(2)}) async-start(bf16[16,40,256]{2,1,0:T(8,128)(2,1)} %fold_weights.1), calls=%async_computation.1 | async-start | bytes 655360 | tf_op jit(solution)/shard_map/all_to_all | solution.py:333
  29.1 0.0 copy-done.3
  29.1 0.0 copy-done.4
  29.1 0.0 copy-done.5
  29.1 3.0 %tree.1 = (s32[168]{0:T(256)S(1)}, f32[32,128]{1,0:T(8,128)S(1)}, f32[1,256]{1,0:T(1,128)S(1)}, f32[1,256]{1,0:T(1,128)S(1)}) custom-call(s32[32]{0:T(128)S(1)} %copy-done.3, s32[32]{0:T(128)S(1)} %copy-done.4, s32[32]{0:T(128)S(1)} %copy-done.5), custom_call_target="tpu_custom_call" | custom-call | tf_op jit(solution)/shard_map/tree/pallas_call | solution.py:382
  32.1 0.6 fusion
  32.6 7.2 %all-to-all-done.1.weights_ref = bf16[16,40,256]{2,1,0:T(8,128)(2,1)S(1)} async-done(((bf16[16,40,256]{2,1,0:T(8,128)(2,1)}), bf16[16,40,256]{2,1,0:T(8,128)(2,1)S(1)}, u32[]{:S(2)}, u32[]{:S(2)}) %all-to-all-start.1) | async-done | bytes 327712 | tf_op jit(solution)/shard_map/all_to_all | solution.py:333
  39.8 5.8 %collective-permute-start.1 = (bf16[16,40,256]{2,1,0:T(8,128)(2,1)S(1)}, bf16[16,40,256]{2,1,0:T(8,128)(2,1)S(1)}, u32[]{:S(2)}, u32[]{:S(2)}) collective-permute-start(bf16[16,40,256]{2,1,0:T(8,128)(2,1)S(1)} %all-to-all-done.1.weights_ref), channel_id=1, source_target_pairs={{0,16},{16,0},{1,17},{17,1},{2,18},{18,2},{3,19},{19,3},{4,20},{20... | collective-permute-start | bytes 983048 | tf_op jit(solution)/shard_map/ppermute | solution.py:406
  45.6 0.8 project_near_keys.1.near_ref
  46.4 0.4 collective-permute-done.1.weights_ref
  46.9 0.8 project_far_keys.1
  47.6 13.7 %all_to_all.37.keys_ref = bf16[8,40,256]{2,1,0:T(8,128)(2,1)S(1)} all-to-all(bf16[8,40,256]{2,1,0:T(8,128)(2,1)S(1)} %get-tuple-element.56), channel_id=1, replica_groups=mesh['y'=8,'zl'=2,'c'=2,'zh'=4,'x'=4] {'y'}, dimensions={0} | all-to-all | bytes 327680 | tf_op jit(solution)/shard_map/all_to_all | solution.py:333
  61.3 1.1 spread_keys.1
  62.4 4.3 %all-to-all-start.3 = ((bf16[8,8,32,256]{3,2,1,0:T(8,128)(2,1)}), bf16[8,8,32,256]{3,2,1,0:T(8,128)(2,1)S(1)}, u32[]{:S(2)}, u32[]{:S(2)}) async-start(bf16[8,8,32,256]{3,2,1,0:T(8,128)(2,1)} %spread_keys.1), calls=%async_computation.3 | async-start | bytes 2097152 | tf_op jit(solution)/shard_map/all_to_all | solution.py:333
  66.7 3.4 %collective-permute-start.2 = (bf16[8,8,256]{2,1,0:T(8,128)(2,1)S(1)}, bf16[8,8,256]{2,1,0:T(8,128)(2,1)S(1)}, u32[]{:S(2)}, u32[]{:S(2)}) collective-permute-start(bf16[8,8,256]{2,1,0:T(8,128)(2,1)S(1)} %get-tuple-element.77), channel_id=1, source_target_pairs={{0,16},{16,0},{1,17},{17,1},{2,18},{18,2},{3,19},{19,3},{4,20},{20... | collective-permute-start | bytes 98312 | tf_op jit(solution)/shard_map/ppermute | solution.py:457
  70.1 0.8 collective-permute-done.2
  71.0 3.6 %collective-permute-start.3 = (bf16[2,8,8,256]{3,2,1,0:T(8,128)(2,1)S(1)}, bf16[2,8,8,256]{3,2,1,0:T(8,128)(2,1)S(1)}, u32[]{:S(2)}, u32[]{:S(2)}) collective-permute-start(bf16[2,8,8,256]{3,2,1,0:T(8,128)(2,1)S(1)} %pad_maximum_fusion.own_ref), channel_id=1, source_target_pairs={{0,32},{32,0},{1,33},{33,1},{2,34},{34,2},{3,35},{35,3},{4,36},{36... | collective-permute-start | bytes 196616 | tf_op jit(solution)/shard_map/ppermute | solution.py:459
  74.6 0.3 all-gather.2.cloned.1.call-done
  74.9 2.2 %copy-done.1 = bf16[256,8192]{1,0:T(8,128)(2,1)S(1)} copy-done((bf16[256,8192]{1,0:T(8,128)(2,1)S(1)}, bf16[256,8192]{1,0:T(8,128)(2,1)}, u32[]{:S(2)}) %copy-start.1) | copy-done | bytes 4194328
  77.1 2.2 %copy-done.2 = bf16[8192,256]{1,0:T(8,128)(2,1)S(1)} copy-done((bf16[8192,256]{1,0:T(8,128)(2,1)S(1)}, bf16[8192,256]{1,0:T(8,128)(2,1)}, u32[]{:S(2)}) %copy-start.2) | copy-done | bytes 4194328
  79.2 1.4 %project_queries.1.query_ref = bf16[128,512]{1,0:T(8,128)(2,1)S(1)} custom-call(bf16[256,8192]{1,0:T(8,128)(2,1)S(1)} %copy-done.1, bf16[32,256,256]{2,1,0:T(8,128)(2,1)S(1)} %bitcast.16, f32[128,256]{1,0:T(8,128)S(1)} %get-tuple-element.54.cosine_ref, f32[128,256]{1,0:T(8,128)S(1)} %get-tuple-element.58.sine_ref), custom_call_target="tpu_custom_call" | custom-call | flops 1073741824 | bytes 8388608 | tf_op jit(solution)/shard_map/project_queries/pallas_call | solution.py:460
  80.6 0.0 collective-permute-done.3.other_ref
  80.7 0.0 all-to-all-done.3.keys_ref
  80.7 3.9 %collective-permute-start.4 = (bf16[8,8,32,256]{3,2,1,0:T(8,128)(2,1)S(1)}, bf16[8,8,32,256]{3,2,1,0:T(8,128)(2,1)S(1)}, u32[]{:S(2)}, u32[]{:S(2)}) collective-permute-start(bf16[8,8,32,256]{3,2,1,0:T(8,128)(2,1)S(1)} %all-to-all-done.3.keys_ref), channel_id=1, source_target_pairs={{0,16},{16,0},{1,17},{17,1},{2,18},{18,2},{3,19},{19,3},{4,20},{20... | collective-permute-start | bytes 3145736 | tf_op jit(solution)/shard_map/ppermute | solution.py:475
  84.6 1.0 attend_near.1
  85.6 1.3 %collective-permute-done.4.keys_ref = bf16[8,8,32,256]{3,2,1,0:T(8,128)(2,1)S(1)} collective-permute-done((bf16[8,8,32,256]{3,2,1,0:T(8,128)(2,1)S(1)}, bf16[8,8,32,256]{3,2,1,0:T(8,128)(2,1)S(1)}, u32[]{:S(2)}, u32[]{:S(2)}) %collective-permute-start.4) | collective-permute-done | bytes 1048608 | tf_op jit(solution)/shard_map/ppermute | solution.py:475
  86.9 1.8 %attend_far.1 = f32[16,1,256]{2,1,0:T(1,128)S(1)} custom-call(s32[168]{0:T(256)S(1)} %get-tuple-element.39.meta_ref, bf16[128,512]{1,0:T(8,128)(2,1)S(1)} %project_queries.1.query_ref, bf16[8,8,32,256]{3,2,1,0:T(8,128)(2,1)S(1)} %collective-permute-done.4.keys_ref, bf16[2,8,8,256]{3,2,1,0:T(8,128)(2,1)S(1)} %pad_maximum_fusion.own_ref, ...), custom_call_target="tpu_custom_call" | custom-call | tf_op jit(solution)/shard_map/attend_far/pallas_call | solution.py:494
  88.6 21.0 %all_to_all.38.parts_ref = f32[16,1,256]{2,1,0:T(1,128)S(1)} all-to-all(f32[16,1,256]{2,1,0:T(1,128)S(1)} %attend_far.1), channel_id=1, replica_groups=mesh['y'=8,'zl'=2,'c'=2,'zh'=4,'x'=4] {'zh','x'}, dimensions={0} | all-to-all | bytes 32768 | tf_op jit(solution)/shard_map/all_to_all | solution.py:333
  109.6 0.6 token_values.1
  110.2 11.8 %all_to_all.39 = f32[32,1,128]{2,1,0:T(1,128)S(1)} all-to-all(f32[32,1,128]{2,1,0:T(1,128)S(1)} %bitcast.17), channel_id=1, replica_groups=mesh['y'=8,'zl'=2,'c'=2,'zh'=4,'x'=4] {'y','zl','c'}, dimensions={0} | all-to-all | bytes 32768 | tf_op jit(solution)/shard_map/all_to_all | solution.py:333
  122.0 0.5 multiply_reduce_fusion
  (10 shorter events, 0.1 us)
Async XLA Ops:
  8.5 12.0 %all-to-all-start = ((bf16[4,32,256]{2,1,0:T(8,128)(2,1)}), bf16[4,32,256]{2,1,0:T(8,128)(2,1)S(1)}, u32[]{:S(2)}, u32[]{:S(2)}) async-start(bf16[4,32,256]{2,1,0:T(8,128)(2,1)} %broadcast_in_dim.20), calls=%async_computation | async-start | bytes 131072 | tf_op jit(solution)/shard_map/all_to_all | solution.py:333
  13.4 61.5 %all-gather.2.cloned.1.call-start = ((), (), s32[]{:S(2)}) async-start(), calls=%async_computation.6 | async-start | bytes 4456448 | tf_op jit(solution)/shard_map/all_gather | solution.py:378
  13.4 8.0 %collective-permute-start = (bf16[256,256]{1,0:T(8,128)(2,1)}, bf16[256,256]{1,0:T(8,128)(2,1)S(1)}, u32[]{:S(2)}, u32[]{:S(2)}) collective-permute-start(bf16[256,256]{1,0:T(8,128)(2,1)} %param.10), channel_id=1, source_target_pairs={{0,32},{32,0},{1,33},{33,1},{2,34},{34,2},{3,35},{35,3},{4,36},{36... | collective-permute-start | bytes 393224 | tf_op jit(solution)/shard_map/ppermute | solution.py:351
  20.4 8.6 %copy-start.3 = (s32[32]{0:T(128)S(1)}, s32[32]{0:T(128)}, u32[]{:S(2)}) copy-start(s32[32]{0:T(128)} %parents_src.1) | copy-start | bytes 388
  20.5 8.6 %copy-start.4 = (s32[32]{0:T(128)S(1)}, s32[32]{0:T(128)}, u32[]{:S(2)}) copy-start(s32[32]{0:T(128)} %placed_src.1) | copy-start | bytes 388
  20.5 8.6 %copy-start.5 = (s32[32]{0:T(128)S(1)}, s32[32]{0:T(128)}, u32[]{:S(2)}) copy-start(s32[32]{0:T(128)} %lengths_src.1) | copy-start | bytes 388
  21.4 0.7 copy-start.6
  22.1 17.7 %all-to-all-start.1 = ((bf16[16,40,256]{2,1,0:T(8,128)(2,1)}), bf16[16,40,256]{2,1,0:T(8,128)(2,1)S(1)}, u32[]{:S(2)}, u32[]{:S(2)}) async-start(bf16[16,40,256]{2,1,0:T(8,128)(2,1)} %fold_weights.1), calls=%async_computation.1 | async-start | bytes 655360 | tf_op jit(solution)/shard_map/all_to_all | solution.py:333
  39.8 5.9 %copy-start = (bf16[256,8192]{1,0:T(8,128)(2,1)S(1)}, bf16[256,8192]{1,0:T(8,128)(2,1)}, u32[]{:S(2)}) copy-start(bf16[256,8192]{1,0:T(8,128)(2,1)} %tokens_ref.5) | copy-start | bytes 12582916
  39.8 7.1 %collective-permute-start.1 = (bf16[16,40,256]{2,1,0:T(8,128)(2,1)S(1)}, bf16[16,40,256]{2,1,0:T(8,128)(2,1)S(1)}, u32[]{:S(2)}, u32[]{:S(2)}) collective-permute-start(bf16[16,40,256]{2,1,0:T(8,128)(2,1)S(1)} %all-to-all-done.1.weights_ref), channel_id=1, source_target_pairs={{0,16},{16,0},{1,17},{17,1},{2,18},{18,2},{3,19},{19,3},{4,20},{20... | collective-permute-start | bytes 983048 | tf_op jit(solution)/shard_map/ppermute | solution.py:406
  62.4 18.3 %all-to-all-start.3 = ((bf16[8,8,32,256]{3,2,1,0:T(8,128)(2,1)}), bf16[8,8,32,256]{3,2,1,0:T(8,128)(2,1)S(1)}, u32[]{:S(2)}, u32[]{:S(2)}) async-start(bf16[8,8,32,256]{3,2,1,0:T(8,128)(2,1)} %spread_keys.1), calls=%async_computation.3 | async-start | bytes 2097152 | tf_op jit(solution)/shard_map/all_to_all | solution.py:333
  66.7 4.3 %collective-permute-start.2 = (bf16[8,8,256]{2,1,0:T(8,128)(2,1)S(1)}, bf16[8,8,256]{2,1,0:T(8,128)(2,1)S(1)}, u32[]{:S(2)}, u32[]{:S(2)}) collective-permute-start(bf16[8,8,256]{2,1,0:T(8,128)(2,1)S(1)} %get-tuple-element.77), channel_id=1, source_target_pairs={{0,16},{16,0},{1,17},{17,1},{2,18},{18,2},{3,19},{19,3},{4,20},{20... | collective-permute-start | bytes 98312 | tf_op jit(solution)/shard_map/ppermute | solution.py:457
  71.0 9.7 %collective-permute-start.3 = (bf16[2,8,8,256]{3,2,1,0:T(8,128)(2,1)S(1)}, bf16[2,8,8,256]{3,2,1,0:T(8,128)(2,1)S(1)}, u32[]{:S(2)}, u32[]{:S(2)}) collective-permute-start(bf16[2,8,8,256]{3,2,1,0:T(8,128)(2,1)S(1)} %pad_maximum_fusion.own_ref), channel_id=1, source_target_pairs={{0,32},{32,0},{1,33},{33,1},{2,34},{34,2},{3,35},{35,3},{4,36},{36... | collective-permute-start | bytes 196616 | tf_op jit(solution)/shard_map/ppermute | solution.py:459
  74.9 2.2 %copy-start.1 = (bf16[256,8192]{1,0:T(8,128)(2,1)S(1)}, bf16[256,8192]{1,0:T(8,128)(2,1)}, u32[]{:S(2)}) copy-start(bf16[256,8192]{1,0:T(8,128)(2,1)} %tokens_ref.5) | copy-start | bytes 12582916
  77.1 2.2 %copy-start.2 = (bf16[8192,256]{1,0:T(8,128)(2,1)S(1)}, bf16[8192,256]{1,0:T(8,128)(2,1)}, u32[]{:S(2)}) copy-start(bf16[8192,256]{1,0:T(8,128)(2,1)} %all-gather.2.cloned.1.call-done) | copy-start | bytes 12582916
  80.7 6.2 %collective-permute-start.4 = (bf16[8,8,32,256]{3,2,1,0:T(8,128)(2,1)S(1)}, bf16[8,8,32,256]{3,2,1,0:T(8,128)(2,1)S(1)}, u32[]{:S(2)}, u32[]{:S(2)}) collective-permute-start(bf16[8,8,32,256]{3,2,1,0:T(8,128)(2,1)S(1)} %all-to-all-done.3.keys_ref), channel_id=1, source_target_pairs={{0,16},{16,0},{1,17},{17,1},{2,18},{18,2},{3,19},{19,3},{4,20},{20... | collective-permute-start | bytes 3145736 | tf_op jit(solution)/shard_map/ppermute | solution.py:475
Sparse Core Ops, SparseCore 0:
  22.2 52.5 all-gather.1
